TPU v7x, 128 devices: a whole 4x4x4 slice. The times are simulated.
128 devices in a mesh: dp: 32 (over y, z, core), noise: 4 (over x).
Axes of the slice: x: 4, y: 4, z: 4, core: 2. Of those that a mesh axis runs over, the one named last changes fastest.
Arguments:
- noise_latents: bfloat16 [1536, 16384], P('noise', 'dp'), may hold values from -6 to 6
- data_latents: bfloat16 [12288, 16384], P('dp'), may hold values from -6 to 6
Outputs:
- targets: bfloat16 [1536, 16384], P('noise', 'dp')
All inputs are finite; a program needn't handle non-finite values.
Results may differ from a plain program's by a relative error of at most 0.022.
Values may be sent and summed in bfloat16 or wider, within the bound.
No kernel may reach another device: no remote copies, remote signals or barrier semaphores. Data moves between devices by JAX's collectives and lax.ppermute only.
A program may use at most 128 MiB of HBM per device.

v0:
```python
import jax
import jax.numpy as jnp
from jax import lax
from jax.sharding import PartitionSpec as P

ITERS = 3


EPS = 0.004


def row_lse(scores):
    peak = lax.pmax(jnp.max(scores, axis=1), "dp")
    total = lax.psum(jnp.sum(jnp.exp(scores - peak[:, None]), axis=1), "dp")
    return peak + jnp.log(total)


def col_lse(scores):
    peak = lax.pmax(jnp.max(scores, axis=0), "noise")
    total = lax.psum(jnp.sum(jnp.exp(scores - peak[None, :]), axis=0), "noise")
    return peak + jnp.log(total)


def body(noise_latents, data_latents):
    data_rows = data_latents.shape[0]
    width = data_latents.shape[1]
    piece = lax.all_gather(noise_latents, "dp", axis=1, tiled=True)
    block = data_latents
    dots = lax.dot_general(
        piece, block, (((1,), (1,)), ((), ())), preferred_element_type=jnp.float32
    )
    piece_f = piece.astype(jnp.float32)
    dots, sq_noise = (dots, jnp.sum(piece_f * piece_f, axis=1))
    data_f = data_latents.astype(jnp.float32)
    sq_data = jnp.sum(data_f * data_f, axis=1)
    cost = (sq_noise[:, None] + sq_data[None, :] - 2.0 * dots) / width
    g_pot = jnp.zeros((data_rows,), jnp.float32)
    for step in range(ITERS):
        f_pot = -EPS * row_lse((g_pot[None, :] - cost) / EPS)
        g_pot = -EPS * col_lse((f_pot[:, None] - cost) / EPS)
    scores = (g_pot[None, :] - cost) / EPS
    weights = jnp.exp(scores - row_lse(scores)[:, None]).astype(jnp.bfloat16)
    block = data_latents
    shares = lax.psum_scatter(
        lax.dot_general(
            block, weights, (((0,), (1,)), ((), ())), preferred_element_type=jnp.float32
        ).astype(jnp.bfloat16),
        "dp",
        scatter_dimension=0,
        tiled=True,
    ).astype(jnp.float32)
    return shares.T.astype(jnp.bfloat16)


def solution(mesh):
    return jax.shard_map(
        body,
        mesh=mesh,
        in_specs=(P("noise", "dp"), P("dp", None)),
        out_specs=P("noise", "dp"),
        check_vma=False,
    )
```

profile of v0, /device:TPU:0, one launch (start us, length us, event | category | flops | bytes accessed | tf_op | source)
XLA Modules:
  0.0 787.9 jit_solution(3504850687837078529)
XLA Ops:
  6.5 0.7 all-gather.2.cloned.1.call-update
  7.3 7.1 multiply_reduce_fusion
  14.4 67.9 %all-gather.2.cloned.1.call-done = bf16[384,16384]{1,0:T(8,128)(2,1)} async-done(((bf16[384,512]{1,0:T(8,128)(2,1)}), bf16[384,16384]{1,0:T(8,128)(2,1)}) %all-gather.2.cloned.1.call-update) | async-done | bytes 12582928 | tf_op jit(solution)/shard_map/all_gather | solution.py:27
  82.4 7.1 multiply_reduce_fusion.1
  89.5 17.4 %fusion.3 = (f32[384]{0:T(512)S(1)}, f32[384,384]{0,1:T(8,128)S(1)}) fusion(bf16[384,16384]{1,0:T(8,128)(2,1)} %all-gather.2.cloned.1.call-done, bf16[384,16384]{1,0:T(8,128)(2,1)} %param.3, f32[384]{0:T(512)S(1)} %multiply_reduce_fusion, f32[384]{0:T(512)S(1)} %multiply_reduce_fusion.1), kind=kOutput, calls=%fused_computation.22 | convolution fusion | flops 4832869888 | bytes 25760256 | tf_op jit(solution)/shard_map/dot_general | solution.py:29
  106.9 65.6 %pmax.49 = f32[384]{0:T(512)S(1)} all-reduce(f32[384]{0:T(512)S(1)} %get-tuple-element.5), channel_id=1, replica_groups=mesh['dp'=32,'noise'=4] {'dp'}, use_global_device_ids=true, to_apply=%region_3.0 | all-reduce | flops 384 | bytes 3072 | tf_op jit(solution)/shard_map/pmax | solution.py:13
  172.5 0.1 exponential_reduce_fusion.6
  172.7 62.7 %psum.49 = f32[384]{0:T(512)S(1)} all-reduce(f32[384]{0:T(512)S(1)} %exponential_reduce_fusion.6), channel_id=1, replica_groups=mesh['dp'=32,'noise'=4] {'dp'}, use_global_device_ids=true, to_apply=%region_5.0 | all-reduce | flops 384 | bytes 3072 | tf_op jit(solution)/shard_map/psum | solution.py:14
  235.4 0.2 fusion.4
  235.5 10.4 %pmax.50 = f32[384]{0:T(512)S(1)} all-reduce(f32[384]{0:T(512)S(1)} %fusion.4), channel_id=1, replica_groups=mesh['dp'=32,'noise'=4] {'noise'}, use_global_device_ids=true, to_apply=%region_7.0 | all-reduce | flops 384 | bytes 3072 | tf_op jit(solution)/shard_map/pmax | solution.py:19
  245.9 0.3 exponential_reduce_fusion.5
  246.2 7.7 psum.50
  254.1 62.7 %pmax.51 = f32[384]{0:T(512)S(1)} all-reduce(f32[384]{0:T(512)S(1)} %fusion.5), channel_id=1, replica_groups=mesh['dp'=32,'noise'=4] {'dp'}, use_global_device_ids=true, to_apply=%region_11.0 | all-reduce | flops 384 | bytes 3072 | tf_op jit(solution)/shard_map/pmax | solution.py:13
  316.8 0.2 exponential_reduce_fusion.4
  317.0 62.7 %psum.51 = f32[384]{0:T(512)S(1)} all-reduce(f32[384]{0:T(512)S(1)} %exponential_reduce_fusion.4), channel_id=1, replica_groups=mesh['dp'=32,'noise'=4] {'dp'}, use_global_device_ids=true, to_apply=%region_13.0 | all-reduce | flops 384 | bytes 3072 | tf_op jit(solution)/shard_map/psum | solution.py:14
  379.7 0.2 fusion.6
  379.8 9.7 %pmax.52 = f32[384]{0:T(512)S(1)} all-reduce(f32[384]{0:T(512)S(1)} %fusion.6), channel_id=1, replica_groups=mesh['dp'=32,'noise'=4] {'noise'}, use_global_device_ids=true, to_apply=%region_15.0 | all-reduce | flops 384 | bytes 3072 | tf_op jit(solution)/shard_map/pmax | solution.py:19
  389.6 0.3 exponential_reduce_fusion.3
  389.8 7.7 psum.52
  397.7 62.7 %pmax.53 = f32[384]{0:T(512)S(1)} all-reduce(f32[384]{0:T(512)S(1)} %fusion.7), channel_id=1, replica_groups=mesh['dp'=32,'noise'=4] {'dp'}, use_global_device_ids=true, to_apply=%region_19.0 | all-reduce | flops 384 | bytes 3072 | tf_op jit(solution)/shard_map/pmax | solution.py:13
  460.4 0.2 exponential_reduce_fusion.2
  460.6 62.7 %psum.53 = f32[384]{0:T(512)S(1)} all-reduce(f32[384]{0:T(512)S(1)} %exponential_reduce_fusion.2), channel_id=1, replica_groups=mesh['dp'=32,'noise'=4] {'dp'}, use_global_device_ids=true, to_apply=%region_21.0 | all-reduce | flops 384 | bytes 3072 | tf_op jit(solution)/shard_map/psum | solution.py:14
  523.3 0.2 fusion.8
  523.5 9.7 %pmax.54 = f32[384]{0:T(512)S(1)} all-reduce(f32[384]{0:T(512)S(1)} %fusion.8), channel_id=1, replica_groups=mesh['dp'=32,'noise'=4] {'noise'}, use_global_device_ids=true, to_apply=%region_23.0 | all-reduce | flops 384 | bytes 3072 | tf_op jit(solution)/shard_map/pmax | solution.py:19
  533.2 0.3 exponential_reduce_fusion.1
  533.5 7.7 psum.54
  541.2 0.1 fusion.9
  541.4 62.7 %pmax.55 = f32[384]{0:T(512)S(1)} all-reduce(f32[384]{0:T(512)S(1)} %fusion.9), channel_id=1, replica_groups=mesh['dp'=32,'noise'=4] {'dp'}, use_global_device_ids=true, to_apply=%region_27.0 | all-reduce | flops 384 | bytes 3072 | tf_op jit(solution)/shard_map/pmax | solution.py:13
  604.0 0.2 exponential_reduce_fusion
  604.2 62.9 %psum.55 = f32[384]{0:T(512)S(1)} all-reduce(f32[384]{0:T(512)S(1)} %exponential_reduce_fusion), channel_id=1, replica_groups=mesh['dp'=32,'noise'=4] {'dp'}, use_global_device_ids=true, to_apply=%region_29.0 | all-reduce | flops 384 | bytes 3072 | tf_op jit(solution)/shard_map/psum | solution.py:14
  667.1 14.0 %fusion = bf16[16384,384]{0,1:T(8,128)(2,1)} fusion(bf16[384,16384]{1,0:T(8,128)(2,1)} %param.3, f32[384,384]{0,1:T(8,128)S(1)} %get-tuple-element.6, f32[384]{0:T(512)S(1)} %log_add_fusion, f32[384]{0:T(512)S(1)} %add_multiply_fusion), kind=kOutput, calls=%fused_computation.3 | convolution fusion | flops 4838719488 | bytes 25758720 | tf_op jit(solution)/shard_map/dot_general | solution.py:45
  681.2 99.9 %reduce-scatter.2.cloned.1.call-done = bf16[512,384]{0,1:T(8,128)(2,1)} async-done(((bf16[16384,384]{0,1:T(8,128)(2,1)}), bf16[512,384]{0,1:T(8,128)(2,1)}) %reduce-scatter.2.cloned.1.call-update) | async-done | bytes 393232 | tf_op jit(solution)/shard_map/reduce_scatter | solution.py:44
  (12 shorter events, 0.4 us)
Async XLA Ops:
  6.5 75.8 %all-gather.2.cloned.1.call-start = ((), (), s32[]{:S(2)}) async-start(), calls=%async_computation.1 | async-start | bytes 12976128 | tf_op jit(solution)/shard_map/all_gather | solution.py:27
  7.3 773.8 %reduce-scatter.2.cloned.1.call-start = ((), (), s32[]{:S(2)}) async-start(), calls=%async_computation.2 | async-start | bytes 12976128 | tf_op jit(solution)/shard_map/reduce_scatter | solution.py:44
Sparse Core Ops, SparseCore 0:
  9.5 72.7 all-gather.1
  681.3 99.7 reduce-scatter.1
where the time goes:
time: 788 us
  blocking collectives  558 us (71%)
  waiting for transfers between devices  169 us (21%)
  matrix products  31.4 us (4%)
  other arithmetic  16.8 us (2%)
  between operations  13.4 us (2%)
    pmax x4, blocking collectives, row_lse(): peak = lax.pmax(jnp.max(scores, axis=1), 'dp')  254 us
    psum x4, blocking collectives, row_lse(): total = lax.psum(jnp.sum(jnp.exp(scores - peak[:, None]), axis=1), 'dp')  251 us
    reduce_scatter x1, waiting for transfers between devices, body(): lax.psum_scatter(lax.dot_general(block, weights, (((0,), (1,)), ((), ()))...  99.9 us
    all_gather x1, waiting for transfers between devices, body(): piece = lax.all_gather(noise_latents, 'dp', axis=1, tiled=True)  67.9 us
    pmax x3, blocking collectives, col_lse(): peak = lax.pmax(jnp.max(scores, axis=0), 'noise')  29.9 us
    psum x3, blocking collectives, col_lse(): total = lax.psum(jnp.sum(jnp.exp(scores - peak[None, :]), axis=0), 'noise')  23.2 us
    dot_general x1, matrix products, body(): lax.dot_general(piece, block, (((1,), (1,)), ((), ())), preferred_element...  17.4 us
  transfers between devices with their start and end apart: 2, of which 2 were waited for; matrix products, arithmetic and copies ran while one was open for 1% of the time, Pallas kernels for 0%

commit v1 on v0

v1 whole, which is shorter than its diff:
```python
import jax
import jax.numpy as jnp
from jax import lax
from jax.sharding import PartitionSpec as P

ITERS = 3
EPS = 0.004


def lse(values, axis):
    peak = jnp.max(values, axis=axis, keepdims=True)
    total = jnp.sum(jnp.exp(values - peak), axis=axis)
    return jnp.squeeze(peak, axis) + jnp.log(total)


def to_all_dp(values):
    n = lax.axis_size("dp")
    return lax.all_to_all(
        jnp.broadcast_to(values[None], (n,) + values.shape), "dp", 0, 0
    )


def to_all_noise(values):
    n = lax.axis_size("noise")
    parts = [values]
    for k in range(1, n):
        parts.append(
            lax.ppermute(values, "noise", [(i, (i + k) % n) for i in range(n)])
        )
    return jnp.stack(parts)


def body(noise_latents, data_latents):
    width = data_latents.shape[1]
    piece = lax.all_gather(noise_latents, "dp", axis=1, tiled=True)
    dots = lax.dot_general(
        piece, data_latents, (((1,), (1,)), ((), ())), preferred_element_type=jnp.float32
    )
    noise_f = noise_latents.astype(jnp.float32)
    sx_part = jnp.sum(noise_f * noise_f, axis=1)
    data_f = data_latents.astype(jnp.float32)
    sq_data = jnp.sum(data_f * data_f, axis=1)
    scale = 1.0 / (width * EPS)
    twice = dots * (2.0 * scale)
    sy = sq_data * scale
    sx = None
    g = jnp.zeros_like(sy)
    for step in range(ITERS):
        local = lse(twice + (g - sy)[None, :], 1)
        if sx is None:
            got = to_all_dp(jnp.stack([local, sx_part]))
            sx = jnp.sum(got[:, 1], axis=0) * scale
            got = got[:, 0]
        else:
            got = to_all_dp(local)
        f = sx - lse(got, 0)
        local = lse(twice + (f - sx)[:, None], 0)
        g = sy - lse(to_all_noise(local), 0)
    coupling = jnp.exp(twice + (f - sx)[:, None] + (g - sy)[None, :])
    row_part = jnp.sum(coupling, axis=1)
    row_sum = jnp.sum(to_all_dp(row_part), axis=0)
    shares = lax.psum_scatter(
        lax.dot_general(
            data_latents,
            coupling.astype(jnp.bfloat16),
            (((0,), (1,)), ((), ())),
            preferred_element_type=jnp.float32,
        ).astype(jnp.bfloat16),
        "dp",
        scatter_dimension=0,
        tiled=True,
    ).astype(jnp.float32)
    return (shares.T / row_sum[:, None]).astype(jnp.bfloat16)


def solution(mesh):
    return jax.shard_map(
        body,
        mesh=mesh,
        in_specs=(P("noise", "dp"), P("dp", None)),
        out_specs=P("noise", "dp"),
        check_vma=False,
    )
```

time: 788 us -> 284 us (0.36)
  blocking collectives: 558 us -> 45.7 us
  starting transfers between devices: 0.04 us -> 10.4 us
    pmax x7 -> x0, blocking collectives: 284 us -> none  [the longest x4 254 us: row_lse(): peak = lax.pmax(jnp.max(scores, axis=1), 'dp')]
    psum x7 -> x0, blocking collectives: 274 us -> none  [the longest x4 251 us: row_lse(): total = lax.psum(jnp.sum(jnp.exp(scores - peak[:, None]), axis=1), 'dp')]
    all_to_all x0 -> x4, blocking collectives: none -> 45.7 us  [to_all_dp(): lax.all_to_all(jnp.broadcast_to(values[None], (n,) + values.shape), 'dp',...]
    ppermute x0 -> x9, waiting for transfers between devices: none -> 12.1 us  [to_all_noise(): lax.ppermute(values, 'noise', [(i, (i + k) % n) for i in range(n)])]
    ppermute x0 -> x9, starting transfers between devices: none -> 10.4 us  [to_all_noise(): lax.ppermute(values, 'noise', [(i, (i + k) % n) for i in range(n)])]
    reduce_scatter x1, waiting for transfers between devices: 99.9 us -> 89.5 us  [body(): lax.psum_scatter(lax.dot_general(data_latents, coupling.astype(jnp.bfloat...]
  transfers between devices with their start and end apart: 2 -> 11, of which waited for: 2 -> 10; matrix products, arithmetic and copies ran while one was open for 1% -> 3% of each run, Pallas kernels for 0% -> 0%
where the time goes in v1:
time: 284 us; the launch traced here: 283 us
  waiting for transfers between devices  169 us (60%)
  blocking collectives  45.7 us (16%)
  matrix products  31.4 us (11%)
  between operations  13.5 us (5%)
  other arithmetic  13.1 us (5%)
  starting transfers between devices  10.4 us (4%)
    reduce_scatter x1, waiting for transfers between devices, body(): lax.psum_scatter(lax.dot_general(data_latents, coupling.astype(jnp.bfloat...  89.5 us
    all_gather x1, waiting for transfers between devices, body(): piece = lax.all_gather(noise_latents, 'dp', axis=1, tiled=True)  66.7 us
    all_to_all x4, blocking collectives, to_all_dp(): lax.all_to_all(jnp.broadcast_to(values[None], (n,) + values.shape), 'dp',...  45.7 us
    dot_general x1, matrix products, body(): lax.dot_general(piece, data_latents, (((1,), (1,)), ((), ())), preferred_...  17.4 us
    dot_general x1, matrix products, body(): lax.dot_general(data_latents, coupling.astype(jnp.bfloat16), (((0,), (1,)...  14 us
    ppermute x9, waiting for transfers between devices, to_all_noise(): lax.ppermute(values, 'noise', [(i, (i + k) % n) for i in range(n)])  12.1 us
    ppermute x9, starting transfers between devices, to_all_noise(): lax.ppermute(values, 'noise', [(i, (i + k) % n) for i in range(n)])  10.4 us
    reduce_sum x1, other arithmetic, body(): sq_data = jnp.sum(data_f * data_f, axis=1)  7.14 us
  transfers between devices with their start and end apart: 11, of which 10 were waited for; matrix products, arithmetic and copies ran while one was open for 3% of the time, Pallas kernels for 0%

profile of v1, /device:TPU:0, one launch (start us, length us, event | category | flops | bytes accessed | tf_op | source)
XLA Modules:
  0.0 283.4 jit_solution(8139719349359961752)
XLA Ops:
  6.5 0.7 all-gather.2.cloned.1.call-update
  7.3 1.2 multiply_reduce_fusion.1
  8.5 7.1 %multiply_reduce_fusion = f32[384]{0:T(512)S(1)} fusion(bf16[384,16384]{1,0:T(8,128)(2,1)} %param.3), kind=kLoop, calls=%fused_computation | loop fusion | flops 18873984 | bytes 12584448 | tf_op jit(solution)/shard_map/reduce_sum | solution.py:42
  15.6 66.7 %all-gather.2.cloned.1.call-done = bf16[384,16384]{1,0:T(8,128)(2,1)} async-done(((bf16[384,512]{1,0:T(8,128)(2,1)}), bf16[384,16384]{1,0:T(8,128)(2,1)}) %all-gather.2.cloned.1.call-update) | async-done | bytes 12582928 | tf_op jit(solution)/shard_map/all_gather | solution.py:35
  82.4 17.4 %add_reduce_fusion.4 = (f32[384]{0:T(512)S(1)}, f32[384,384]{0,1:T(8,128)S(1)}) fusion(f32[384]{0:T(512)S(1)} %multiply_subtract_fusion, bf16[384,16384]{1,0:T(8,128)(2,1)} %all-gather.2.cloned.1.call-done, bf16[384,16384]{1,0:T(8,128)(2,1)} %param.3), kind=kOutput, calls=%fused_computation.17 | convolution fusion | flops 4832280064 | bytes 25758720 | tf_op jit(solution)/shard_map/dot_general | solution.py:36
  100.0 13.2 %all_to_all.29 = f32[32,2,384]{2,1,0:T(2,128)S(1)} all-to-all(f32[32,2,384]{2,1,0:T(2,128)S(1)} %broadcast_in_dim.11), channel_id=1, replica_groups=mesh['dp'=32,'noise'=4] {'dp'}, dimensions={0} | all-to-all | bytes 196608 | tf_op jit(solution)/shard_map/all_to_all | solution.py:18
  113.5 0.3 exponential_reduce_fusion.4
  113.8 2.8 collective-permute-start.2
  116.5 0.8 collective-permute-start.1
  117.4 0.9 collective-permute-start
  118.2 3.4 %collective-permute-done.1 = f32[384]{0:T(512)S(1)} collective-permute-done((f32[384]{0:T(512)S(1)}, f32[384]{0:T(512)S(1)}, u32[]{:S(2)}, u32[]{:S(2)}) %collective-permute-start.1) | collective-permute-done | bytes 1568 | tf_op jit(solution)/shard_map/ppermute | solution.py:28
  121.6 0.5 collective-permute-done
  122.6 10.9 %all_to_all.30 = f32[32,1,384]{2,1,0:T(1,128)S(1)} all-to-all(f32[32,1,384]{2,1,0:T(1,128)S(1)} %broadcast_in_dim.12), channel_id=1, replica_groups=mesh['dp'=32,'noise'=4] {'dp'}, dimensions={0} | all-to-all | bytes 98304 | tf_op jit(solution)/shard_map/all_to_all | solution.py:18
  133.7 0.3 exponential_reduce_fusion.2
  134.0 0.4 collective-permute-start.5
  134.4 1.4 collective-permute-start.4
  135.8 1.2 collective-permute-start.3
  137.0 0.7 collective-permute-done.5
  137.7 1.8 collective-permute-done.4
  139.5 1.1 collective-permute-done.3
  141.0 10.8 %all_to_all.31 = f32[32,1,384]{2,1,0:T(1,128)S(1)} all-to-all(f32[32,1,384]{2,1,0:T(1,128)S(1)} %broadcast_in_dim.13), channel_id=1, replica_groups=mesh['dp'=32,'noise'=4] {'dp'}, dimensions={0} | all-to-all | bytes 98304 | tf_op jit(solution)/shard_map/all_to_all | solution.py:18
  152.1 0.3 exponential_reduce_fusion
  152.4 1.8 collective-permute-start.8
  154.2 0.9 collective-permute-start.7
  155.1 0.2 collective-permute-start.6
  155.3 0.7 collective-permute-done.8
  156.0 3.3 %collective-permute-done.7 = f32[384]{0:T(512)S(1)} collective-permute-done((f32[384]{0:T(512)S(1)}, f32[384]{0:T(512)S(1)}, u32[]{:S(2)}, u32[]{:S(2)}) %collective-permute-start.7) | collective-permute-done | bytes 1568 | tf_op jit(solution)/shard_map/ppermute | solution.py:28
  159.3 0.6 collective-permute-done.6
  160.0 14.0 %fusion = bf16[16384,384]{0,1:T(8,128)(2,1)} fusion(bf16[384,16384]{1,0:T(8,128)(2,1)} %param.3, f32[384,384]{0,1:T(8,128)S(1)} %get-tuple-element.9, f32[384]{0:T(512)S(1)} %subtract_subtract_fusion, f32[384]{0:T(512)S(1)} %subtract_subtract_fusion.1), kind=kOutput, calls=%fused_computation.2 | convolution fusion | flops 4838572032 | bytes 25758720 | tf_op jit(solution)/shard_map/dot_general | solution.py:63
  174.3 10.8 %all_to_all.32 = f32[32,1,384]{2,1,0:T(1,128)S(1)} all-to-all(f32[32,1,384]{2,1,0:T(1,128)S(1)} %broadcast_in_dim.14), channel_id=1, replica_groups=mesh['dp'=32,'noise'=4] {'dp'}, dimensions={0} | all-to-all | bytes 98304 | tf_op jit(solution)/shard_map/all_to_all | solution.py:18
  185.1 89.5 %reduce-scatter.2.cloned.1.call-done = bf16[512,384]{0,1:T(8,128)(2,1)} async-done(((bf16[16384,384]{0,1:T(8,128)(2,1)}), bf16[512,384]{0,1:T(8,128)(2,1)}) %reduce-scatter.2.cloned.1.call-update) | async-done | bytes 393232 | tf_op jit(solution)/shard_map/reduce_scatter | solution.py:62
  274.6 1.9 fusion.3
  (58 shorter events, 2.3 us)
Async XLA Ops:
  6.5 75.8 %all-gather.2.cloned.1.call-start = ((), (), s32[]{:S(2)}) async-start(), calls=%async_computation.5 | async-start | bytes 12976128 | tf_op jit(solution)/shard_map/all_gather | solution.py:35
  7.3 267.4 %reduce-scatter.2.cloned.1.call-start = ((), (), s32[]{:S(2)}) async-start(), calls=%async_computation.6 | async-start | bytes 12976128 | tf_op jit(solution)/shard_map/reduce_scatter | solution.py:62
  113.8 4.5 %collective-permute-start.2 = (f32[384]{0:T(512)S(1)}, f32[384]{0:T(512)S(1)}, u32[]{:S(2)}, u32[]{:S(2)}) collective-permute-start(f32[384]{0:T(512)S(1)} %log_add_fusion.4), channel_id=1, source_target_pairs={{0,3},{1,0},{2,1},{3,2},{4,7},{5,4},{6,5},{7,6},{8,11},{9,8},{10,9... | collective-permute-start | bytes 4616 | tf_op jit(solution)/shard_map/ppermute | solution.py:28
  116.5 5.1 %collective-permute-start.1 = (f32[384]{0:T(512)S(1)}, f32[384]{0:T(512)S(1)}, u32[]{:S(2)}, u32[]{:S(2)}) collective-permute-start(f32[384]{0:T(512)S(1)} %log_add_fusion.4), channel_id=1, source_target_pairs={{0,2},{1,3},{2,0},{3,1},{4,6},{5,7},{6,4},{7,5},{8,10},{9,11},{10,... | collective-permute-start | bytes 4616 | tf_op jit(solution)/shard_map/ppermute | solution.py:28
  117.4 4.8 %collective-permute-start = (f32[384]{0:T(512)S(1)}, f32[384]{0:T(512)S(1)}, u32[]{:S(2)}, u32[]{:S(2)}) collective-permute-start(f32[384]{0:T(512)S(1)} %log_add_fusion.4), channel_id=1, source_target_pairs={{0,1},{1,2},{2,3},{3,0},{4,5},{5,6},{6,7},{7,4},{8,9},{9,10},{10,1... | collective-permute-start | bytes 4616 | tf_op jit(solution)/shard_map/ppermute | solution.py:28
  134.0 3.7 %collective-permute-start.5 = (f32[384]{0:T(512)S(1)}, f32[384]{0:T(512)S(1)}, u32[]{:S(2)}, u32[]{:S(2)}) collective-permute-start(f32[384]{0:T(512)S(1)} %log_add_fusion.2), channel_id=1, source_target_pairs={{0,3},{1,0},{2,1},{3,2},{4,7},{5,4},{6,5},{7,6},{8,11},{9,8},{10,9... | collective-permute-start | bytes 4616 | tf_op jit(solution)/shard_map/ppermute | solution.py:28
  134.4 5.1 %collective-permute-start.4 = (f32[384]{0:T(512)S(1)}, f32[384]{0:T(512)S(1)}, u32[]{:S(2)}, u32[]{:S(2)}) collective-permute-start(f32[384]{0:T(512)S(1)} %log_add_fusion.2), channel_id=1, source_target_pairs={{0,2},{1,3},{2,0},{3,1},{4,6},{5,7},{6,4},{7,5},{8,10},{9,11},{10,... | collective-permute-start | bytes 4616 | tf_op jit(solution)/shard_map/ppermute | solution.py:28
  135.8 4.8 %collective-permute-start.3 = (f32[384]{0:T(512)S(1)}, f32[384]{0:T(512)S(1)}, u32[]{:S(2)}, u32[]{:S(2)}) collective-permute-start(f32[384]{0:T(512)S(1)} %log_add_fusion.2), channel_id=1, source_target_pairs={{0,1},{1,2},{2,3},{3,0},{4,5},{5,6},{6,7},{7,4},{8,9},{9,10},{10,1... | collective-permute-start | bytes 4616 | tf_op jit(solution)/shard_map/ppermute | solution.py:28
  152.4 3.7 %collective-permute-start.8 = (f32[384]{0:T(512)S(1)}, f32[384]{0:T(512)S(1)}, u32[]{:S(2)}, u32[]{:S(2)}) collective-permute-start(f32[384]{0:T(512)S(1)} %log_add_fusion), channel_id=1, source_target_pairs={{0,3},{1,0},{2,1},{3,2},{4,7},{5,4},{6,5},{7,6},{8,11},{9,8},{10,9... | collective-permute-start | bytes 4616 | tf_op jit(solution)/shard_map/ppermute | solution.py:28
  154.2 5.1 %collective-permute-start.7 = (f32[384]{0:T(512)S(1)}, f32[384]{0:T(512)S(1)}, u32[]{:S(2)}, u32[]{:S(2)}) collective-permute-start(f32[384]{0:T(512)S(1)} %log_add_fusion), channel_id=1, source_target_pairs={{0,2},{1,3},{2,0},{3,1},{4,6},{5,7},{6,4},{7,5},{8,10},{9,11},{10,... | collective-permute-start | bytes 4616 | tf_op jit(solution)/shard_map/ppermute | solution.py:28
  155.1 4.8 %collective-permute-start.6 = (f32[384]{0:T(512)S(1)}, f32[384]{0:T(512)S(1)}, u32[]{:S(2)}, u32[]{:S(2)}) collective-permute-start(f32[384]{0:T(512)S(1)} %log_add_fusion), channel_id=1, source_target_pairs={{0,1},{1,2},{2,3},{3,0},{4,5},{5,6},{6,7},{7,4},{8,9},{9,10},{10,1... | collective-permute-start | bytes 4616 | tf_op jit(solution)/shard_map/ppermute | solution.py:28
Sparse Core Ops, SparseCore 0:
  9.5 72.7 all-gather.1
  174.2 100.4 reduce-scatter.1

commit v2 on v1

--- a/solution.py
+++ b/solution.py
@@ -1,10 +1,25 @@
 import jax
 import jax.numpy as jnp
 from jax import lax
+from jax.experimental import pallas as pl
+from jax.experimental.pallas import tpu as pltpu
 from jax.sharding import PartitionSpec as P
 
 ITERS = 3
 EPS = 0.004
+SIDE = 4
+OFFS = (2, 1, 3)
+VMEM = 48 * 1024 * 1024
+
+
+def shift(values, dy, dz, dc=0):
+    pairs = []
+    for y in range(SIDE):
+        for z in range(SIDE):
+            for c in range(2):
+                to = (((y + dy) % SIDE) * SIDE + (z + dz) % SIDE) * 2 + (c ^ dc)
+                pairs.append(((y * SIDE + z) * 2 + c, to))
+    return lax.ppermute(values, "dp", pairs)
 
 
 def lse(values, axis):
@@ -30,9 +45,157 @@
     return jnp.stack(parts)
 
 
+def other_columns(data, core):
+    rows, width = data.shape
+    block = width // (2 * SIDE * SIDE)
+
+    def kernel(core_ref, in_ref, out_ref):
+        out_ref[...] = in_ref[...]
+
+    return pl.pallas_call(
+        kernel,
+        grid_spec=pltpu.PrefetchScalarGridSpec(
+            num_scalar_prefetch=1,
+            grid=(SIDE * SIDE,),
+            in_specs=[pl.BlockSpec((rows, block), lambda t, c: (0, 2 * t + 1 - c[0]))],
+            out_specs=pl.BlockSpec((rows, block), lambda t, c: (0, t)),
+        ),
+        out_shape=jax.ShapeDtypeStruct((rows, width // 2), data.dtype),
+        compiler_params=pltpu.CompilerParams(vmem_limit_bytes=VMEM),
+        cost_estimate=pl.CostEstimate(
+            flops=0, bytes_accessed=rows * width * 2, transcendentals=0
+        ),
+    )(core, data)
+
+
+def block_sum(w_own, w_oth, d_own, d_oth):
+    total = jnp.dot(w_own[...], d_own[...], preferred_element_type=jnp.float32)
+    total += jnp.dot(w_oth[...], d_oth[...], preferred_element_type=jnp.float32)
+    return total.astype(jnp.bfloat16)
+
+
+def sums(kernel, where, n, ins, out_shape, out_specs):
+    w_own, w_oth, d_own, d_oth = ins
+    rows, inner = w_own.shape
+    block = d_own.shape[1] // (2 * SIDE * SIDE)
+    return pl.pallas_call(
+        kernel,
+        grid_spec=pltpu.PrefetchScalarGridSpec(
+            num_scalar_prefetch=1,
+            grid=(n,),
+            in_specs=[
+                pl.BlockSpec((rows, inner), lambda t, w: (0, 0)),
+                pl.BlockSpec((rows, inner), lambda t, w: (0, 0)),
+                pl.BlockSpec((inner, block), lambda t, w: (0, 2 * w[t] + w[n])),
+                pl.BlockSpec((inner, block), lambda t, w: (0, w[t])),
+            ],
+            out_specs=out_specs,
+        ),
+        out_shape=out_shape,
+        compiler_params=pltpu.CompilerParams(vmem_limit_bytes=VMEM),
+        cost_estimate=pl.CostEstimate(
+            flops=n * 4 * rows * inner * block,
+            bytes_accessed=n * (4 * inner * block + 2 * rows * block),
+            transcendentals=0,
+        ),
+    )(where, *ins)
+
+
+def far_kernel(where, w_own, w_oth, d_own, d_oth, *outs):
+    t = pl.program_id(0)
+    total = block_sum(w_own, w_oth, d_own, d_oth)
+    half = total.shape[0] // 2
+    for k in range(3):
+
+        @pl.when(t // 3 == k)
+        def _():
+            outs[k][0] = total[:half]
+
+        @pl.when(t % 3 == k)
+        def _():
+            outs[3 + k][0] = total[half:]
+
+
+def near_kernel(where, w_own, w_oth, d_own, d_oth, along_z, along_y, mine):
+    t = pl.program_id(0)
+    total = block_sum(w_own, w_oth, d_own, d_oth)
+
+    @pl.when(t < 3)
+    def _():
+        along_z[0] = total
+
+    @pl.when((t >= 3) & (t < 6))
+    def _():
+        along_y[0] = total
+
+    @pl.when(t == 6)
+    def _():
+        mine[...] = total
+
+
+def scattered_sums(ins, y, z, core):
+    rows = ins[0].shape[0]
+    block = ins[2].shape[1] // (2 * SIDE * SIDE)
+    half = rows // 2
+
+    def places(offsets):
+        chips = [((y + dy) % SIDE) * SIDE + (z + dz) % SIDE for dy, dz in offsets]
+        return jnp.stack(chips + [core]).astype(jnp.int32)
+
+    far = [(dy, dz) for dy in OFFS for dz in OFFS]
+    part = jax.ShapeDtypeStruct((3, half, block), jnp.bfloat16)
+    specs = []
+    for k in range(3):
+        specs.append(
+            pl.BlockSpec(
+                (1, half, block), lambda t, w, k=k: (jnp.clip(t - 3 * k, 0, 2), 0, 0)
+            )
+        )
+    for k in range(3):
+        specs.append(pl.BlockSpec((1, half, block), lambda t, w: (t // 3, 0, 0)))
+    parts = sums(far_kernel, places(far), 9, ins, [part] * 6, specs)
+    got_y = [shift(parts[k], OFFS[k], 0) for k in range(3)]
+    got_z = [shift(parts[3 + k], 0, OFFS[k]) for k in range(3)]
+
+    near = [(0, dz) for dz in OFFS] + [(dy, 0) for dy in OFFS] + [(0, 0)]
+    whole = jax.ShapeDtypeStruct((3, rows, block), jnp.bfloat16)
+    along_z, along_y, mine = sums(
+        near_kernel,
+        places(near),
+        7,
+        ins,
+        [whole, whole, jax.ShapeDtypeStruct((rows, block), jnp.bfloat16)],
+        [
+            pl.BlockSpec((1, rows, block), lambda t, w: (jnp.minimum(t, 2), 0, 0)),
+            pl.BlockSpec((1, rows, block), lambda t, w: (jnp.clip(t - 3, 0, 2), 0, 0)),
+            pl.BlockSpec((rows, block), lambda t, w: (0, 0)),
+        ],
+    )
+
+    def add(first, others):
+        total = first.astype(jnp.float32)
+        for other in others:
+            total += other.astype(jnp.float32)
+        return total
+
+    sum_z = add(along_z[:, :half], got_y).astype(jnp.bfloat16)
+    sum_y = add(along_y[:, half:], got_z).astype(jnp.bfloat16)
+    got = []
+    for k in range(3):
+        got.append(shift(jnp.concatenate([sum_z[k], along_z[k, half:]]), 0, OFFS[k]))
+        got.append(shift(jnp.concatenate([along_y[k, :half], sum_y[k]]), OFFS[k], 0))
+    return add(mine, got)
+
+
 def body(noise_latents, data_latents):
     width = data_latents.shape[1]
+    place = lax.axis_index("dp")
+    core = place % 2
+    z = (place // 2) % SIDE
+    y = place // (2 * SIDE)
+
     piece = lax.all_gather(noise_latents, "dp", axis=1, tiled=True)
+    data_other = shift(other_columns(data_latents, core[None]), 0, 0, 1)
     dots = lax.dot_general(
         piece, data_latents, (((1,), (1,)), ((), ())), preferred_element_type=jnp.float32
     )
@@ -57,20 +220,12 @@
         local = lse(twice + (f - sx)[:, None], 0)
         g = sy - lse(to_all_noise(local), 0)
     coupling = jnp.exp(twice + (f - sx)[:, None] + (g - sy)[None, :])
-    row_part = jnp.sum(coupling, axis=1)
-    row_sum = jnp.sum(to_all_dp(row_part), axis=0)
-    shares = lax.psum_scatter(
-        lax.dot_general(
-            data_latents,
-            coupling.astype(jnp.bfloat16),
-            (((0,), (1,)), ((), ())),
-            preferred_element_type=jnp.float32,
-        ).astype(jnp.bfloat16),
-        "dp",
-        scatter_dimension=0,
-        tiled=True,
-    ).astype(jnp.float32)
-    return (shares.T / row_sum[:, None]).astype(jnp.bfloat16)
+    weights = coupling.astype(jnp.bfloat16)
+    total = scattered_sums(
+        (weights, shift(weights, 0, 0, 1), data_latents, data_other), y, z, core
+    )
+    row_sum = jnp.sum(to_all_dp(jnp.sum(coupling, axis=1)), axis=0)
+    return (total / row_sum[:, None]).astype(jnp.bfloat16)
 
 
 def solution(mesh):

time: 284 us -> 253 us (0.89)
  waiting for transfers between devices: 169 us -> 102 us
  Pallas kernels: 0 us -> 29 us
  starting transfers between devices: 10.4 us -> 26.1 us
  matrix products: 31.4 us -> 17.5 us
    reduce_scatter x1 -> x0, waiting for transfers between devices: 89.5 us -> none  [body(): lax.psum_scatter(lax.dot_general(data_latents, coupling.astype(jnp.bfloat...]
    ppermute x0 -> x14, waiting for transfers between devices: none -> 32.8 us  [shift(): return lax.ppermute(values, 'dp', pairs)]
    pallas_call x0 -> x3, Pallas kernels: none -> 29 us  [the longest x2 17.8 us: sums(): pl.pallas_call(kernel, grid_spec=pltpu.PrefetchScalarGridSpec(num_scalar_...]
    ppermute x0 -> x14, starting transfers between devices: none -> 15.7 us  [shift(): return lax.ppermute(values, 'dp', pairs)]
    dot_general x1 -> x0, matrix products: 14 us -> none  [body(): lax.dot_general(data_latents, coupling.astype(jnp.bfloat16), (((0,), (1,)...]
    all_gather x1, waiting for transfers between devices: 66.7 us -> 56.3 us  [body(): piece = lax.all_gather(noise_latents, 'dp', axis=1, tiled=True)]
  transfers between devices with their start and end apart: 11 -> 24, of which waited for: 10 -> 14; matrix products, arithmetic and copies ran while one was open for 3% -> 11% of each run, Pallas kernels for 0% -> 7%
where the time goes in v2:
time: 253 us; the launch traced here: 251 us
  waiting for transfers between devices  102 us (40%)
  blocking collectives  46.2 us (18%)
  Pallas kernels  29 us (11%)
  starting transfers between devices  26.1 us (10%)
  matrix products  17.5 us (7%)
  other arithmetic  15.1 us (6%)
  between operations  13.8 us (5%)
    all_gather x1, waiting for transfers between devices, body(): piece = lax.all_gather(noise_latents, 'dp', axis=1, tiled=True)  56.3 us
    all_to_all x4, blocking collectives, to_all_dp(): lax.all_to_all(jnp.broadcast_to(values[None], (n,) + values.shape), 'dp',...  46.2 us
    ppermute x14, waiting for transfers between devices, shift(): return lax.ppermute(values, 'dp', pairs)  32.8 us
    pallas_call x2, Pallas kernels, sums(): pl.pallas_call(kernel, grid_spec=pltpu.PrefetchScalarGridSpec(num_scalar_...  17.8 us
    dot_general x1, matrix products, body(): lax.dot_general(piece, data_latents, (((1,), (1,)), ((), ())), preferred_...  17.5 us
    ppermute x14, starting transfers between devices, shift(): return lax.ppermute(values, 'dp', pairs)  15.7 us
    ppermute x9, waiting for transfers between devices, to_all_noise(): lax.ppermute(values, 'noise', [(i, (i + k) % n) for i in range(n)])  12.3 us
    pallas_call x1, Pallas kernels, other_columns(): pl.pallas_call(kernel, grid_spec=pltpu.PrefetchScalarGridSpec(num_scalar_...  11.1 us
  transfers between devices with their start and end apart: 24, of which 14 were waited for; matrix products, arithmetic and copies ran while one was open for 11% of the time, Pallas kernels for 7%

profile of v2, /device:TPU:0, one launch (start us, length us, event | category | flops | bytes accessed | tf_op | source)
XLA Modules:
  0.0 251.1 jit_solution(12868652378068595457)
XLA Ops:
  7.3 11.1 %shard_map.28 = bf16[384,8192]{1,0:T(8,128)(2,1)} custom-call(s32[1]{0:T(128)} %bitcast.7.core_ref, bf16[384,16384]{1,0:T(8,128)(2,1)} %d_own.3), custom_call_target="tpu_custom_call" | custom-call | bytes 12582912 | tf_op jit(solution)/shard_map/pallas_call | solution.py:55
  18.6 7.4 %multiply_reduce_fusion = f32[384]{0:T(512)S(1)} fusion(bf16[384,16384]{1,0:T(8,128)(2,1)} %d_own.3), kind=kLoop, calls=%fused_computation | loop fusion | flops 18873984 | bytes 12584448 | tf_op jit(solution)/shard_map/reduce_sum | solution.py:205
  26.1 56.3 %all-gather.2.cloned.1.call-done = bf16[384,16384]{1,0:T(8,128)(2,1)} async-done(((bf16[384,512]{1,0:T(8,128)(2,1)}), bf16[384,16384]{1,0:T(8,128)(2,1)}) %all-gather.2.cloned.1.call-update) | async-done | bytes 12582928 | tf_op jit(solution)/shard_map/all_gather | solution.py:197
  82.4 17.5 %add_reduce_fusion.4 = (f32[384]{0:T(512)S(1)}, f32[384,384]{1,0:T(8,128)S(1)}) fusion(f32[384]{0:T(512)S(1)} %multiply_subtract_fusion, bf16[384,16384]{1,0:T(8,128)(2,1)} %all-gather.2.cloned.1.call-done, bf16[384,16384]{1,0:T(8,128)(2,1)} %d_own.3), kind=kOutput, calls=%fused_computation.17 | convolution fusion | flops 4832280064 | bytes 25758720 | tf_op jit(solution)/shard_map/dot_general | solution.py:199
  100.2 13.2 %all_to_all.29 = f32[32,2,384]{2,1,0:T(2,128)S(1)} all-to-all(f32[32,2,384]{2,1,0:T(2,128)S(1)} %broadcast_in_dim.11), channel_id=1, replica_groups=mesh['dp'=32,'noise'=4] {'dp'}, dimensions={0} | all-to-all | bytes 196608 | tf_op jit(solution)/shard_map/all_to_all | solution.py:33
  113.9 2.8 %collective-permute-start.2 = (f32[384]{0:T(512)S(1)}, f32[384]{0:T(512)S(1)}, u32[]{:S(2)}, u32[]{:S(2)}) collective-permute-start(f32[384]{0:T(512)S(1)} %log_add_fusion.4), channel_id=1, source_target_pairs={{0,3},{1,0},{2,1},{3,2},{4,7},{5,4},{6,5},{7,6},{8,11},{9,8},{10,9... | collective-permute-start | bytes 4616 | tf_op jit(solution)/shard_map/ppermute | solution.py:43
  118.4 3.4 %collective-permute-done.1 = f32[384]{0:T(512)S(1)} collective-permute-done((f32[384]{0:T(512)S(1)}, f32[384]{0:T(512)S(1)}, u32[]{:S(2)}, u32[]{:S(2)}) %collective-permute-start.1) | collective-permute-done | bytes 1568 | tf_op jit(solution)/shard_map/ppermute | solution.py:43
  122.9 10.9 %all_to_all.30 = f32[32,1,384]{2,1,0:T(1,128)S(1)} all-to-all(f32[32,1,384]{2,1,0:T(1,128)S(1)} %broadcast_in_dim.12), channel_id=1, replica_groups=mesh['dp'=32,'noise'=4] {'dp'}, dimensions={0} | all-to-all | bytes 98304 | tf_op jit(solution)/shard_map/all_to_all | solution.py:33
  134.6 1.4 collective-permute-start.4
  136.0 1.2 collective-permute-start.3
  137.8 1.8 collective-permute-done.4
  139.7 1.1 collective-permute-done.3
  141.3 10.8 %all_to_all.31 = f32[32,1,384]{2,1,0:T(1,128)S(1)} all-to-all(f32[32,1,384]{2,1,0:T(1,128)S(1)} %broadcast_in_dim.13), channel_id=1, replica_groups=mesh['dp'=32,'noise'=4] {'dp'}, dimensions={0} | all-to-all | bytes 98304 | tf_op jit(solution)/shard_map/all_to_all | solution.py:33
  152.6 2.0 collective-permute-start.8
  156.4 3.3 %collective-permute-done.7 = f32[384]{0:T(512)S(1)} collective-permute-done((f32[384]{0:T(512)S(1)}, f32[384]{0:T(512)S(1)}, u32[]{:S(2)}, u32[]{:S(2)}) %collective-permute-start.7) | collective-permute-done | bytes 1568 | tf_op jit(solution)/shard_map/ppermute | solution.py:43
  161.0 1.3 collective-permute-done.9.w_oth
  162.3 10.2 %shard_map.30 = (bf16[3,192,512]{2,1,0:T(8,128)(2,1)}, bf16[3,192,512]{2,1,0:T(8,128)(2,1)S(1)}, bf16[3,192,512]{2,1,0:T(8,128)(2,1)S(1)}, bf16[3,192,512]{2,1,0...) custom-call(s32[10]{0:T(128)S(1)} %stack.136.where, ...), custom_call_target="tpu_custom_call" | custom-call | flops 2717908992 | bytes 10616832 | tf_op jit(solution)/shard_map/pallas_call | solution.py:81
  173.3 1.2 collective-permute-start.11
  175.4 2.5 collective-permute-start.13
  177.9 1.1 collective-permute-start.15
  179.9 11.4 %collective-permute-done.11 = bf16[3,192,512]{2,1,0:T(8,128)(2,1)} collective-permute-done((bf16[3,192,512]{2,1,0:T(8,128)(2,1)}, bf16[3,192,512]{2,1,0:T(8,128)(2,1)}, u32[]{:S(2)}, u32[]{:S(2)}) %collective-permute-start.11) | collective-permute-done | bytes 589856 | tf_op jit(solution)/shard_map/ppermute | solution.py:22
  191.3 1.2 collective-permute-start.17
  192.5 7.6 %shard_map.29 = (bf16[3,384,512]{2,1,0:T(8,128)(2,1)S(1)}, bf16[3,384,512]{2,1,0:T(8,128)(2,1)S(1)}, bf16[384,512]{1,0:T(8,128)(2,1)S(1)}) custom-call(s32[8]{0:T(128)S(1)} %stack.112.where, bf16[384,384]{1,0:T(8,128)(2,1)S(1)} %get-tuple-element.32.w_own, bf16[384,384]{1,0:T(8,128)(2,1)S(1)} %collective-permute-done.9.w_oth, bf16[384,16384]{1,0:T(8,128)(2,1)} %d_own.3, ...), custom_call_target="tpu_custom_call" | custom-call | flops 2113929216 | bytes 8257536 | tf_op jit(solution)/shard_map/pallas_call | solution.py:81
  200.2 2.8 %collective-permute-done.12 = bf16[3,192,512]{2,1,0:T(8,128)(2,1)S(1)} collective-permute-done((bf16[3,192,512]{2,1,0:T(8,128)(2,1)}, bf16[3,192,512]{2,1,0:T(8,128)(2,1)S(1)}, u32[]{:S(2)}, u32[]{:S(2)}) %collective-permute-start.12) | collective-permute-done | bytes 589856 | tf_op jit(solution)/shard_map/ppermute | solution.py:22
  203.0 3.5 %collective-permute-done.16 = bf16[3,192,512]{2,1,0:T(8,128)(2,1)S(1)} collective-permute-done((bf16[3,192,512]{2,1,0:T(8,128)(2,1)S(1)}, bf16[3,192,512]{2,1,0:T(8,128)(2,1)S(1)}, u32[]{:S(2)}, u32[]{:S(2)}) %collective-permute-start.16) | collective-permute-done | bytes 589856 | tf_op jit(solution)/shard_map/ppermute | solution.py:22
  206.6 1.8 add_convert_fusion
  208.5 3.3 %collective-permute-start.22 = (bf16[384,512]{1,0:T(8,128)(2,1)S(1)}, bf16[384,512]{1,0:T(8,128)(2,1)}, u32[]{:S(2)}, u32[]{:S(2)}) collective-permute-start(bf16[384,512]{1,0:T(8,128)(2,1)S(1)} %pad_maximum_fusion.5), channel_id=1, source_target_pairs={{0,96},{4,100},{8,104},{12,108},{16,112},{20,116},{24,120},{28,124... | collective-permute-start | bytes 1179656 | tf_op jit(solution)/shard_map/ppermute | solution.py:22
  212.7 2.7 %collective-permute-start.21 = (bf16[384,512]{1,0:T(8,128)(2,1)S(1)}, bf16[384,512]{1,0:T(8,128)(2,1)}, u32[]{:S(2)}, u32[]{:S(2)}) collective-permute-start(bf16[384,512]{1,0:T(8,128)(2,1)S(1)} %pad_maximum_fusion.4), channel_id=1, source_target_pairs={{0,24},{4,28},{8,0},{12,4},{16,8},{20,12},{24,16},{28,20},{32,56},... | collective-permute-start | bytes 1179656 | tf_op jit(solution)/shard_map/ppermute | solution.py:22
  215.5 13.7 %collective-permute-done.20 = bf16[384,512]{1,0:T(8,128)(2,1)S(1)} collective-permute-done((bf16[384,512]{1,0:T(8,128)(2,1)S(1)}, bf16[384,512]{1,0:T(8,128)(2,1)S(1)}, u32[]{:S(2)}, u32[]{:S(2)}) %collective-permute-start.20) | collective-permute-done | bytes 393248 | tf_op jit(solution)/shard_map/ppermute | solution.py:22
  229.2 1.1 collective-permute-start.14
  230.3 11.4 %all_to_all.32 = f32[32,1,384]{2,1,0:T(1,128)S(1)} all-to-all(f32[32,1,384]{2,1,0:T(1,128)S(1)} %broadcast_in_dim.14), channel_id=1, replica_groups=mesh['dp'=32,'noise'=4] {'dp'}, dimensions={0} | all-to-all | bytes 98304 | tf_op jit(solution)/shard_map/all_to_all | solution.py:33
  241.8 2.5 %divide_convert_fusion = bf16[384,512]{1,0:T(8,128)(2,1)} fusion(bf16[384,512]{1,0:T(8,128)(2,1)} %collective-permute-done.22, bf16[384,512]{1,0:T(8,128)(2,1)} %collective-permute-done.21, bf16[384,512]{1,0:T(8,128)(2,1)S(1)} %collective-permute-done.20, bf16[384,512]{1,0:T(8,128)(2,1)} %collective-permute-done.19, ...), kind=kLoop, calls=%fused_computation.4 | loop fusion | flops 2949120 | bytes 3147264 | tf_op jit(solution)/shard_map/convert_element_type | solution.py:228
  (102 shorter events, 13.7 us)
Async XLA Ops:
  6.5 75.8 %all-gather.2.cloned.1.call-start = ((), (), s32[]{:S(2)}) async-start(), calls=%async_computation.4 | async-start | bytes 12976128 | tf_op jit(solution)/shard_map/all_gather | solution.py:197
  7.3 11.2 %copy-start.1 = (bf16[384,512]{1,0:T(8,128)(2,1)S(1)}, bf16[384,512]{1,0:T(8,128)(2,1)}, u32[]{:S(2)}) copy-start(bf16[384,512]{1,0:T(8,128)(2,1)} %param.2) | copy-start | bytes 1179652
  18.4 142.5 %collective-permute-start.10 = (bf16[384,8192]{1,0:T(8,128)(2,1)}, bf16[384,8192]{1,0:T(8,128)(2,1)}, u32[]{:S(2)}, u32[]{:S(2)}) collective-permute-start(bf16[384,8192]{1,0:T(8,128)(2,1)} %shard_map.28), channel_id=1, source_target_pairs={{0,4},{4,0},{8,12},{12,8},{16,20},{20,16},{24,28},{28,24},{32,36},... | collective-permute-start | bytes 18874376 | tf_op jit(solution)/shard_map/ppermute | solution.py:22
  113.9 4.5 %collective-permute-start.2 = (f32[384]{0:T(512)S(1)}, f32[384]{0:T(512)S(1)}, u32[]{:S(2)}, u32[]{:S(2)}) collective-permute-start(f32[384]{0:T(512)S(1)} %log_add_fusion.4), channel_id=1, source_target_pairs={{0,3},{1,0},{2,1},{3,2},{4,7},{5,4},{6,5},{7,6},{8,11},{9,8},{10,9... | collective-permute-start | bytes 4616 | tf_op jit(solution)/shard_map/ppermute | solution.py:43
  116.7 5.1 %collective-permute-start.1 = (f32[384]{0:T(512)S(1)}, f32[384]{0:T(512)S(1)}, u32[]{:S(2)}, u32[]{:S(2)}) collective-permute-start(f32[384]{0:T(512)S(1)} %log_add_fusion.4), channel_id=1, source_target_pairs={{0,2},{1,3},{2,0},{3,1},{4,6},{5,7},{6,4},{7,5},{8,10},{9,11},{10,... | collective-permute-start | bytes 4616 | tf_op jit(solution)/shard_map/ppermute | solution.py:43
  117.5 4.8 %collective-permute-start = (f32[384]{0:T(512)S(1)}, f32[384]{0:T(512)S(1)}, u32[]{:S(2)}, u32[]{:S(2)}) collective-permute-start(f32[384]{0:T(512)S(1)} %log_add_fusion.4), channel_id=1, source_target_pairs={{0,1},{1,2},{2,3},{3,0},{4,5},{5,6},{6,7},{7,4},{8,9},{9,10},{10,1... | collective-permute-start | bytes 4616 | tf_op jit(solution)/shard_map/ppermute | solution.py:43
  134.2 3.7 %collective-permute-start.5 = (f32[384]{0:T(512)S(1)}, f32[384]{0:T(512)S(1)}, u32[]{:S(2)}, u32[]{:S(2)}) collective-permute-start(f32[384]{0:T(512)S(1)} %log_add_fusion.2), channel_id=1, source_target_pairs={{0,3},{1,0},{2,1},{3,2},{4,7},{5,4},{6,5},{7,6},{8,11},{9,8},{10,9... | collective-permute-start | bytes 4616 | tf_op jit(solution)/shard_map/ppermute | solution.py:43
  134.6 5.1 %collective-permute-start.4 = (f32[384]{0:T(512)S(1)}, f32[384]{0:T(512)S(1)}, u32[]{:S(2)}, u32[]{:S(2)}) collective-permute-start(f32[384]{0:T(512)S(1)} %log_add_fusion.2), channel_id=1, source_target_pairs={{0,2},{1,3},{2,0},{3,1},{4,6},{5,7},{6,4},{7,5},{8,10},{9,11},{10,... | collective-permute-start | bytes 4616 | tf_op jit(solution)/shard_map/ppermute | solution.py:43
  136.0 4.8 %collective-permute-start.3 = (f32[384]{0:T(512)S(1)}, f32[384]{0:T(512)S(1)}, u32[]{:S(2)}, u32[]{:S(2)}) collective-permute-start(f32[384]{0:T(512)S(1)} %log_add_fusion.2), channel_id=1, source_target_pairs={{0,1},{1,2},{2,3},{3,0},{4,5},{5,6},{6,7},{7,4},{8,9},{9,10},{10,1... | collective-permute-start | bytes 4616 | tf_op jit(solution)/shard_map/ppermute | solution.py:43
  152.6 3.8 %collective-permute-start.8 = (f32[384]{0:T(512)S(1)}, f32[384]{0:T(512)S(1)}, u32[]{:S(2)}, u32[]{:S(2)}) collective-permute-start(f32[384]{0:T(512)S(1)} %log_add_fusion), channel_id=1, source_target_pairs={{0,3},{1,0},{2,1},{3,2},{4,7},{5,4},{6,5},{7,6},{8,11},{9,8},{10,9... | collective-permute-start | bytes 4616 | tf_op jit(solution)/shard_map/ppermute | solution.py:43
  154.6 5.1 %collective-permute-start.7 = (f32[384]{0:T(512)S(1)}, f32[384]{0:T(512)S(1)}, u32[]{:S(2)}, u32[]{:S(2)}) collective-permute-start(f32[384]{0:T(512)S(1)} %log_add_fusion), channel_id=1, source_target_pairs={{0,2},{1,3},{2,0},{3,1},{4,6},{5,7},{6,4},{7,5},{8,10},{9,11},{10,... | collective-permute-start | bytes 4616 | tf_op jit(solution)/shard_map/ppermute | solution.py:43
  155.5 4.8 %collective-permute-start.6 = (f32[384]{0:T(512)S(1)}, f32[384]{0:T(512)S(1)}, u32[]{:S(2)}, u32[]{:S(2)}) collective-permute-start(f32[384]{0:T(512)S(1)} %log_add_fusion), channel_id=1, source_target_pairs={{0,1},{1,2},{2,3},{3,0},{4,5},{5,6},{6,7},{7,4},{8,9},{9,10},{10,1... | collective-permute-start | bytes 4616 | tf_op jit(solution)/shard_map/ppermute | solution.py:43
  160.6 1.7 collective-permute-start.9
  172.5 0.8 copy-start
  173.3 18.0 %collective-permute-start.11 = (bf16[3,192,512]{2,1,0:T(8,128)(2,1)}, bf16[3,192,512]{2,1,0:T(8,128)(2,1)}, u32[]{:S(2)}, u32[]{:S(2)}) collective-permute-start(bf16[3,192,512]{2,1,0:T(8,128)(2,1)} %get-tuple-element.16), channel_id=1, source_target_pairs={{0,64},{4,68},{8,72},{12,76},{16,80},{20,84},{24,88},{28,92},{32,9... | collective-permute-start | bytes 1769480 | tf_op jit(solution)/shard_map/ppermute | solution.py:22
  174.6 28.4 %collective-permute-start.12 = (bf16[3,192,512]{2,1,0:T(8,128)(2,1)}, bf16[3,192,512]{2,1,0:T(8,128)(2,1)S(1)}, u32[]{:S(2)}, u32[]{:S(2)}) collective-permute-start(bf16[3,192,512]{2,1,0:T(8,128)(2,1)} %copy-done), channel_id=1, source_target_pairs={{0,32},{4,36},{8,40},{12,44},{16,48},{20,52},{24,56},{28,60},{32,6... | collective-permute-start | bytes 1769480 | tf_op jit(solution)/shard_map/ppermute | solution.py:22
  175.4 27.6 %collective-permute-start.13 = (bf16[3,192,512]{2,1,0:T(8,128)(2,1)S(1)}, bf16[3,192,512]{2,1,0:T(8,128)(2,1)S(1)}, u32[]{:S(2)}, u32[]{:S(2)}) collective-permute-start(bf16[3,192,512]{2,1,0:T(8,128)(2,1)S(1)} %get-tuple-element.18), channel_id=1, source_target_pairs={{0,96},{4,100},{8,104},{12,108},{16,112},{20,116},{24,120},{28,124... | collective-permute-start | bytes 1769480 | tf_op jit(solution)/shard_map/ppermute | solution.py:22
  177.9 25.2 %collective-permute-start.15 = (bf16[3,192,512]{2,1,0:T(8,128)(2,1)S(1)}, bf16[3,192,512]{2,1,0:T(8,128)(2,1)S(1)}, u32[]{:S(2)}, u32[]{:S(2)}) collective-permute-start(bf16[3,192,512]{2,1,0:T(8,128)(2,1)S(1)} %get-tuple-element.20), channel_id=1, source_target_pairs={{0,16},{4,20},{8,24},{12,28},{16,0},{20,4},{24,8},{28,12},{32,48},... | collective-permute-start | bytes 1769480 | tf_op jit(solution)/shard_map/ppermute | solution.py:22
  179.0 27.6 %collective-permute-start.16 = (bf16[3,192,512]{2,1,0:T(8,128)(2,1)S(1)}, bf16[3,192,512]{2,1,0:T(8,128)(2,1)S(1)}, u32[]{:S(2)}, u32[]{:S(2)}) collective-permute-start(bf16[3,192,512]{2,1,0:T(8,128)(2,1)S(1)} %get-tuple-element.21), channel_id=1, source_target_pairs={{0,8},{4,12},{8,16},{12,20},{16,24},{20,28},{24,0},{28,4},{32,40},... | collective-permute-start | bytes 1769480 | tf_op jit(solution)/shard_map/ppermute | solution.py:22
  191.3 15.2 %collective-permute-start.17 = (bf16[3,192,512]{2,1,0:T(8,128)(2,1)S(1)}, bf16[3,192,512]{2,1,0:T(8,128)(2,1)S(1)}, u32[]{:S(2)}, u32[]{:S(2)}) collective-permute-start(bf16[3,192,512]{2,1,0:T(8,128)(2,1)S(1)} %get-tuple-element.22), channel_id=1, source_target_pairs={{0,24},{4,28},{8,0},{12,4},{16,8},{20,12},{24,16},{28,20},{32,56},... | collective-permute-start | bytes 1769480 | tf_op jit(solution)/shard_map/ppermute | solution.py:22
  208.4 20.7 %collective-permute-start.20 = (bf16[384,512]{1,0:T(8,128)(2,1)S(1)}, bf16[384,512]{1,0:T(8,128)(2,1)S(1)}, u32[]{:S(2)}, u32[]{:S(2)}) collective-permute-start(bf16[384,512]{1,0:T(8,128)(2,1)S(1)} %pad_maximum_fusion.3), channel_id=1, source_target_pairs={{0,32},{4,36},{8,40},{12,44},{16,48},{20,52},{24,56},{28,60},{32,6... | collective-permute-start | bytes 1179656 | tf_op jit(solution)/shard_map/ppermute | solution.py:22
  208.5 33.2 %collective-permute-start.22 = (bf16[384,512]{1,0:T(8,128)(2,1)S(1)}, bf16[384,512]{1,0:T(8,128)(2,1)}, u32[]{:S(2)}, u32[]{:S(2)}) collective-permute-start(bf16[384,512]{1,0:T(8,128)(2,1)S(1)} %pad_maximum_fusion.5), channel_id=1, source_target_pairs={{0,96},{4,100},{8,104},{12,108},{16,112},{20,116},{24,120},{28,124... | collective-permute-start | bytes 1179656 | tf_op jit(solution)/shard_map/ppermute | solution.py:22
  211.8 29.9 %collective-permute-start.18 = (bf16[384,512]{1,0:T(8,128)(2,1)S(1)}, bf16[384,512]{1,0:T(8,128)(2,1)}, u32[]{:S(2)}, u32[]{:S(2)}) collective-permute-start(bf16[384,512]{1,0:T(8,128)(2,1)S(1)} %pad_maximum_fusion.1), channel_id=1, source_target_pairs={{0,64},{4,68},{8,72},{12,76},{16,80},{20,84},{24,88},{28,92},{32,9... | collective-permute-start | bytes 1179656 | tf_op jit(solution)/shard_map/ppermute | solution.py:22
  212.0 29.7 %collective-permute-start.19 = (bf16[384,512]{1,0:T(8,128)(2,1)S(1)}, bf16[384,512]{1,0:T(8,128)(2,1)}, u32[]{:S(2)}, u32[]{:S(2)}) collective-permute-start(bf16[384,512]{1,0:T(8,128)(2,1)S(1)} %pad_maximum_fusion.2), channel_id=1, source_target_pairs={{0,8},{4,12},{8,16},{12,20},{16,24},{20,28},{24,0},{28,4},{32,40},... | collective-permute-start | bytes 1179656 | tf_op jit(solution)/shard_map/ppermute | solution.py:22
  212.7 29.1 %collective-permute-start.21 = (bf16[384,512]{1,0:T(8,128)(2,1)S(1)}, bf16[384,512]{1,0:T(8,128)(2,1)}, u32[]{:S(2)}, u32[]{:S(2)}) collective-permute-start(bf16[384,512]{1,0:T(8,128)(2,1)S(1)} %pad_maximum_fusion.4), channel_id=1, source_target_pairs={{0,24},{4,28},{8,0},{12,4},{16,8},{20,12},{24,16},{28,20},{32,56},... | collective-permute-start | bytes 1179656 | tf_op jit(solution)/shard_map/ppermute | solution.py:22
  229.2 12.6 %collective-permute-start.14 = (bf16[384,512]{1,0:T(8,128)(2,1)S(1)}, bf16[384,512]{1,0:T(8,128)(2,1)S(1)}, u32[]{:S(2)}, u32[]{:S(2)}) collective-permute-start(bf16[384,512]{1,0:T(8,128)(2,1)S(1)} %pad_maximum_fusion), channel_id=1, source_target_pairs={{0,16},{4,20},{8,24},{12,28},{16,0},{20,4},{24,8},{28,12},{32,48},... | collective-permute-start | bytes 1179656 | tf_op jit(solution)/shard_map/ppermute | solution.py:22
Sparse Core Ops, SparseCore 0:
  9.5 72.7 all-gather.1

commit v3 on v1

--- a/solution.py
+++ b/solution.py
@@ -1,10 +1,45 @@
 import jax
 import jax.numpy as jnp
 from jax import lax
+from jax.experimental import pallas as pl
+from jax.experimental.pallas import tpu as pltpu
 from jax.sharding import PartitionSpec as P
 
 ITERS = 3
 EPS = 0.004
+SIDE = 4
+OFFS = (2, 1, 3)
+BLOCKS = SIDE * SIDE
+VMEM = 48 * 1024 * 1024
+
+
+def swap(values):
+    n = lax.axis_size("dp")
+    return lax.ppermute(values, "dp", [(i, i ^ 1) for i in range(n)])
+
+
+def hop(values, k, first):
+    pairs = []
+    for y in range(SIDE):
+        for z in range(SIDE):
+            for c in range(2):
+                along_z = (c == 0) == first
+                to_y, to_z = (y, (z + k) % SIDE) if along_z else ((y + k) % SIDE, z)
+                pairs.append(((y * SIDE + z) * 2 + c, (to_y * SIDE + to_z) * 2 + c))
+    return lax.ppermute(values, "dp", pairs)
+
+
+def block_ids(y, z, core):
+    spots = [(0, 0, 0)]
+    spots += [(0, m, b) for m in OFFS for b in (0, 1)]
+    spots += [(k, m, 0) for k in OFFS for m in OFFS]
+    ids = []
+    for k, m, b in spots:
+        dy = jnp.where(core == 0, k, m)
+        dz = jnp.where(core == 0, m, k)
+        chip = ((y + dy) % SIDE) * SIDE + (z + dz) % SIDE
+        ids.append(chip * 2 + jnp.where(core == 0, b, 1 - b))
+    return jnp.stack(ids).astype(jnp.int32)
 
 
 def lse(values, axis):
@@ -30,12 +65,234 @@
     return jnp.stack(parts)
 
 
+def call(kernel, ids, ins, out_shape, scratch, flops, moved):
+    return pl.pallas_call(
+        kernel,
+        in_specs=[pl.BlockSpec(memory_space=pltpu.SMEM)]
+        + [pl.BlockSpec(memory_space=pl.ANY)] * len(ins),
+        out_specs=[pl.BlockSpec(memory_space=pl.ANY)] * len(out_shape),
+        out_shape=out_shape,
+        scratch_shapes=scratch,
+        compiler_params=pltpu.CompilerParams(vmem_limit_bytes=VMEM),
+        cost_estimate=pl.CostEstimate(
+            flops=flops, bytes_accessed=moved, transcendentals=0
+        ),
+    )(ids, *ins)
+
+
+def columns(ref, place, block):
+    return ref.at[:, pl.ds(pl.multiple_of(place * block, block), block)]
+
+
+def picked_columns(data, ids):
+    rows, width = data.shape
+    block = width // (2 * BLOCKS)
+
+    def kernel(ids_ref, in_ref, out_ref, sems):
+        copies = []
+        for t in range(BLOCKS):
+            copies.append(
+                pltpu.make_async_copy(
+                    columns(in_ref, ids_ref[t], block),
+                    out_ref.at[:, pl.ds(t * block, block)],
+                    sems.at[t],
+                )
+            )
+            copies[-1].start()
+        for copy in copies:
+            copy.wait()
+
+    return call(
+        kernel,
+        ids,
+        [data],
+        [jax.ShapeDtypeStruct((rows, width // 2), data.dtype)],
+        [pltpu.SemaphoreType.DMA((BLOCKS,))],
+        0,
+        rows * width * 2,
+    )[0]
+
+
+def part_dots(ids, start, groups, data, data_other, before):
+    sizes = [g.shape[0] for g in groups]
+    n = sum(sizes)
+    rows, block = groups[0].shape[1:]
+    inner = data.shape[0]
+    spots = [(a, i) for a, size in enumerate(sizes) for i in range(size)]
+    n_in = len(groups) + 2 + (0 if before is None else 2)
+
+    def kernel(ids_ref, *refs):
+        ins, (own, oth) = refs[:n_in], refs[n_in : n_in + 2]
+        pieces, d_own, d_oth, acc, sems, acc_sems = refs[n_in + 2 :]
+        data_ref, data_other_ref = ins[len(groups) : len(groups) + 2]
+        copies = []
+        if before is not None:
+            for b in range(2):
+                copy = pltpu.make_async_copy(
+                    ins[len(groups) + 2 + b], acc.at[b], acc_sems.at[b]
+                )
+                copy.start()
+                copies.append(copy)
+        steps = []
+        for t, (a, i) in enumerate(spots):
+            sources = (
+                ins[a].at[i],
+                columns(data_ref, ids_ref[t + start], block),
+                data_other_ref.at[:, pl.ds((t + start) * block, block)],
+            )
+            steps.append(
+                [
+                    pltpu.make_async_copy(source, to.at[t], sems.at[b, t])
+                    for b, (source, to) in enumerate(
+                        zip(sources, (pieces, d_own, d_oth))
+                    )
+                ]
+            )
+            for copy in steps[-1]:
+                copy.start()
+        for copy in copies:
+            copy.wait()
+        for t, step in enumerate(steps):
+            for copy in step:
+                copy.wait()
+            for b, d in enumerate((d_own, d_oth)):
+                part = lax.dot_general(
+                    pieces[t],
+                    d[t],
+                    (((1,), (1,)), ((), ())),
+                    preferred_element_type=jnp.float32,
+                )
+                if t == 0 and before is None:
+                    acc[b] = part
+                else:
+                    acc[b] += part
+        copies = []
+        for b, out in enumerate((own, oth)):
+            copies.append(pltpu.make_async_copy(acc.at[b], out, acc_sems.at[b]))
+            copies[-1].start()
+        for copy in copies:
+            copy.wait()
+
+    shape = jax.ShapeDtypeStruct((rows, inner), jnp.float32)
+    return call(
+        kernel,
+        ids,
+        list(groups) + [data, data_other] + ([] if before is None else list(before)),
+        [shape, shape],
+        [
+            pltpu.VMEM((n, rows, block), data.dtype),
+            pltpu.VMEM((n, inner, block), data.dtype),
+            pltpu.VMEM((n, inner, block), data.dtype),
+            pltpu.VMEM((2, rows, inner), jnp.float32),
+            pltpu.SemaphoreType.DMA((3, n)),
+            pltpu.SemaphoreType.DMA((2,)),
+        ],
+        n * 4 * rows * inner * block,
+        n * block * (4 * inner + 2 * rows),
+    )
+
+
+def gathered_dots(noise, data, data_other, ids):
+    both = jnp.stack([noise, swap(noise)])
+    first = [hop(both, -k, True) for k in OFFS]
+    passing = jnp.stack([got[0] for got in first])
+    second = [hop(passing, -k, False) for k in OFFS]
+    dots = part_dots(ids, 0, [noise[None]] + first, data, data_other, None)
+    own, other = part_dots(ids, 7, second, data, data_other, dots)
+    return own + swap(other)
+
+
+def part_sums(ids, start, sizes, ins):
+    rows, inner = ins[0].shape
+    dtype = ins[2].dtype
+    block = ins[3].shape[1] // BLOCKS
+    spots = [(a, i) for a, size in enumerate(sizes) for i in range(size)]
+    n = len(spots)
+
+    def kernel(ids_ref, w_own_ref, w_oth_ref, data_ref, data_other_ref, *refs):
+        outs = refs[: len(sizes)]
+        weights, d_own, d_oth, totals, w_sems, sems = refs[len(sizes) :]
+        first = []
+        for b, w in enumerate((w_own_ref, w_oth_ref)):
+            first.append(pltpu.make_async_copy(w, weights.at[b], w_sems.at[b]))
+            first[-1].start()
+        steps = []
+        for t in range(n):
+            sources = (
+                columns(data_ref, ids_ref[t + start], block),
+                data_other_ref.at[:, pl.ds((t + start) * block, block)],
+            )
+            steps.append(
+                [
+                    pltpu.make_async_copy(source, to.at[t], sems.at[b, t])
+                    for b, (source, to) in enumerate(zip(sources, (d_own, d_oth)))
+                ]
+            )
+            for copy in steps[-1]:
+                copy.start()
+        for copy in first:
+            copy.wait()
+        last = []
+        for t, (a, i) in enumerate(spots):
+            for copy in steps[t]:
+                copy.wait()
+            total = jnp.dot(weights[0], d_own[t], preferred_element_type=jnp.float32)
+            total += jnp.dot(weights[1], d_oth[t], preferred_element_type=jnp.float32)
+            totals[t] = total.astype(dtype)
+            last.append(pltpu.make_async_copy(totals.at[t], outs[a].at[i], sems.at[2, t]))
+            last[-1].start()
+        for copy in last:
+            copy.wait()
+
+    return call(
+        kernel,
+        ids,
+        ins,
+        [jax.ShapeDtypeStruct((size, rows, block), dtype) for size in sizes],
+        [
+            pltpu.VMEM((2, rows, inner), dtype),
+            pltpu.VMEM((n, inner, block), dtype),
+            pltpu.VMEM((n, inner, block), dtype),
+            pltpu.VMEM((n, rows, block), dtype),
+            pltpu.SemaphoreType.DMA((2,)),
+            pltpu.SemaphoreType.DMA((3, n)),
+        ],
+        n * 4 * rows * inner * block,
+        n * (4 * inner * block + 2 * rows * block),
+    )
+
+
+def added(first, others):
+    total = first.astype(jnp.float32)
+    for other in others:
+        total += other.astype(jnp.float32)
+    return total
+
+
+def scattered_sums(ids, ins, row_part):
+    far = part_sums(ids, 7, [3, 3, 3], ins)
+    got = [hop(part, k, False) for part, k in zip(far, OFFS)]
+    mine, *near = part_sums(ids, 0, [1, 2, 2, 2], ins)
+    row_part, *near = lax.optimization_barrier((row_part, *near))
+    row_sum = jnp.sum(to_all_dp(row_part), axis=0)
+    row_sum, *got = lax.optimization_barrier((row_sum, *got))
+    last = []
+    for a, k in enumerate(OFFS):
+        total = added(near[a][0], [g[a] for g in got]).astype(jnp.bfloat16)
+        last.append(hop(jnp.stack([total, near[a][1]]), k, True))
+    other = added(last[0][1], [g[1] for g in last[1:]])
+    return added(mine[0], [g[0] for g in last] + [swap(other)]), row_sum
+
+
 def body(noise_latents, data_latents):
     width = data_latents.shape[1]
-    piece = lax.all_gather(noise_latents, "dp", axis=1, tiled=True)
-    dots = lax.dot_general(
-        piece, data_latents, (((1,), (1,)), ((), ())), preferred_element_type=jnp.float32
-    )
+    place = lax.axis_index("dp")
+    core = place % 2
+    z = (place // 2) % SIDE
+    y = place // (2 * SIDE)
+    ids = block_ids(y, z, core)
+    data_other = swap(picked_columns(data_latents, block_ids(y, z, 1 - core)))
+    dots = gathered_dots(noise_latents, data_latents, data_other, ids)
     noise_f = noise_latents.astype(jnp.float32)
     sx_part = jnp.sum(noise_f * noise_f, axis=1)
     data_f = data_latents.astype(jnp.float32)
@@ -57,20 +314,13 @@
         local = lse(twice + (f - sx)[:, None], 0)
         g = sy - lse(to_all_noise(local), 0)
     coupling = jnp.exp(twice + (f - sx)[:, None] + (g - sy)[None, :])
-    row_part = jnp.sum(coupling, axis=1)
-    row_sum = jnp.sum(to_all_dp(row_part), axis=0)
-    shares = lax.psum_scatter(
-        lax.dot_general(
-            data_latents,
-            coupling.astype(jnp.bfloat16),
-            (((0,), (1,)), ((), ())),
-            preferred_element_type=jnp.float32,
-        ).astype(jnp.bfloat16),
-        "dp",
-        scatter_dimension=0,
-        tiled=True,
-    ).astype(jnp.float32)
-    return (shares.T / row_sum[:, None]).astype(jnp.bfloat16)
+    weights = coupling.astype(jnp.bfloat16)
+    total, row_sum = scattered_sums(
+        ids,
+        (weights, swap(weights), data_latents, data_other),
+        jnp.sum(coupling, axis=1),
+    )
+    return (total / row_sum[:, None]).astype(jnp.bfloat16)
 
 
 def solution(mesh):

time: 284 us -> 404 us (1.42)
  Pallas kernels: 0 us -> 221 us
  waiting for transfers between devices: 169 us -> 85.4 us
  matrix products: 31.4 us -> 0 us
  starting transfers between devices: 10.4 us -> 41.6 us
  between operations: 13.5 us -> 0.37 us
  blocking collectives: 45.7 us -> 35.7 us
    pallas_call x0 -> x5, Pallas kernels: none -> 221 us  [call(): pl.pallas_call(kernel, in_specs=[pl.BlockSpec(memory_space=pltpu.SMEM)] +...]
    reduce_scatter x1 -> x0, waiting for transfers between devices: 89.5 us -> none  [body(): lax.psum_scatter(lax.dot_general(data_latents, coupling.astype(jnp.bfloat...]
    all_gather x1 -> x0, waiting for transfers between devices: 66.7 us -> none  [body(): piece = lax.all_gather(noise_latents, 'dp', axis=1, tiled=True)]
    ppermute x0 -> x17, waiting for transfers between devices: none -> 63.6 us  [the longest x12 53.3 us: hop(): return lax.ppermute(values, 'dp', pairs)]
    dot_general x2 -> x0, matrix products: 31.4 us -> none  [the longest x1 17.4 us: body(): lax.dot_general(piece, data_latents, (((1,), (1,)), ((), ())), preferred_...]
    ppermute x0 -> x17, starting transfers between devices: none -> 22.9 us  [the longest x12 21.7 us: hop(): return lax.ppermute(values, 'dp', pairs)]
    all_to_all x0 -> x1, waiting for transfers between devices: none -> 14 us  [to_all_dp(): lax.all_to_all(jnp.broadcast_to(values[None], (n,) + values.shape), 'dp',...]
    all_to_all x4 -> x3, blocking collectives: 45.7 us -> 35.7 us  [to_all_dp(): lax.all_to_all(jnp.broadcast_to(values[None], (n,) + values.shape), 'dp',...]
  transfers between devices with their start and end apart: 11 -> 27, of which waited for: 10 -> 18; matrix products, arithmetic and copies ran while one was open for 3% -> 3% of each run, Pallas kernels for 0% -> 3%
where the time goes in v3:
time: 404 us; the launch traced here: 402 us
  Pallas kernels  221 us (55%)
  waiting for transfers between devices  85.4 us (21%)
  starting transfers between devices  41.6 us (10%)
  blocking collectives  35.7 us (9%)
  other arithmetic  16.5 us (4%)
    pallas_call x5, Pallas kernels, call(): pl.pallas_call(kernel, in_specs=[pl.BlockSpec(memory_space=pltpu.SMEM)] +...  221 us
    ppermute x12, waiting for transfers between devices, hop(): return lax.ppermute(values, 'dp', pairs)  53.3 us
    all_to_all x3, blocking collectives, to_all_dp(): lax.all_to_all(jnp.broadcast_to(values[None], (n,) + values.shape), 'dp',...  35.7 us
    ppermute x12, starting transfers between devices, hop(): return lax.ppermute(values, 'dp', pairs)  21.7 us
    ppermute x9, starting transfers between devices, to_all_noise(): lax.ppermute(values, 'noise', [(i, (i + k) % n) for i in range(n)])  14.2 us
    all_to_all x1, waiting for transfers between devices, to_all_dp(): lax.all_to_all(jnp.broadcast_to(values[None], (n,) + values.shape), 'dp',...  14 us
    ppermute x5, waiting for transfers between devices, swap(): return lax.ppermute(values, 'dp', [(i, i ^ 1) for i in range(n)])  10.3 us
  transfers between devices with their start and end apart: 27, of which 18 were waited for; matrix products, arithmetic and copies ran while one was open for 3% of the time, Pallas kernels for 3%

profile of v3, /device:TPU:0, one launch (start us, length us, event | category | flops | bytes accessed | tf_op | source)
XLA Modules:
  0.0 402.1 jit_solution(11472580442441456536)
XLA Ops:
  0.1 192.4 %shard_map.28 = bf16[384,8192]{1,0:T(8,128)(2,1)} custom-call(s32[16]{0:T(128)S(1)} %stack.209.ids_ref, bf16[384,16384]{1,0:T(8,128)(2,1)} %data_ref.3), custom_call_target="tpu_custom_call" | custom-call | bytes 12582912 | tf_op jit(solution)/shard_map/pallas_call | solution.py:69
  193.1 6.5 %collective-permute-done = bf16[384,512]{1,0:T(8,128)(2,1)S(1)} collective-permute-done((bf16[384,512]{1,0:T(8,128)(2,1)S(1)}, bf16[384,512]{1,0:T(8,128)(2,1)S(1)}, u32[]{:S(2)}, u32[]{:S(2)}) %collective-permute-start) | collective-permute-done | bytes 393248 | tf_op jit(solution)/shard_map/ppermute | solution.py:18
  199.6 4.1 %collective-permute-start.1 = (bf16[2,384,512]{2,1,0:T(8,128)(2,1)S(1)}, bf16[2,384,512]{2,1,0:T(8,128)(2,1)S(1)}, u32[]{:S(2)}, u32[]{:S(2)}) collective-permute-start(bf16[2,384,512]{2,1,0:T(8,128)(2,1)S(1)} %pad_maximum_fusion.1), channel_id=1, source_target_pairs={{0,16},{4,68},{8,24},{12,76},{16,0},{20,84},{24,8},{28,92},{32,48}... | collective-permute-start | bytes 2359304 | tf_op jit(solution)/shard_map/ppermute | solution.py:29
  205.8 8.0 %collective-permute-done.1.refs_1_ = bf16[2,384,512]{2,1,0:T(8,128)(2,1)S(1)} collective-permute-done((bf16[2,384,512]{2,1,0:T(8,128)(2,1)S(1)}, bf16[2,384,512]{2,1,0:T(8,128)(2,1)S(1)}, u32[]{:S(2)}, u32[]{:S(2)}) %collective-permute-start.1) | collective-permute-done | bytes 786464 | tf_op jit(solution)/shard_map/ppermute | solution.py:29
  213.9 9.3 %collective-permute-done.2.refs_2_ = bf16[2,384,512]{2,1,0:T(8,128)(2,1)S(1)} collective-permute-done((bf16[2,384,512]{2,1,0:T(8,128)(2,1)S(1)}, bf16[2,384,512]{2,1,0:T(8,128)(2,1)S(1)}, u32[]{:S(2)}, u32[]{:S(2)}) %collective-permute-start.2) | collective-permute-done | bytes 786464 | tf_op jit(solution)/shard_map/ppermute | solution.py:29
  224.5 3.2 collective-permute-start.4
  229.8 5.9 %shard_map.29 = (f32[384,384]{1,0:T(8,128)S(1)}, f32[384,384]{1,0:T(8,128)S(1)}) custom-call(s32[16]{0:T(128)S(1)} %stack.188.ids_ref, bf16[1,384,512]{2,1,0:T(8,128)(2,1)S(1)} %bitcast.61, bf16[2,384,512]{2,1,0:T(8,128)(2,1)S(1)} %collective-permute-done.1.refs_1_, bf16[2,384,512]{2,1,0:T(8,128)(2,1)S(1)} %collective-permute-done.2.refs_2_, ...), custom_call_target="tpu_custom_call" | custom-call | flops 2113929216 | bytes 8257536 | tf_op jit(solution)/shard_map/pallas_call | solution.py:69
  235.8 6.9 %collective-permute-done.4.refs_0_ = bf16[3,384,512]{2,1,0:T(8,128)(2,1)} collective-permute-done((bf16[3,384,512]{2,1,0:T(8,128)(2,1)}, bf16[3,384,512]{2,1,0:T(8,128)(2,1)}, u32[]{:S(2)}, u32[]{:S(2)}) %collective-permute-start.4) | collective-permute-done | bytes 1179680 | tf_op jit(solution)/shard_map/ppermute | solution.py:29
  242.6 12.9 %collective-permute-done.5.refs_1_ = bf16[3,384,512]{2,1,0:T(8,128)(2,1)} collective-permute-done((bf16[3,384,512]{2,1,0:T(8,128)(2,1)}, bf16[3,384,512]{2,1,0:T(8,128)(2,1)}, u32[]{:S(2)}, u32[]{:S(2)}) %collective-permute-start.5) | collective-permute-done | bytes 1179680 | tf_op jit(solution)/shard_map/ppermute | solution.py:29
  255.6 7.1 %shard_map.30 = (f32[384,384]{1,0:T(8,128)S(1)}, f32[384,384]{1,0:T(8,128)S(1)}) custom-call(s32[16]{0:T(128)S(1)} %stack.188.ids_ref, bf16[3,384,512]{2,1,0:T(8,128)(2,1)} %collective-permute-done.4.refs_0_, bf16[3,384,512]{2,1,0:T(8,128)(2,1)} %collective-permute-done.5.refs_1_, bf16[3,384,512]{2,1,0:T(8,128)(2,1)} %collective-permute-done.6.refs_2_, ...), custom_call_target="tpu_custom_call" | custom-call | flops 2717908992 | bytes 10616832 | tf_op jit(solution)/shard_map/pallas_call | solution.py:69
  262.9 7.1 %multiply_reduce_fusion = f32[384]{0:T(512)S(1)} fusion(bf16[384,16384]{1,0:T(8,128)(2,1)} %data_ref.3), kind=kLoop, calls=%fused_computation | loop fusion | flops 18873984 | bytes 12584448 | tf_op jit(solution)/shard_map/reduce_sum | solution.py:299
  270.7 14.1 %all_to_all.29 = f32[32,2,384]{2,1,0:T(2,128)S(1)} all-to-all(f32[32,2,384]{2,1,0:T(2,128)S(1)} %broadcast_in_dim.11), channel_id=1, replica_groups=mesh['dp'=32,'noise'=4] {'dp'}, dimensions={0} | all-to-all | bytes 196608 | tf_op jit(solution)/shard_map/all_to_all | solution.py:53
  285.3 1.6 collective-permute-start.9
  286.9 2.7 collective-permute-start.10
  289.6 1.4 collective-permute-start.11
  293.7 10.9 %all_to_all.30 = f32[32,1,384]{2,1,0:T(1,128)S(1)} all-to-all(f32[32,1,384]{2,1,0:T(1,128)S(1)} %broadcast_in_dim.12), channel_id=1, replica_groups=mesh['dp'=32,'noise'=4] {'dp'}, dimensions={0} | all-to-all | bytes 98304 | tf_op jit(solution)/shard_map/all_to_all | solution.py:53
  305.4 3.8 collective-permute-start.13
  310.8 2.0 collective-permute-done.14
  313.3 10.8 %all_to_all.31 = f32[32,1,384]{2,1,0:T(1,128)S(1)} all-to-all(f32[32,1,384]{2,1,0:T(1,128)S(1)} %broadcast_in_dim.13), channel_id=1, replica_groups=mesh['dp'=32,'noise'=4] {'dp'}, dimensions={0} | all-to-all | bytes 98304 | tf_op jit(solution)/shard_map/all_to_all | solution.py:53
  324.6 2.7 collective-permute-start.16
  331.6 1.6 collective-permute-done.18.w_oth_ref
  333.2 7.9 %shard_map.32 = (bf16[3,384,512]{2,1,0:T(8,128)(2,1)}, bf16[3,384,512]{2,1,0:T(8,128)(2,1)}, bf16[3,384,512]{2,1,0:T(8,128)(2,1)}) custom-call(s32[16]{0:T(128)S(1)} %stack.188.ids_ref, bf16[384,384]{1,0:T(8,128)(2,1)S(1)} %get-tuple-element.50.w_own_ref, bf16[384,384]{1,0:T(8,128)(2,1)S(1)} %collective-permute-done.18.w_oth_ref, ...), custom_call_target="tpu_custom_call" | custom-call | flops 2717908992 | bytes 10616832 | tf_op jit(solution)/shard_map/pallas_call | solution.py:69
  343.2 2.5 collective-permute-start.21
  345.7 7.2 %shard_map.31 = (bf16[1,384,512]{2,1,0:T(8,128)(2,1)S(1)}, bf16[2,384,512]{2,1,0:T(8,128)(2,1)S(1)}, bf16[2,384,512]{2,1,0:T(8,128)(2,1)S(1)}, bf16[2,384,512]{2,1,0:T(8,128)(2,1)S(1)}) custom-call(s32[16]{0:T(128)S(1)} %stack.188.ids_ref, bf16[384,384]{1,0:T(8,128)(2,1)S(1)} %get-tuple-element.50.w_own_ref, ...), custom_call_target="tpu_custom_call" | custom-call | flops 2113929216 | bytes 8257536 | tf_op jit(solution)/shard_map/pallas_call | solution.py:69
  353.5 4.5 %all-to-all-start.3 = ((f32[32,1,384]{2,1,0:T(1,128)}), f32[32,1,384]{2,1,0:T(1,128)}, u32[]{:S(2)}, u32[]{:S(2)}) async-start(f32[32,1,384]{2,1,0:T(1,128)} %broadcast_in_dim.14), calls=%async_computation.3 | async-start | bytes 98304 | tf_op jit(solution)/shard_map/all_to_all | solution.py:53
  358.9 14.0 %all-to-all-done.3 = f32[32,1,384]{2,1,0:T(1,128)} async-done(((f32[32,1,384]{2,1,0:T(1,128)}), f32[32,1,384]{2,1,0:T(1,128)}, u32[]{:S(2)}, u32[]{:S(2)}) %all-to-all-start.3) | async-done | bytes 49184 | tf_op jit(solution)/shard_map/all_to_all | solution.py:53
  373.8 2.6 add_convert_fusion.2
  376.5 2.4 collective-permute-start.22
  379.7 2.7 collective-permute-start.24
  382.5 7.7 %collective-permute-done.22 = bf16[2,384,512]{2,1,0:T(8,128)(2,1)S(1)} collective-permute-done((bf16[2,384,512]{2,1,0:T(8,128)(2,1)S(1)}, bf16[2,384,512]{2,1,0:T(8,128)(2,1)S(1)}, u32[]{:S(2)}, u32[]{:S(2)}) %collective-permute-start.22) | collective-permute-done | bytes 786464 | tf_op jit(solution)/shard_map/ppermute | solution.py:29
  390.2 8.3 %collective-permute-done.23 = bf16[2,384,512]{2,1,0:T(8,128)(2,1)S(1)} collective-permute-done((bf16[2,384,512]{2,1,0:T(8,128)(2,1)S(1)}, bf16[2,384,512]{2,1,0:T(8,128)(2,1)S(1)}, u32[]{:S(2)}, u32[]{:S(2)}) %collective-permute-start.23) | collective-permute-done | bytes 786464 | tf_op jit(solution)/shard_map/ppermute | solution.py:29
  398.8 2.3 collective-permute-done.25
  (110 shorter events, 24.4 us)
Async XLA Ops:
  0.1 192.5 %copy-start = (bf16[384,512]{1,0:T(8,128)(2,1)S(1)}, bf16[384,512]{1,0:T(8,128)(2,1)}, u32[]{:S(2)}) copy-start(bf16[384,512]{1,0:T(8,128)(2,1)} %param.2) | copy-start | bytes 1179652
  192.5 37.3 %collective-permute-start.7 = (bf16[384,8192]{1,0:T(8,128)(2,1)}, bf16[384,8192]{1,0:T(8,128)(2,1)}, u32[]{:S(2)}, u32[]{:S(2)}) collective-permute-start(bf16[384,8192]{1,0:T(8,128)(2,1)} %shard_map.28), channel_id=1, source_target_pairs={{0,4},{4,0},{8,12},{12,8},{16,20},{20,16},{24,28},{28,24},{32,36},... | collective-permute-start | bytes 18874376 | tf_op jit(solution)/shard_map/ppermute | solution.py:18
  192.6 7.0 %collective-permute-start = (bf16[384,512]{1,0:T(8,128)(2,1)S(1)}, bf16[384,512]{1,0:T(8,128)(2,1)S(1)}, u32[]{:S(2)}, u32[]{:S(2)}) collective-permute-start(bf16[384,512]{1,0:T(8,128)(2,1)S(1)} %copy-done), channel_id=1, source_target_pairs={{0,4},{4,0},{8,12},{12,8},{16,20},{20,16},{24,28},{28,24},{32,36},... | collective-permute-start | bytes 1179656 | tf_op jit(solution)/shard_map/ppermute | solution.py:18
  199.6 14.2 %collective-permute-start.1 = (bf16[2,384,512]{2,1,0:T(8,128)(2,1)S(1)}, bf16[2,384,512]{2,1,0:T(8,128)(2,1)S(1)}, u32[]{:S(2)}, u32[]{:S(2)}) collective-permute-start(bf16[2,384,512]{2,1,0:T(8,128)(2,1)S(1)} %pad_maximum_fusion.1), channel_id=1, source_target_pairs={{0,16},{4,68},{8,24},{12,76},{16,0},{20,84},{24,8},{28,92},{32,48}... | collective-permute-start | bytes 2359304 | tf_op jit(solution)/shard_map/ppermute | solution.py:29
  203.8 19.5 %collective-permute-start.2 = (bf16[2,384,512]{2,1,0:T(8,128)(2,1)S(1)}, bf16[2,384,512]{2,1,0:T(8,128)(2,1)S(1)}, u32[]{:S(2)}, u32[]{:S(2)}) collective-permute-start(bf16[2,384,512]{2,1,0:T(8,128)(2,1)S(1)} %pad_maximum_fusion.1), channel_id=1, source_target_pairs={{0,24},{4,100},{8,0},{12,108},{16,8},{20,116},{24,16},{28,124},{32... | collective-permute-start | bytes 2359304 | tf_op jit(solution)/shard_map/ppermute | solution.py:29
  204.5 18.8 %collective-permute-start.3 = (bf16[2,384,512]{2,1,0:T(8,128)(2,1)S(1)}, bf16[2,384,512]{2,1,0:T(8,128)(2,1)S(1)}, u32[]{:S(2)}, u32[]{:S(2)}) collective-permute-start(bf16[2,384,512]{2,1,0:T(8,128)(2,1)S(1)} %pad_maximum_fusion.1), channel_id=1, source_target_pairs={{0,8},{4,36},{8,16},{12,44},{16,24},{20,52},{24,0},{28,60},{32,40}... | collective-permute-start | bytes 2359304 | tf_op jit(solution)/shard_map/ppermute | solution.py:29
  224.5 18.1 %collective-permute-start.4 = (bf16[3,384,512]{2,1,0:T(8,128)(2,1)}, bf16[3,384,512]{2,1,0:T(8,128)(2,1)}, u32[]{:S(2)}, u32[]{:S(2)}) collective-permute-start(bf16[3,384,512]{2,1,0:T(8,128)(2,1)} %pad_maximum_fusion), channel_id=1, source_target_pairs={{0,64},{4,20},{8,72},{12,28},{16,80},{20,4},{24,88},{28,12},{32,96... | collective-permute-start | bytes 3538952 | tf_op jit(solution)/shard_map/ppermute | solution.py:29
  227.7 27.9 %collective-permute-start.5 = (bf16[3,384,512]{2,1,0:T(8,128)(2,1)}, bf16[3,384,512]{2,1,0:T(8,128)(2,1)}, u32[]{:S(2)}, u32[]{:S(2)}) collective-permute-start(bf16[3,384,512]{2,1,0:T(8,128)(2,1)} %pad_maximum_fusion), channel_id=1, source_target_pairs={{0,96},{4,28},{8,104},{12,4},{16,112},{20,12},{24,120},{28,20},{32... | collective-permute-start | bytes 3538952 | tf_op jit(solution)/shard_map/ppermute | solution.py:29
  228.8 26.8 %collective-permute-start.6 = (bf16[3,384,512]{2,1,0:T(8,128)(2,1)}, bf16[3,384,512]{2,1,0:T(8,128)(2,1)}, u32[]{:S(2)}, u32[]{:S(2)}) collective-permute-start(bf16[3,384,512]{2,1,0:T(8,128)(2,1)} %pad_maximum_fusion), channel_id=1, source_target_pairs={{0,32},{4,12},{8,40},{12,20},{16,48},{20,28},{24,56},{28,4},{32,64... | collective-permute-start | bytes 3538952 | tf_op jit(solution)/shard_map/ppermute | solution.py:29
  262.6 7.6 %collective-permute-start.8 = (f32[384,384]{1,0:T(8,128)S(1)}, f32[384,384]{1,0:T(8,128)S(1)}, u32[]{:S(2)}, u32[]{:S(2)}) collective-permute-start(f32[384,384]{1,0:T(8,128)S(1)} %get-tuple-element.27), channel_id=1, source_target_pairs={{0,4},{4,0},{8,12},{12,8},{16,20},{20,16},{24,28},{28,24},{32,36},... | collective-permute-start | bytes 1769480 | tf_op jit(solution)/shard_map/ppermute | solution.py:18
  285.3 5.7 %collective-permute-start.9 = (f32[384]{0:T(512)S(1)}, f32[384]{0:T(512)S(1)}, u32[]{:S(2)}, u32[]{:S(2)}) collective-permute-start(f32[384]{0:T(512)S(1)} %log_add_fusion.4), channel_id=1, source_target_pairs={{0,1},{1,2},{2,3},{3,0},{4,5},{5,6},{6,7},{7,4},{8,9},{9,10},{10,1... | collective-permute-start | bytes 4616 | tf_op jit(solution)/shard_map/ppermute | solution.py:63
  286.9 5.1 %collective-permute-start.10 = (f32[384]{0:T(512)S(1)}, f32[384]{0:T(512)S(1)}, u32[]{:S(2)}, u32[]{:S(2)}) collective-permute-start(f32[384]{0:T(512)S(1)} %log_add_fusion.4), channel_id=1, source_target_pairs={{0,2},{1,3},{2,0},{3,1},{4,6},{5,7},{6,4},{7,5},{8,10},{9,11},{10,... | collective-permute-start | bytes 4616 | tf_op jit(solution)/shard_map/ppermute | solution.py:63
  289.6 3.6 collective-permute-start.11
  305.0 4.9 %collective-permute-start.12 = (f32[384]{0:T(512)S(1)}, f32[384]{0:T(512)S(1)}, u32[]{:S(2)}, u32[]{:S(2)}) collective-permute-start(f32[384]{0:T(512)S(1)} %log_add_fusion.2), channel_id=1, source_target_pairs={{0,1},{1,2},{2,3},{3,0},{4,5},{5,6},{6,7},{7,4},{8,9},{9,10},{10,1... | collective-permute-start | bytes 4616 | tf_op jit(solution)/shard_map/ppermute | solution.py:63
  305.4 5.4 %collective-permute-start.13 = (f32[384]{0:T(512)S(1)}, f32[384]{0:T(512)S(1)}, u32[]{:S(2)}, u32[]{:S(2)}) collective-permute-start(f32[384]{0:T(512)S(1)} %log_add_fusion.2), channel_id=1, source_target_pairs={{0,2},{1,3},{2,0},{3,1},{4,6},{5,7},{6,4},{7,5},{8,10},{9,11},{10,... | collective-permute-start | bytes 4616 | tf_op jit(solution)/shard_map/ppermute | solution.py:63
  309.2 3.6 collective-permute-start.14
  324.6 4.9 %collective-permute-start.15 = (f32[384]{0:T(512)S(1)}, f32[384]{0:T(512)S(1)}, u32[]{:S(2)}, u32[]{:S(2)}) collective-permute-start(f32[384]{0:T(512)S(1)} %log_add_fusion), channel_id=1, source_target_pairs={{0,1},{1,2},{2,3},{3,0},{4,5},{5,6},{6,7},{7,4},{8,9},{9,10},{10,1... | collective-permute-start | bytes 4616 | tf_op jit(solution)/shard_map/ppermute | solution.py:63
  324.6 5.2 %collective-permute-start.16 = (f32[384]{0:T(512)S(1)}, f32[384]{0:T(512)S(1)}, u32[]{:S(2)}, u32[]{:S(2)}) collective-permute-start(f32[384]{0:T(512)S(1)} %log_add_fusion), channel_id=1, source_target_pairs={{0,2},{1,3},{2,0},{3,1},{4,6},{5,7},{6,4},{7,5},{8,10},{9,11},{10,... | collective-permute-start | bytes 4616 | tf_op jit(solution)/shard_map/ppermute | solution.py:63
  327.4 3.6 collective-permute-start.17
  331.3 1.9 collective-permute-start.18
  341.1 32.7 %collective-permute-start.19 = (bf16[3,384,512]{2,1,0:T(8,128)(2,1)}, bf16[3,384,512]{2,1,0:T(8,128)(2,1)}, u32[]{:S(2)}, u32[]{:S(2)}) collective-permute-start(bf16[3,384,512]{2,1,0:T(8,128)(2,1)} %get-tuple-element.34), channel_id=1, source_target_pairs={{0,64},{4,20},{8,72},{12,28},{16,80},{20,4},{24,88},{28,12},{32,96... | collective-permute-start | bytes 3538952 | tf_op jit(solution)/shard_map/ppermute | solution.py:29
  342.4 31.4 %collective-permute-start.20 = (bf16[3,384,512]{2,1,0:T(8,128)(2,1)}, bf16[3,384,512]{2,1,0:T(8,128)(2,1)}, u32[]{:S(2)}, u32[]{:S(2)}) collective-permute-start(bf16[3,384,512]{2,1,0:T(8,128)(2,1)} %get-tuple-element.35), channel_id=1, source_target_pairs={{0,32},{4,12},{8,40},{12,20},{16,48},{20,28},{24,56},{28,4},{32,64... | collective-permute-start | bytes 3538952 | tf_op jit(solution)/shard_map/ppermute | solution.py:29
  343.2 30.7 %collective-permute-start.21 = (bf16[3,384,512]{2,1,0:T(8,128)(2,1)}, bf16[3,384,512]{2,1,0:T(8,128)(2,1)}, u32[]{:S(2)}, u32[]{:S(2)}) collective-permute-start(bf16[3,384,512]{2,1,0:T(8,128)(2,1)} %get-tuple-element.36), channel_id=1, source_target_pairs={{0,96},{4,28},{8,104},{12,4},{16,112},{20,12},{24,120},{28,20},{32... | collective-permute-start | bytes 3538952 | tf_op jit(solution)/shard_map/ppermute | solution.py:29
  353.5 19.4 %all-to-all-start.3 = ((f32[32,1,384]{2,1,0:T(1,128)}), f32[32,1,384]{2,1,0:T(1,128)}, u32[]{:S(2)}, u32[]{:S(2)}) async-start(f32[32,1,384]{2,1,0:T(1,128)} %broadcast_in_dim.14), calls=%async_computation.3 | async-start | bytes 98304 | tf_op jit(solution)/shard_map/all_to_all | solution.py:53
  373.8 2.7 copy-start.1
  376.5 13.7 %collective-permute-start.22 = (bf16[2,384,512]{2,1,0:T(8,128)(2,1)S(1)}, bf16[2,384,512]{2,1,0:T(8,128)(2,1)S(1)}, u32[]{:S(2)}, u32[]{:S(2)}) collective-permute-start(bf16[2,384,512]{2,1,0:T(8,128)(2,1)S(1)} %pad_maximum_fusion.2), channel_id=1, source_target_pairs={{0,16},{4,68},{8,24},{12,76},{16,0},{20,84},{24,8},{28,92},{32,48}... | collective-permute-start | bytes 2359304 | tf_op jit(solution)/shard_map/ppermute | solution.py:29
  379.0 19.5 %collective-permute-start.23 = (bf16[2,384,512]{2,1,0:T(8,128)(2,1)S(1)}, bf16[2,384,512]{2,1,0:T(8,128)(2,1)S(1)}, u32[]{:S(2)}, u32[]{:S(2)}) collective-permute-start(bf16[2,384,512]{2,1,0:T(8,128)(2,1)S(1)} %pad_maximum_fusion.3), channel_id=1, source_target_pairs={{0,8},{4,36},{8,16},{12,44},{16,24},{20,52},{24,0},{28,60},{32,40}... | collective-permute-start | bytes 2359304 | tf_op jit(solution)/shard_map/ppermute | solution.py:29
  379.7 18.8 %collective-permute-start.24 = (bf16[2,384,512]{2,1,0:T(8,128)(2,1)S(1)}, bf16[2,384,512]{2,1,0:T(8,128)(2,1)S(1)}, u32[]{:S(2)}, u32[]{:S(2)}) collective-permute-start(bf16[2,384,512]{2,1,0:T(8,128)(2,1)S(1)} %pad_maximum_fusion.4), channel_id=1, source_target_pairs={{0,24},{4,100},{8,0},{12,108},{16,8},{20,116},{24,16},{28,124},{32... | collective-permute-start | bytes 2359304 | tf_op jit(solution)/shard_map/ppermute | solution.py:29
  398.7 2.4 collective-permute-start.25

commit v4 on v3

v4 whole, which is shorter than its diff:
```python
import jax
import jax.numpy as jnp
from jax import lax
from jax.experimental import pallas as pl
from jax.experimental.pallas import tpu as pltpu
from jax.sharding import PartitionSpec as P

ITERS = 3
EPS = 0.004
SIDE = 4
OFFS = (2, 1, 3)
BLOCKS = SIDE * SIDE
VMEM = 48 * 1024 * 1024

SPOTS = [(k, m) for k in (0, 1, 3, 2) for m in OFFS + (0,)]


def swap(values):
    n = lax.axis_size("dp")
    return lax.ppermute(values, "dp", [(i, i ^ 1) for i in range(n)])


def hop(values, k, first):
    pairs = []
    for y in range(SIDE):
        for z in range(SIDE):
            for c in range(2):
                along_z = (c == 0) == first
                to_y, to_z = (y, (z + k) % SIDE) if along_z else ((y + k) % SIDE, z)
                pairs.append(((y * SIDE + z) * 2 + c, (to_y * SIDE + to_z) * 2 + c))
    return lax.ppermute(values, "dp", pairs)


def block_ids(y, z, core):
    ids = []
    for k, m in SPOTS:
        dy = jnp.where(core == 0, k, m)
        dz = jnp.where(core == 0, m, k)
        ids.append((((y + dy) % SIDE) * SIDE + (z + dz) % SIDE) * 2 + core)
    return jnp.stack(ids).astype(jnp.int32)


def lse(values, axis):
    peak = jnp.max(values, axis=axis, keepdims=True)
    total = jnp.sum(jnp.exp(values - peak), axis=axis)
    return jnp.squeeze(peak, axis) + jnp.log(total)


def to_all_dp(values):
    n = lax.axis_size("dp")
    return lax.all_to_all(
        jnp.broadcast_to(values[None], (n,) + values.shape), "dp", 0, 0
    )


def to_all_noise(values):
    n = lax.axis_size("noise")
    parts = [values]
    for k in range(1, n):
        parts.append(
            lax.ppermute(values, "noise", [(i, (i + k) % n) for i in range(n)])
        )
    return jnp.stack(parts)


def call(kernel, ids, ins, out_shape, scratch, flops, moved):
    return pl.pallas_call(
        kernel,
        in_specs=[pl.BlockSpec(memory_space=pltpu.SMEM)]
        + [pl.BlockSpec(memory_space=pl.ANY)] * len(ins),
        out_specs=[pl.BlockSpec(memory_space=pl.ANY)] * len(out_shape),
        out_shape=out_shape,
        scratch_shapes=scratch,
        compiler_params=pltpu.CompilerParams(vmem_limit_bytes=VMEM),
        cost_estimate=pl.CostEstimate(
            flops=flops, bytes_accessed=moved, transcendentals=0
        ),
    )(ids, *ins)


def columns(ref, place, block):
    return ref.at[:, pl.ds(pl.multiple_of(place * block, block), block)]


def part_dots(ids, start, groups, data, data_other, before):
    sizes = [g[0].shape[0] for g in groups]
    n = sum(sizes)
    rows = sum(p.shape[1] for p in groups[0])
    block = groups[0][0].shape[2]
    inner = data.shape[0]
    spots = [(a, i) for a, size in enumerate(sizes) for i in range(size)]
    parts = [p for g in groups for p in g]
    per = len(groups[0])
    height = rows // per
    n_in = len(parts) + 2 + (0 if before is None else 2)

    def kernel(ids_ref, *refs):
        ins, outs = refs[:n_in], refs[n_in : n_in + 2]
        pieces, held, acc, sems, acc_sems = refs[n_in + 2 :]
        data_ref, data_other_ref = ins[len(parts) : len(parts) + 2]
        halves = [acc.at[:, pl.ds(b * inner, inner)] for b in range(2)]
        first = []
        if before is not None:
            for b in range(2):
                source = ins[len(parts) + 2 + b]
                first.append(
                    pltpu.make_async_copy(source, halves[b], acc_sems.at[b])
                )
                first[-1].start()
        steps = []
        for t, (a, i) in enumerate(spots):
            places = [
                (ins[a * per + p].at[i], pieces.at[t, pl.ds(p * height, height)])
                for p in range(per)
            ] + [
                (
                    columns(data_ref, ids_ref[t + start], block),
                    held.at[t, pl.ds(0, inner)],
                ),
                (
                    columns(data_other_ref, ids_ref[t + start], block),
                    held.at[t, pl.ds(inner, inner)],
                ),
            ]
            steps.append(
                [
                    pltpu.make_async_copy(source, to, sems.at[b, t])
                    for b, (source, to) in enumerate(places)
                ]
            )
            for copy in steps[-1]:
                copy.start()
        for copy in first:
            copy.wait()
        for t, step in enumerate(steps):
            for copy in step:
                copy.wait()
            part = lax.dot_general(
                pieces[t],
                held[t],
                (((1,), (1,)), ((), ())),
                preferred_element_type=jnp.float32,
            )
            if t == 0 and before is None:
                acc[...] = part
            else:
                acc[...] += part
        last = []
        for b in range(2):
            last.append(pltpu.make_async_copy(halves[b], outs[b], acc_sems.at[b]))
            last[-1].start()
        for copy in last:
            copy.wait()

    shape = jax.ShapeDtypeStruct((rows, inner), jnp.float32)
    return call(
        kernel,
        ids,
        parts + [data, data_other] + ([] if before is None else list(before)),
        [shape, shape],
        [
            pltpu.VMEM((n, rows, block), data.dtype),
            pltpu.VMEM((n, 2 * inner, block), data.dtype),
            pltpu.VMEM((rows, 2 * inner), jnp.float32),
            pltpu.SemaphoreType.DMA((per + 2, n)),
            pltpu.SemaphoreType.DMA((2,)),
        ],
        n * 4 * rows * inner * block,
        n * block * (4 * inner + 2 * rows),
    )


def gathered_dots(noise, data, data_other, ids, sq_data):
    half = noise.shape[0] // 2
    along = [hop(noise, -k, True) for k in OFFS] + [noise]
    top = jnp.stack([block[:half] for block in along])
    bottom = jnp.stack([block[half:] for block in along])
    top, bottom, sq_data = lax.optimization_barrier((top, bottom, sq_data))
    up_top, down_bottom = hop(top, -1, False), hop(bottom, 1, False)
    up_bottom, down_top = hop(bottom, -1, False), hop(top, 1, False)
    groups = [[block[None]] for block in along]
    dots = part_dots(ids, 0, groups, data, data_other, None)
    up_top, down_bottom, *dots = lax.optimization_barrier((up_top, down_bottom, *dots))
    far = [hop(up_top, -1, False), hop(down_bottom, 1, False)]
    groups = [[up_top, up_bottom], [down_top, down_bottom]]
    dots = part_dots(ids, 4, groups, data, data_other, dots)
    own, other = part_dots(ids, 12, [far], data, data_other, dots)
    return own + swap(other), sq_data


def part_sums(ids, start, sizes, ins, per=1):
    rows, inner = ins[0].shape
    dtype = ins[2].dtype
    block = ins[2].shape[1] // (2 * BLOCKS)
    spots = [(a, i) for a, size in enumerate(sizes) for i in range(size)]
    n = len(spots)
    height = rows // per

    def kernel(ids_ref, w_own_ref, w_oth_ref, data_ref, data_other_ref, *refs):
        outs = refs[: per * len(sizes)]
        weights, held, totals, w_sems, sems = refs[per * len(sizes) :]
        first = []
        for b, w in enumerate((w_own_ref, w_oth_ref)):
            to = weights.at[:, pl.ds(b * inner, inner)]
            first.append(pltpu.make_async_copy(w, to, w_sems.at[b]))
            first[-1].start()
        steps = []
        for t in range(n):
            sources = [
                columns(ref, ids_ref[t + start], block)
                for ref in (data_ref, data_other_ref)
            ]
            steps.append(
                [
                    pltpu.make_async_copy(
                        source, held.at[t, pl.ds(b * inner, inner)], sems.at[b, t]
                    )
                    for b, source in enumerate(sources)
                ]
            )
            for copy in steps[-1]:
                copy.start()
        for copy in first:
            copy.wait()
        last = []
        for t, (a, i) in enumerate(spots):
            for copy in steps[t]:
                copy.wait()
            total = jnp.dot(weights[...], held[t], preferred_element_type=jnp.float32)
            totals[t] = total.astype(dtype)
            for p in range(per):
                source = totals.at[t, pl.ds(p * height, height)]
                to = outs[a * per + p].at[i]
                last.append(pltpu.make_async_copy(source, to, sems.at[2 + p, t]))
                last[-1].start()
        for copy in last:
            copy.wait()

    return call(
        kernel,
        ids,
        ins,
        [
            jax.ShapeDtypeStruct((size, height, block), dtype)
            for size in sizes
            for p in range(per)
        ],
        [
            pltpu.VMEM((rows, 2 * inner), dtype),
            pltpu.VMEM((n, 2 * inner, block), dtype),
            pltpu.VMEM((n, rows, block), dtype),
            pltpu.SemaphoreType.DMA((2,)),
            pltpu.SemaphoreType.DMA((2 + per, n)),
        ],
        n * 4 * rows * inner * block,
        n * (4 * inner * block + 2 * rows * block),
    )


def added(first, others):
    total = first.astype(jnp.float32)
    for other in others:
        total += other.astype(jnp.float32)
    return total


def scattered_sums(ids, ins, row_part):
    top, bottom = part_sums(ids, 12, [4], ins, 2)
    ids, top, bottom = lax.optimization_barrier((ids, top, bottom))
    top, bottom = hop(top, 1, False), hop(bottom, -1, False)
    up_top, up_bottom, down_top, down_bottom = part_sums(ids, 4, [4, 4], ins, 2)
    ids, up_bottom, down_top = lax.optimization_barrier((ids, up_bottom, down_top))
    tops, bottoms = [hop(down_top, -1, False)], [hop(up_bottom, 1, False)]
    near_top, near_bottom = part_sums(ids, 0, [4], ins, 2)
    tops.append(hop(added(up_top, [top]).astype(top.dtype), 1, False))
    bottoms.append(hop(added(down_bottom, [bottom]).astype(top.dtype), -1, False))
    totals = []
    for a in range(3):
        total = [
            added(near_top[a], [got[a] for got in tops]),
            added(near_bottom[a], [got[a] for got in bottoms]),
        ]
        totals.append(jnp.concatenate(total).astype(top.dtype))
    row_part, *totals = lax.optimization_barrier((row_part, *totals))
    sums = [hop(total, k, True) for total, k in zip(totals, OFFS)]
    row_sum = jnp.sum(to_all_dp(row_part), axis=0)
    row_sum, near_top = lax.optimization_barrier((row_sum, near_top))
    total = [
        added(near_top[3], [got[3] for got in tops]),
        added(near_bottom[3], [got[3] for got in bottoms]),
    ]
    return added(jnp.concatenate(total), sums), row_sum


def body(noise_latents, data_latents):
    width = data_latents.shape[1]
    place = lax.axis_index("dp")
    core = place % 2
    z = (place // 2) % SIDE
    y = place // (2 * SIDE)
    ids = block_ids(y, z, core)
    data_other = swap(data_latents)
    noise_f = noise_latents.astype(jnp.float32)
    sx_part = jnp.sum(noise_f * noise_f, axis=1)
    data_f = data_latents.astype(jnp.float32)
    sq_data = jnp.sum(data_f * data_f, axis=1)
    dots, sq_data = gathered_dots(
        noise_latents, data_latents, data_other, ids, sq_data
    )
    scale = 1.0 / (width * EPS)
    twice = dots * (2.0 * scale)
    sy = sq_data * scale
    sx = None
    g = jnp.zeros_like(sy)
    for step in range(ITERS):
        local = lse(twice + (g - sy)[None, :], 1)
        if sx is None:
            got = to_all_dp(jnp.stack([local, sx_part]))
            sx = jnp.sum(got[:, 1], axis=0) * scale
            got = got[:, 0]
        else:
            got = to_all_dp(local)
        f = sx - lse(got, 0)
        local = lse(twice + (f - sx)[:, None], 0)
        g = sy - lse(to_all_noise(local), 0)
    coupling = jnp.exp(twice + (f - sx)[:, None] + (g - sy)[None, :])
    weights = coupling.astype(jnp.bfloat16)
    total, row_sum = scattered_sums(
        ids,
        (weights, swap(weights), data_latents, data_other),
        jnp.sum(coupling, axis=1),
    )
    return (total / row_sum[:, None]).astype(jnp.bfloat16)


def solution(mesh):
    return jax.shard_map(
        body,
        mesh=mesh,
        in_specs=(P("noise", "dp"), P("dp", None)),
        out_specs=P("noise", "dp"),
        check_vma=False,
    )
```

time: 404 us -> 179 us (0.44)
  Pallas kernels: 221 us -> 38.6 us
  waiting for transfers between devices: 85.4 us -> 41.1 us
  blocking collectives: 35.7 us -> 43.1 us
    pallas_call x5 -> x6, Pallas kernels: 221 us -> 38.6 us  [call(): pl.pallas_call(kernel, in_specs=[pl.BlockSpec(memory_space=pltpu.SMEM)] +...]
    ppermute x12 -> x18, waiting for transfers between devices: 53.3 us -> 25.5 us  [hop(): return lax.ppermute(values, 'dp', pairs)]
    all_to_all x1 -> x0, waiting for transfers between devices: 14 us -> none  [to_all_dp(): lax.all_to_all(jnp.broadcast_to(values[None], (n,) + values.shape), 'dp',...]
    all_to_all x3 -> x4, blocking collectives: 35.7 us -> 43.1 us  [to_all_dp(): lax.all_to_all(jnp.broadcast_to(values[None], (n,) + values.shape), 'dp',...]
    ppermute x5 -> x3, waiting for transfers between devices: 10.3 us -> 3.39 us  [swap(): return lax.ppermute(values, 'dp', [(i, i ^ 1) for i in range(n)])]
    ppermute x12 -> x18, starting transfers between devices: 21.7 us -> 27.5 us  [hop(): return lax.ppermute(values, 'dp', pairs)]
    all_to_all x1 -> x0, starting transfers between devices: 4.54 us -> none  [to_all_dp(): lax.all_to_all(jnp.broadcast_to(values[None], (n,) + values.shape), 'dp',...]
    ppermute x9, waiting for transfers between devices: 7.82 us -> 12.2 us  [to_all_noise(): lax.ppermute(values, 'noise', [(i, (i + k) % n) for i in range(n)])]
  transfers between devices with their start and end apart: 27 -> 30, of which waited for: 18 -> 18; matrix products, arithmetic and copies ran while one was open for 3% -> 6% of each run, Pallas kernels for 3% -> 15%
where the time goes in v4:
time: 179 us; the launch traced here: 178 us
  blocking collectives  43.1 us (24%)
  waiting for transfers between devices  41.1 us (23%)
  Pallas kernels  38.6 us (22%)
  starting transfers between devices  38.2 us (21%)
  other arithmetic  16 us (9%)
    all_to_all x4, blocking collectives, to_all_dp(): lax.all_to_all(jnp.broadcast_to(values[None], (n,) + values.shape), 'dp',...  43.1 us
    pallas_call x6, Pallas kernels, call(): pl.pallas_call(kernel, in_specs=[pl.BlockSpec(memory_space=pltpu.SMEM)] +...  38.6 us
    ppermute x18, starting transfers between devices, hop(): return lax.ppermute(values, 'dp', pairs)  27.5 us
    ppermute x18, waiting for transfers between devices, hop(): return lax.ppermute(values, 'dp', pairs)  25.5 us
    ppermute x9, waiting for transfers between devices, to_all_noise(): lax.ppermute(values, 'noise', [(i, (i + k) % n) for i in range(n)])  12.2 us
    ppermute x9, starting transfers between devices, to_all_noise(): lax.ppermute(values, 'noise', [(i, (i + k) % n) for i in range(n)])  10.3 us
    reduce_sum x1, other arithmetic, body(): sq_data = jnp.sum(data_f * data_f, axis=1)  7.14 us
  transfers between devices with their start and end apart: 30, of which 18 were waited for; matrix products, arithmetic and copies ran while one was open for 6% of the time, Pallas kernels for 15%

profile of v4, /device:TPU:0, one launch (start us, length us, event | category | flops | bytes accessed | tf_op | source)
XLA Modules:
  0.0 178.1 jit_solution(10436181806660776995)
XLA Ops:
  0.0 2.1 %collective-permute-start.2 = (bf16[384,512]{1,0:T(8,128)(2,1)}, bf16[384,512]{1,0:T(8,128)(2,1)S(1)}, u32[]{:S(2)}, u32[]{:S(2)}) collective-permute-start(bf16[384,512]{1,0:T(8,128)(2,1)} %param.2), channel_id=1, source_target_pairs={{0,8},{4,36},{8,16},{12,44},{16,24},{20,52},{24,0},{28,60},{32,40}... | collective-permute-start | bytes 1179656 | tf_op jit(solution)/shard_map/ppermute | solution.py:31
  2.1 2.2 %collective-permute-start.1 = (bf16[384,512]{1,0:T(8,128)(2,1)}, bf16[384,512]{1,0:T(8,128)(2,1)S(1)}, u32[]{:S(2)}, u32[]{:S(2)}) collective-permute-start(bf16[384,512]{1,0:T(8,128)(2,1)} %param.2), channel_id=1, source_target_pairs={{0,24},{4,100},{8,0},{12,108},{16,8},{20,116},{24,16},{28,124},{32... | collective-permute-start | bytes 1179656 | tf_op jit(solution)/shard_map/ppermute | solution.py:31
  4.3 1.8 %collective-permute-start = (bf16[384,512]{1,0:T(8,128)(2,1)}, bf16[384,512]{1,0:T(8,128)(2,1)S(1)}, u32[]{:S(2)}, u32[]{:S(2)}) collective-permute-start(bf16[384,512]{1,0:T(8,128)(2,1)} %param.2), channel_id=1, source_target_pairs={{0,16},{4,68},{8,24},{12,76},{16,0},{20,84},{24,8},{28,92},{32,48}... | collective-permute-start | bytes 1179656 | tf_op jit(solution)/shard_map/ppermute | solution.py:31
  6.1 7.1 %multiply_reduce_fusion = f32[384]{0:T(512)S(1)} fusion(bf16[384,16384]{1,0:T(8,128)(2,1)} %data_ref.5), kind=kLoop, calls=%fused_computation | loop fusion | flops 18873984 | bytes 12584448 | tf_op jit(solution)/shard_map/reduce_sum | solution.py:306
  17.3 3.0 %collective-permute-start.3 = (bf16[4,192,512]{2,1,0:T(8,128)(2,1)}, bf16[4,192,512]{2,1,0:T(8,128)(2,1)S(1)}, u32[]{:S(2)}, u32[]{:S(2)}) collective-permute-start(bf16[4,192,512]{2,1,0:T(8,128)(2,1)} %get-tuple-element.38), channel_id=1, source_target_pairs={{0,96},{4,28},{8,104},{12,4},{16,112},{20,12},{24,120},{28,20},{32... | collective-permute-start | bytes 2359304 | tf_op jit(solution)/shard_map/ppermute | solution.py:31
  20.9 2.7 %collective-permute-start.8 = (bf16[4,192,512]{2,1,0:T(8,128)(2,1)}, bf16[4,192,512]{2,1,0:T(8,128)(2,1)}, u32[]{:S(2)}, u32[]{:S(2)}) collective-permute-start(bf16[4,192,512]{2,1,0:T(8,128)(2,1)} %get-tuple-element.39), channel_id=1, source_target_pairs={{0,96},{4,28},{8,104},{12,4},{16,112},{20,12},{24,120},{28,20},{32... | collective-permute-start | bytes 2359304 | tf_op jit(solution)/shard_map/ppermute | solution.py:31
  23.6 4.4 %shard_map.28 = (f32[384,384]{1,0:T(8,128)S(1)}, f32[384,384]{1,0:T(8,128)S(1)}) custom-call(s32[16]{0:T(128)S(1)} %stack.143.ids_ref, bf16[1,384,512]{2,1,0:T(8,128)(2,1)S(1)} %bitcast.73, bf16[1,384,512]{2,1,0:T(8,128)(2,1)S(1)} %bitcast.72, bf16[1,384,512]{2,1,0:T(8,128)(2,1)S(1)} %bitcast.71, bf16[1,384,512]{2,1,0:T(8,128)(2,1)S(1)} %bitcast.70, ...), custom_call_target="tpu_custom_call" | custom-call | flops 1207959552 | bytes 4718592 | tf_op jit(solution)/shard_map/pallas_call | solution.py:67
  28.1 2.0 %collective-permute-done.3.refs_0_ = bf16[4,192,512]{2,1,0:T(8,128)(2,1)S(1)} collective-permute-done((bf16[4,192,512]{2,1,0:T(8,128)(2,1)}, bf16[4,192,512]{2,1,0:T(8,128)(2,1)S(1)}, u32[]{:S(2)}, u32[]{:S(2)}) %collective-permute-start.3) | collective-permute-done | bytes 786464 | tf_op jit(solution)/shard_map/ppermute | solution.py:31
  30.1 3.6 %collective-permute-done.4.refs_3_ = bf16[4,192,512]{2,1,0:T(8,128)(2,1)S(1)} collective-permute-done((bf16[4,192,512]{2,1,0:T(8,128)(2,1)}, bf16[4,192,512]{2,1,0:T(8,128)(2,1)S(1)}, u32[]{:S(2)}, u32[]{:S(2)}) %collective-permute-start.4) | collective-permute-done | bytes 786464 | tf_op jit(solution)/shard_map/ppermute | solution.py:31
  33.7 2.0 %collective-permute-start.7 = (bf16[4,192,512]{2,1,0:T(8,128)(2,1)S(1)}, bf16[4,192,512]{2,1,0:T(8,128)(2,1)S(1)}, u32[]{:S(2)}, u32[]{:S(2)}) collective-permute-start(bf16[4,192,512]{2,1,0:T(8,128)(2,1)S(1)} %collective-permute-done.4.refs_3_), channel_id=1, source_target_pairs={{0,32},{4,12},{8,40},{12,20},{16,48},{20,28},{24,56},{28,4},{32,64... | collective-permute-start | bytes 2359304 | tf_op jit(solution)/shard_map/ppermute | solution.py:31
  35.7 6.5 %collective-permute-done.9.refs_2_ = bf16[4,192,512]{2,1,0:T(8,128)(2,1)} collective-permute-done((bf16[4,192,512]{2,1,0:T(8,128)(2,1)}, bf16[4,192,512]{2,1,0:T(8,128)(2,1)}, u32[]{:S(2)}, u32[]{:S(2)}) %collective-permute-start.9) | collective-permute-done | bytes 786464 | tf_op jit(solution)/shard_map/ppermute | solution.py:31
  42.2 7.6 %shard_map.29 = (f32[384,384]{1,0:T(8,128)S(1)}, f32[384,384]{1,0:T(8,128)S(1)}) custom-call(s32[16]{0:T(128)S(1)} %stack.143.ids_ref, bf16[4,192,512]{2,1,0:T(8,128)(2,1)S(1)} %collective-permute-done.3.refs_0_, bf16[4,192,512]{2,1,0:T(8,128)(2,1)} %collective-permute-done.8.refs_1_, bf16[4,192,512]{2,1,0:T(8,128)(2,1)} %collective-permute-done.9.refs_2_, ...), custom_call_target="tpu_custom_call" | custom-call | flops 2415919104 | bytes 9437184 | tf_op jit(solution)/shard_map/pallas_call | solution.py:67
  50.5 5.3 %shard_map.30 = (f32[384,384]{1,0:T(8,128)S(1)}, f32[384,384]{1,0:T(8,128)S(1)}) custom-call(s32[16]{0:T(128)S(1)} %stack.143.ids_ref, bf16[4,192,512]{2,1,0:T(8,128)(2,1)S(1)} %collective-permute-done.6.refs_0_, bf16[4,192,512]{2,1,0:T(8,128)(2,1)S(1)} %collective-permute-done.7.refs_1_, bf16[384,16384]{1,0:T(8,128)(2,1)} %data_ref.5, ...), custom_call_target="tpu_custom_call" | custom-call | flops 1207959552 | bytes 4718592 | tf_op jit(solution)/shard_map/pallas_call | solution.py:67
  56.1 1.8 %collective-permute-done.10 = f32[384,384]{1,0:T(8,128)S(1)} collective-permute-done((f32[384,384]{1,0:T(8,128)S(1)}, f32[384,384]{1,0:T(8,128)S(1)}, u32[]{:S(2)}, u32[]{:S(2)}) %collective-permute-start.10) | collective-permute-done | bytes 589856 | tf_op jit(solution)/shard_map/ppermute | solution.py:20
  58.4 11.0 %all_to_all.29 = f32[32,2,384]{2,1,0:T(2,128)S(1)} all-to-all(f32[32,2,384]{2,1,0:T(2,128)S(1)} %broadcast_in_dim.23), channel_id=1, replica_groups=mesh['dp'=32,'noise'=4] {'dp'}, dimensions={0} | all-to-all | bytes 196608 | tf_op jit(solution)/shard_map/all_to_all | solution.py:51
  69.9 2.8 %collective-permute-start.13 = (f32[384]{0:T(512)S(1)}, f32[384]{0:T(512)S(1)}, u32[]{:S(2)}, u32[]{:S(2)}) collective-permute-start(f32[384]{0:T(512)S(1)} %log_add_fusion.4), channel_id=1, source_target_pairs={{0,3},{1,0},{2,1},{3,2},{4,7},{5,4},{6,5},{7,6},{8,11},{9,8},{10,9... | collective-permute-start | bytes 4616 | tf_op jit(solution)/shard_map/ppermute | solution.py:61
  74.4 3.4 %collective-permute-done.12 = f32[384]{0:T(512)S(1)} collective-permute-done((f32[384]{0:T(512)S(1)}, f32[384]{0:T(512)S(1)}, u32[]{:S(2)}, u32[]{:S(2)}) %collective-permute-start.12) | collective-permute-done | bytes 1568 | tf_op jit(solution)/shard_map/ppermute | solution.py:61
  78.8 10.9 %all_to_all.30 = f32[32,1,384]{2,1,0:T(1,128)S(1)} all-to-all(f32[32,1,384]{2,1,0:T(1,128)S(1)} %broadcast_in_dim.24), channel_id=1, replica_groups=mesh['dp'=32,'noise'=4] {'dp'}, dimensions={0} | all-to-all | bytes 98304 | tf_op jit(solution)/shard_map/all_to_all | solution.py:51
  93.8 1.8 %collective-permute-done.15 = f32[384]{0:T(512)S(1)} collective-permute-done((f32[384]{0:T(512)S(1)}, f32[384]{0:T(512)S(1)}, u32[]{:S(2)}, u32[]{:S(2)}) %collective-permute-start.15) | collective-permute-done | bytes 1568 | tf_op jit(solution)/shard_map/ppermute | solution.py:61
  97.3 10.8 %all_to_all.31 = f32[32,1,384]{2,1,0:T(1,128)S(1)} all-to-all(f32[32,1,384]{2,1,0:T(1,128)S(1)} %broadcast_in_dim.25), channel_id=1, replica_groups=mesh['dp'=32,'noise'=4] {'dp'}, dimensions={0} | all-to-all | bytes 98304 | tf_op jit(solution)/shard_map/all_to_all | solution.py:51
  108.6 1.8 %collective-permute-start.19 = (f32[384]{0:T(512)S(1)}, f32[384]{0:T(512)S(1)}, u32[]{:S(2)}, u32[]{:S(2)}) collective-permute-start(f32[384]{0:T(512)S(1)} %log_add_fusion), channel_id=1, source_target_pairs={{0,3},{1,0},{2,1},{3,2},{4,7},{5,4},{6,5},{7,6},{8,11},{9,8},{10,9... | collective-permute-start | bytes 4616 | tf_op jit(solution)/shard_map/ppermute | solution.py:61
  112.2 3.2 %collective-permute-done.18 = f32[384]{0:T(512)S(1)} collective-permute-done((f32[384]{0:T(512)S(1)}, f32[384]{0:T(512)S(1)}, u32[]{:S(2)}, u32[]{:S(2)}) %collective-permute-start.18) | collective-permute-done | bytes 1568 | tf_op jit(solution)/shard_map/ppermute | solution.py:61
  118.3 5.8 %shard_map.31 = (bf16[4,192,512]{2,1,0:T(8,128)(2,1)S(1)}, bf16[4,192,512]{2,1,0:T(8,128)(2,1)S(1)}) custom-call(s32[16]{0:T(128)S(1)} %stack.143.ids_ref, bf16[384,384]{1,0:T(8,128)(2,1)S(1)} %get-tuple-element.82.w_own_ref, bf16[384,384]{1,0:T(8,128)(2,1)S(1)} %collective-permute-done.20.w_oth_ref, bf16[384,16384]{1,0:T(8,128)(2,1)} %data_ref.5, ...), custom_call_target="tpu_custom_call" | custom-call | flops 1207959552 | bytes 4718592 | tf_op jit(solution)/shard_map/pallas_call | solution.py:67
  124.8 2.6 %collective-permute-start.25 = (bf16[4,192,512]{2,1,0:T(8,128)(2,1)S(1)}, bf16[4,192,512]{2,1,0:T(8,128)(2,1)S(1)}, u32[]{:S(2)}, u32[]{:S(2)}) collective-permute-start(bf16[4,192,512]{2,1,0:T(8,128)(2,1)S(1)} %get-tuple-element.64), channel_id=1, source_target_pairs={{0,96},{4,28},{8,104},{12,4},{16,112},{20,12},{24,120},{28,20},{32... | collective-permute-start | bytes 2359304 | tf_op jit(solution)/shard_map/ppermute | solution.py:31
  127.4 9.8 %shard_map.32 = (bf16[4,192,512]{2,1,0:T(8,128)(2,1)S(1)}, bf16[4,192,512]{2,1,0:T(8,128)(2,1)S(1)}, bf16[4,192,512]{2,1,0:T(8,128)(2,1)S(1)}, bf16[4,192,512]{2,1,0:T(8,128)(2,1)S(1)}) custom-call(s32[16]{0:T(128)S(1)} %stack.143.ids_ref, bf16[384,384]{1,0:T(8,128)(2,1)S(1)} %get-tuple-element.82.w_own_ref, ...), custom_call_target="tpu_custom_call" | custom-call | flops 2415919104 | bytes 9437184 | tf_op jit(solution)/shard_map/pallas_call | solution.py:67
  137.3 2.0 %collective-permute-start.24 = (bf16[4,192,512]{2,1,0:T(8,128)(2,1)S(1)}, bf16[4,192,512]{2,1,0:T(8,128)(2,1)S(1)}, u32[]{:S(2)}, u32[]{:S(2)}) collective-permute-start(bf16[4,192,512]{2,1,0:T(8,128)(2,1)S(1)} %get-tuple-element.62), channel_id=1, source_target_pairs={{0,32},{4,12},{8,40},{12,20},{16,48},{20,28},{24,56},{28,4},{32,64... | collective-permute-start | bytes 2359304 | tf_op jit(solution)/shard_map/ppermute | solution.py:31
  139.9 3.3 %collective-permute-start.26 = (bf16[4,192,512]{2,1,0:T(8,128)(2,1)S(1)}, bf16[4,192,512]{2,1,0:T(8,128)(2,1)S(1)}, u32[]{:S(2)}, u32[]{:S(2)}) collective-permute-start(bf16[4,192,512]{2,1,0:T(8,128)(2,1)S(1)} %add_convert_fusion), channel_id=1, source_target_pairs={{0,96},{4,28},{8,104},{12,4},{16,112},{20,12},{24,120},{28,20},{32... | collective-permute-start | bytes 2359304 | tf_op jit(solution)/shard_map/ppermute | solution.py:31
  143.1 5.8 %shard_map.33 = (bf16[4,192,512]{2,1,0:T(8,128)(2,1)S(1)}, bf16[4,192,512]{2,1,0:T(8,128)(2,1)S(1)}) custom-call(s32[16]{0:T(128)S(1)} %stack.143.ids_ref, bf16[384,384]{1,0:T(8,128)(2,1)S(1)} %get-tuple-element.82.w_own_ref, bf16[384,384]{1,0:T(8,128)(2,1)S(1)} %collective-permute-done.20.w_oth_ref, bf16[384,16384]{1,0:T(8,128)(2,1)} %data_ref.5, ...), custom_call_target="tpu_custom_call" | custom-call | flops 1207959552 | bytes 4718592 | tf_op jit(solution)/shard_map/pallas_call | solution.py:67
  149.3 9.7 %collective-permute-done.23 = bf16[4,192,512]{2,1,0:T(8,128)(2,1)S(1)} collective-permute-done((bf16[4,192,512]{2,1,0:T(8,128)(2,1)S(1)}, bf16[4,192,512]{2,1,0:T(8,128)(2,1)S(1)}, u32[]{:S(2)}, u32[]{:S(2)}) %collective-permute-start.23) | collective-permute-done | bytes 786464 | tf_op jit(solution)/shard_map/ppermute | solution.py:31
  162.2 2.3 %collective-permute-start.29 = (bf16[384,512]{1,0:T(8,128)(2,1)S(1)}, bf16[384,512]{1,0:T(8,128)(2,1)}, u32[]{:S(2)}, u32[]{:S(2)}) collective-permute-start(bf16[384,512]{1,0:T(8,128)(2,1)S(1)} %pad_maximum_fusion.4), channel_id=1, source_target_pairs={{0,24},{4,100},{8,0},{12,108},{16,8},{20,116},{24,16},{28,124},{32... | collective-permute-start | bytes 1179656 | tf_op jit(solution)/shard_map/ppermute | solution.py:31
  164.5 10.4 %all_to_all.32 = f32[32,1,384]{2,1,0:T(1,128)S(1)} all-to-all(f32[32,1,384]{2,1,0:T(1,128)S(1)} %broadcast_in_dim.26), channel_id=1, replica_groups=mesh['dp'=32,'noise'=4] {'dp'}, dimensions={0} | all-to-all | bytes 98304 | tf_op jit(solution)/shard_map/all_to_all | solution.py:51
  176.1 1.9 %fusion.3 = bf16[384,512]{1,0:T(8,128)(2,1)} fusion(bf16[384,512]{1,0:T(8,128)(2,1)} %collective-permute-done.29, bf16[384,512]{1,0:T(8,128)(2,1)S(1)} %collective-permute-done.28, bf16[384,512]{1,0:T(8,128)(2,1)S(1)} %collective-permute-done.27, f32[192,512]{1,0:T(8,128)S(1)} %get-tuple-element.75, f32[192,512]{1,0:T(8,128)S(1)} %add_bitcast_fusion.1, ...), kind=kLoop, calls=%fused_computation.10 | loop fusion | flops 1769472 | bytes 2360832 | tf_op jit(solution)/shard_map/convert_element_type | solution.py:333
  (119 shorter events, 26.1 us)
Async XLA Ops:
  0.0 13.2 %copy-start = (bf16[384,512]{1,0:T(8,128)(2,1)S(1)}, bf16[384,512]{1,0:T(8,128)(2,1)}, u32[]{:S(2)}) copy-start(bf16[384,512]{1,0:T(8,128)(2,1)} %param.2) | copy-start | bytes 1179652
  0.0 23.6 %collective-permute-start.5 = (bf16[384,16384]{1,0:T(8,128)(2,1)}, bf16[384,16384]{1,0:T(8,128)(2,1)}, u32[]{:S(2)}, u32[]{:S(2)}) collective-permute-start(bf16[384,16384]{1,0:T(8,128)(2,1)} %data_ref.5), channel_id=1, source_target_pairs={{0,4},{4,0},{8,12},{12,8},{16,20},{20,16},{24,28},{28,24},{32,36},... | collective-permute-start | bytes 37748744 | tf_op jit(solution)/shard_map/ppermute | solution.py:20
  0.0 13.2 %collective-permute-start.2 = (bf16[384,512]{1,0:T(8,128)(2,1)}, bf16[384,512]{1,0:T(8,128)(2,1)S(1)}, u32[]{:S(2)}, u32[]{:S(2)}) collective-permute-start(bf16[384,512]{1,0:T(8,128)(2,1)} %param.2), channel_id=1, source_target_pairs={{0,8},{4,36},{8,16},{12,44},{16,24},{20,52},{24,0},{28,60},{32,40}... | collective-permute-start | bytes 1179656 | tf_op jit(solution)/shard_map/ppermute | solution.py:31
  2.1 12.1 %collective-permute-start.1 = (bf16[384,512]{1,0:T(8,128)(2,1)}, bf16[384,512]{1,0:T(8,128)(2,1)S(1)}, u32[]{:S(2)}, u32[]{:S(2)}) collective-permute-start(bf16[384,512]{1,0:T(8,128)(2,1)} %param.2), channel_id=1, source_target_pairs={{0,24},{4,100},{8,0},{12,108},{16,8},{20,116},{24,16},{28,124},{32... | collective-permute-start | bytes 1179656 | tf_op jit(solution)/shard_map/ppermute | solution.py:31
  4.3 11.6 %collective-permute-start = (bf16[384,512]{1,0:T(8,128)(2,1)}, bf16[384,512]{1,0:T(8,128)(2,1)S(1)}, u32[]{:S(2)}, u32[]{:S(2)}) collective-permute-start(bf16[384,512]{1,0:T(8,128)(2,1)} %param.2), channel_id=1, source_target_pairs={{0,16},{4,68},{8,24},{12,76},{16,0},{20,84},{24,8},{28,92},{32,48}... | collective-permute-start | bytes 1179656 | tf_op jit(solution)/shard_map/ppermute | solution.py:31
  17.3 12.8 %collective-permute-start.3 = (bf16[4,192,512]{2,1,0:T(8,128)(2,1)}, bf16[4,192,512]{2,1,0:T(8,128)(2,1)S(1)}, u32[]{:S(2)}, u32[]{:S(2)}) collective-permute-start(bf16[4,192,512]{2,1,0:T(8,128)(2,1)} %get-tuple-element.38), channel_id=1, source_target_pairs={{0,96},{4,28},{8,104},{12,4},{16,112},{20,12},{24,120},{28,20},{32... | collective-permute-start | bytes 2359304 | tf_op jit(solution)/shard_map/ppermute | solution.py:31
  20.3 13.4 %collective-permute-start.4 = (bf16[4,192,512]{2,1,0:T(8,128)(2,1)}, bf16[4,192,512]{2,1,0:T(8,128)(2,1)S(1)}, u32[]{:S(2)}, u32[]{:S(2)}) collective-permute-start(bf16[4,192,512]{2,1,0:T(8,128)(2,1)} %get-tuple-element.39), channel_id=1, source_target_pairs={{0,32},{4,12},{8,40},{12,20},{16,48},{20,28},{24,56},{28,4},{32,64... | collective-permute-start | bytes 2359304 | tf_op jit(solution)/shard_map/ppermute | solution.py:31
  20.3 21.9 %collective-permute-start.9 = (bf16[4,192,512]{2,1,0:T(8,128)(2,1)}, bf16[4,192,512]{2,1,0:T(8,128)(2,1)}, u32[]{:S(2)}, u32[]{:S(2)}) collective-permute-start(bf16[4,192,512]{2,1,0:T(8,128)(2,1)} %get-tuple-element.38), channel_id=1, source_target_pairs={{0,32},{4,12},{8,40},{12,20},{16,48},{20,28},{24,56},{28,4},{32,64... | collective-permute-start | bytes 2359304 | tf_op jit(solution)/shard_map/ppermute | solution.py:31
  20.9 21.4 %collective-permute-start.8 = (bf16[4,192,512]{2,1,0:T(8,128)(2,1)}, bf16[4,192,512]{2,1,0:T(8,128)(2,1)}, u32[]{:S(2)}, u32[]{:S(2)}) collective-permute-start(bf16[4,192,512]{2,1,0:T(8,128)(2,1)} %get-tuple-element.39), channel_id=1, source_target_pairs={{0,96},{4,28},{8,104},{12,4},{16,112},{20,12},{24,120},{28,20},{32... | collective-permute-start | bytes 2359304 | tf_op jit(solution)/shard_map/ppermute | solution.py:31
  33.7 16.1 %collective-permute-start.6 = (bf16[4,192,512]{2,1,0:T(8,128)(2,1)S(1)}, bf16[4,192,512]{2,1,0:T(8,128)(2,1)S(1)}, u32[]{:S(2)}, u32[]{:S(2)}) collective-permute-start(bf16[4,192,512]{2,1,0:T(8,128)(2,1)S(1)} %collective-permute-done.3.refs_0_), channel_id=1, source_target_pairs={{0,96},{4,28},{8,104},{12,4},{16,112},{20,12},{24,120},{28,20},{32... | collective-permute-start | bytes 2359304 | tf_op jit(solution)/shard_map/ppermute | solution.py:31
  33.7 16.8 %collective-permute-start.7 = (bf16[4,192,512]{2,1,0:T(8,128)(2,1)S(1)}, bf16[4,192,512]{2,1,0:T(8,128)(2,1)S(1)}, u32[]{:S(2)}, u32[]{:S(2)}) collective-permute-start(bf16[4,192,512]{2,1,0:T(8,128)(2,1)S(1)} %collective-permute-done.4.refs_3_), channel_id=1, source_target_pairs={{0,32},{4,12},{8,40},{12,20},{16,48},{20,28},{24,56},{28,4},{32,64... | collective-permute-start | bytes 2359304 | tf_op jit(solution)/shard_map/ppermute | solution.py:31
  55.8 2.1 %collective-permute-start.10 = (f32[384,384]{1,0:T(8,128)S(1)}, f32[384,384]{1,0:T(8,128)S(1)}, u32[]{:S(2)}, u32[]{:S(2)}) collective-permute-start(f32[384,384]{1,0:T(8,128)S(1)} %get-tuple-element.49), channel_id=1, source_target_pairs={{0,4},{4,0},{8,12},{12,8},{16,20},{20,16},{24,28},{28,24},{32,36},... | collective-permute-start | bytes 1769480 | tf_op jit(solution)/shard_map/ppermute | solution.py:20
  69.9 4.5 %collective-permute-start.13 = (f32[384]{0:T(512)S(1)}, f32[384]{0:T(512)S(1)}, u32[]{:S(2)}, u32[]{:S(2)}) collective-permute-start(f32[384]{0:T(512)S(1)} %log_add_fusion.4), channel_id=1, source_target_pairs={{0,3},{1,0},{2,1},{3,2},{4,7},{5,4},{6,5},{7,6},{8,11},{9,8},{10,9... | collective-permute-start | bytes 4616 | tf_op jit(solution)/shard_map/ppermute | solution.py:61
  72.7 5.1 %collective-permute-start.12 = (f32[384]{0:T(512)S(1)}, f32[384]{0:T(512)S(1)}, u32[]{:S(2)}, u32[]{:S(2)}) collective-permute-start(f32[384]{0:T(512)S(1)} %log_add_fusion.4), channel_id=1, source_target_pairs={{0,2},{1,3},{2,0},{3,1},{4,6},{5,7},{6,4},{7,5},{8,10},{9,11},{10,... | collective-permute-start | bytes 4616 | tf_op jit(solution)/shard_map/ppermute | solution.py:61
  73.5 4.8 %collective-permute-start.11 = (f32[384]{0:T(512)S(1)}, f32[384]{0:T(512)S(1)}, u32[]{:S(2)}, u32[]{:S(2)}) collective-permute-start(f32[384]{0:T(512)S(1)} %log_add_fusion.4), channel_id=1, source_target_pairs={{0,1},{1,2},{2,3},{3,0},{4,5},{5,6},{6,7},{7,4},{8,9},{9,10},{10,1... | collective-permute-start | bytes 4616 | tf_op jit(solution)/shard_map/ppermute | solution.py:61
  90.2 3.7 %collective-permute-start.16 = (f32[384]{0:T(512)S(1)}, f32[384]{0:T(512)S(1)}, u32[]{:S(2)}, u32[]{:S(2)}) collective-permute-start(f32[384]{0:T(512)S(1)} %log_add_fusion.2), channel_id=1, source_target_pairs={{0,3},{1,0},{2,1},{3,2},{4,7},{5,4},{6,5},{7,6},{8,11},{9,8},{10,9... | collective-permute-start | bytes 4616 | tf_op jit(solution)/shard_map/ppermute | solution.py:61
  90.6 5.1 %collective-permute-start.15 = (f32[384]{0:T(512)S(1)}, f32[384]{0:T(512)S(1)}, u32[]{:S(2)}, u32[]{:S(2)}) collective-permute-start(f32[384]{0:T(512)S(1)} %log_add_fusion.2), channel_id=1, source_target_pairs={{0,2},{1,3},{2,0},{3,1},{4,6},{5,7},{6,4},{7,5},{8,10},{9,11},{10,... | collective-permute-start | bytes 4616 | tf_op jit(solution)/shard_map/ppermute | solution.py:61
  92.0 4.8 %collective-permute-start.14 = (f32[384]{0:T(512)S(1)}, f32[384]{0:T(512)S(1)}, u32[]{:S(2)}, u32[]{:S(2)}) collective-permute-start(f32[384]{0:T(512)S(1)} %log_add_fusion.2), channel_id=1, source_target_pairs={{0,1},{1,2},{2,3},{3,0},{4,5},{5,6},{6,7},{7,4},{8,9},{9,10},{10,1... | collective-permute-start | bytes 4616 | tf_op jit(solution)/shard_map/ppermute | solution.py:61
  108.6 3.7 %collective-permute-start.19 = (f32[384]{0:T(512)S(1)}, f32[384]{0:T(512)S(1)}, u32[]{:S(2)}, u32[]{:S(2)}) collective-permute-start(f32[384]{0:T(512)S(1)} %log_add_fusion), channel_id=1, source_target_pairs={{0,3},{1,0},{2,1},{3,2},{4,7},{5,4},{6,5},{7,6},{8,11},{9,8},{10,9... | collective-permute-start | bytes 4616 | tf_op jit(solution)/shard_map/ppermute | solution.py:61
  110.4 5.1 %collective-permute-start.18 = (f32[384]{0:T(512)S(1)}, f32[384]{0:T(512)S(1)}, u32[]{:S(2)}, u32[]{:S(2)}) collective-permute-start(f32[384]{0:T(512)S(1)} %log_add_fusion), channel_id=1, source_target_pairs={{0,2},{1,3},{2,0},{3,1},{4,6},{5,7},{6,4},{7,5},{8,10},{9,11},{10,... | collective-permute-start | bytes 4616 | tf_op jit(solution)/shard_map/ppermute | solution.py:61
  111.3 4.8 %collective-permute-start.17 = (f32[384]{0:T(512)S(1)}, f32[384]{0:T(512)S(1)}, u32[]{:S(2)}, u32[]{:S(2)}) collective-permute-start(f32[384]{0:T(512)S(1)} %log_add_fusion), channel_id=1, source_target_pairs={{0,1},{1,2},{2,3},{3,0},{4,5},{5,6},{6,7},{7,4},{8,9},{9,10},{10,1... | collective-permute-start | bytes 4616 | tf_op jit(solution)/shard_map/ppermute | solution.py:61
  116.4 1.9 %collective-permute-start.20 = (bf16[384,384]{1,0:T(8,128)(2,1)S(1)}, bf16[384,384]{1,0:T(8,128)(2,1)S(1)}, u32[]{:S(2)}, u32[]{:S(2)}) collective-permute-start(bf16[384,384]{1,0:T(8,128)(2,1)S(1)} %get-tuple-element.82.w_own_ref), channel_id=1, source_target_pairs={{0,4},{4,0},{8,12},{12,8},{16,20},{20,16},{24,28},{28,24},{32,36},... | collective-permute-start | bytes 884744 | tf_op jit(solution)/shard_map/ppermute | solution.py:20
  124.1 15.2 %collective-permute-start.22 = (bf16[4,192,512]{2,1,0:T(8,128)(2,1)S(1)}, bf16[4,192,512]{2,1,0:T(8,128)(2,1)S(1)}, u32[]{:S(2)}, u32[]{:S(2)}) collective-permute-start(bf16[4,192,512]{2,1,0:T(8,128)(2,1)S(1)} %get-tuple-element.60), channel_id=1, source_target_pairs={{0,32},{4,12},{8,40},{12,20},{16,48},{20,28},{24,56},{28,4},{32,64... | collective-permute-start | bytes 2359304 | tf_op jit(solution)/shard_map/ppermute | solution.py:31
  124.8 14.9 %collective-permute-start.25 = (bf16[4,192,512]{2,1,0:T(8,128)(2,1)S(1)}, bf16[4,192,512]{2,1,0:T(8,128)(2,1)S(1)}, u32[]{:S(2)}, u32[]{:S(2)}) collective-permute-start(bf16[4,192,512]{2,1,0:T(8,128)(2,1)S(1)} %get-tuple-element.64), channel_id=1, source_target_pairs={{0,96},{4,28},{8,104},{12,4},{16,112},{20,12},{24,120},{28,20},{32... | collective-permute-start | bytes 2359304 | tf_op jit(solution)/shard_map/ppermute | solution.py:31
  137.2 12.1 %collective-permute-start.21 = (bf16[4,192,512]{2,1,0:T(8,128)(2,1)S(1)}, bf16[4,192,512]{2,1,0:T(8,128)(2,1)S(1)}, u32[]{:S(2)}, u32[]{:S(2)}) collective-permute-start(bf16[4,192,512]{2,1,0:T(8,128)(2,1)S(1)} %get-tuple-element.58), channel_id=1, source_target_pairs={{0,96},{4,28},{8,104},{12,4},{16,112},{20,12},{24,120},{28,20},{32... | collective-permute-start | bytes 2359304 | tf_op jit(solution)/shard_map/ppermute | solution.py:31
  137.3 21.9 %collective-permute-start.24 = (bf16[4,192,512]{2,1,0:T(8,128)(2,1)S(1)}, bf16[4,192,512]{2,1,0:T(8,128)(2,1)S(1)}, u32[]{:S(2)}, u32[]{:S(2)}) collective-permute-start(bf16[4,192,512]{2,1,0:T(8,128)(2,1)S(1)} %get-tuple-element.62), channel_id=1, source_target_pairs={{0,32},{4,12},{8,40},{12,20},{16,48},{20,28},{24,56},{28,4},{32,64... | collective-permute-start | bytes 2359304 | tf_op jit(solution)/shard_map/ppermute | solution.py:31
  139.5 19.5 %collective-permute-start.23 = (bf16[4,192,512]{2,1,0:T(8,128)(2,1)S(1)}, bf16[4,192,512]{2,1,0:T(8,128)(2,1)S(1)}, u32[]{:S(2)}, u32[]{:S(2)}) collective-permute-start(bf16[4,192,512]{2,1,0:T(8,128)(2,1)S(1)} %add_convert_fusion.1), channel_id=1, source_target_pairs={{0,32},{4,12},{8,40},{12,20},{16,48},{20,28},{24,56},{28,4},{32,64... | collective-permute-start | bytes 2359304 | tf_op jit(solution)/shard_map/ppermute | solution.py:31
  139.9 19.4 %collective-permute-start.26 = (bf16[4,192,512]{2,1,0:T(8,128)(2,1)S(1)}, bf16[4,192,512]{2,1,0:T(8,128)(2,1)S(1)}, u32[]{:S(2)}, u32[]{:S(2)}) collective-permute-start(bf16[4,192,512]{2,1,0:T(8,128)(2,1)S(1)} %add_convert_fusion), channel_id=1, source_target_pairs={{0,96},{4,28},{8,104},{12,4},{16,112},{20,12},{24,120},{28,20},{32... | collective-permute-start | bytes 2359304 | tf_op jit(solution)/shard_map/ppermute | solution.py:31
  149.3 10.3 %copy-start.1 = (bf16[4,192,512]{2,1,0:T(8,128)(2,1)}, bf16[4,192,512]{2,1,0:T(8,128)(2,1)S(1)}, u32[]{:S(2)}) copy-start(bf16[4,192,512]{2,1,0:T(8,128)(2,1)S(1)} %collective-permute-done.21) | copy-start | bytes 2359300
  160.0 16.1 %collective-permute-start.27 = (bf16[384,512]{1,0:T(8,128)(2,1)S(1)}, bf16[384,512]{1,0:T(8,128)(2,1)S(1)}, u32[]{:S(2)}, u32[]{:S(2)}) collective-permute-start(bf16[384,512]{1,0:T(8,128)(2,1)S(1)} %pad_maximum_fusion.2), channel_id=1, source_target_pairs={{0,16},{4,68},{8,24},{12,76},{16,0},{20,84},{24,8},{28,92},{32,48}... | collective-permute-start | bytes 1179656 | tf_op jit(solution)/shard_map/ppermute | solution.py:31
  161.2 14.9 %collective-permute-start.28 = (bf16[384,512]{1,0:T(8,128)(2,1)S(1)}, bf16[384,512]{1,0:T(8,128)(2,1)S(1)}, u32[]{:S(2)}, u32[]{:S(2)}) collective-permute-start(bf16[384,512]{1,0:T(8,128)(2,1)S(1)} %pad_maximum_fusion.3), channel_id=1, source_target_pairs={{0,8},{4,36},{8,16},{12,44},{16,24},{20,52},{24,0},{28,60},{32,40}... | collective-permute-start | bytes 1179656 | tf_op jit(solution)/shard_map/ppermute | solution.py:31
  162.2 14.0 %collective-permute-start.29 = (bf16[384,512]{1,0:T(8,128)(2,1)S(1)}, bf16[384,512]{1,0:T(8,128)(2,1)}, u32[]{:S(2)}, u32[]{:S(2)}) collective-permute-start(bf16[384,512]{1,0:T(8,128)(2,1)S(1)} %pad_maximum_fusion.4), channel_id=1, source_target_pairs={{0,24},{4,100},{8,0},{12,108},{16,8},{20,116},{24,16},{28,124},{32... | collective-permute-start | bytes 1179656 | tf_op jit(solution)/shard_map/ppermute | solution.py:31
  (1 other events, 0.9 us)

commit v5 on v1

v5 whole, which is shorter than its diff:
```python
import jax
import jax.numpy as jnp
from jax import lax
from jax.experimental import pallas as pl
from jax.experimental.pallas import tpu as pltpu
from jax.sharding import PartitionSpec as P

ITERS = 3
EPS = 0.004
SIDE = 4
OFFS = (2, 1, 3)
BLOCKS = SIDE * SIDE
VMEM_LIMIT = 24 * 1024 * 1024

SPOTS = [(k, m) for k in (0, 1, 3, 2) for m in OFFS + (0,)]


def swap(values):
    n = lax.axis_size("dp")
    return lax.ppermute(values, "dp", [(i, i ^ 1) for i in range(n)])


def hop(values, k, first):
    pairs = []
    for y in range(SIDE):
        for z in range(SIDE):
            for c in range(2):
                along_z = (c == 0) == first
                to_y, to_z = (y, (z + k) % SIDE) if along_z else ((y + k) % SIDE, z)
                pairs.append(((y * SIDE + z) * 2 + c, (to_y * SIDE + to_z) * 2 + c))
    return lax.ppermute(values, "dp", pairs)


def block_ids(y, z, core):
    ids = []
    for k, m in SPOTS:
        dy = jnp.where(core == 0, k, m)
        dz = jnp.where(core == 0, m, k)
        ids.append((((y + dy) % SIDE) * SIDE + (z + dz) % SIDE) * 2 + core)
    return jnp.stack(ids).astype(jnp.int32)


def lse(values, axis):
    peak = jnp.max(values, axis=axis, keepdims=True)
    total = jnp.sum(jnp.exp(values - peak), axis=axis)
    return jnp.squeeze(peak, axis) + jnp.log(total)


def to_all_dp(values):
    n = lax.axis_size("dp")
    return lax.all_to_all(
        jnp.broadcast_to(values[None], (n,) + values.shape), "dp", 0, 0
    )


def to_all_noise(values):
    n = lax.axis_size("noise")
    parts = [values]
    for k in range(1, n):
        parts.append(
            lax.ppermute(values, "noise", [(i, (i + k) % n) for i in range(n)])
        )
    return jnp.stack(parts)


def call(kernel, ins, in_specs, out_shape, out_specs, scratch, flops, moved):
    return pl.pallas_call(
        kernel,
        in_specs=in_specs,
        out_specs=out_specs,
        out_shape=out_shape,
        scratch_shapes=scratch,
        compiler_params=pltpu.CompilerParams(vmem_limit_bytes=VMEM_LIMIT),
        cost_estimate=pl.CostEstimate(
            flops=flops, bytes_accessed=moved, transcendentals=0
        ),
    )(*ins)


IN_SMEM = pl.BlockSpec(memory_space=pltpu.SMEM)
IN_VMEM = pl.BlockSpec(memory_space=pltpu.VMEM)
ANYWHERE = pl.BlockSpec(memory_space=pl.ANY)


def in_hbm(arrays):
    return [pltpu.with_memory_space_constraint(a, pltpu.HBM) for a in arrays]


def block_copies(ids_ref, t, refs, to, spot, sems):
    rows, width = refs[0].shape
    block = width // (2 * BLOCKS)
    place = pl.multiple_of(ids_ref[t] * block, block)
    return [
        pltpu.make_async_copy(
            ref.at[:, pl.ds(place, block)],
            to.at[pl.ds(b * rows, rows), pl.ds(spot * block, block)],
            sems.at[b, spot],
        )
        for b, ref in enumerate(refs)
    ]


def held_blocks(ids, data, data_other):
    rows, width = data.shape

    def kernel(ids_ref, data_ref, data_other_ref, held, sems):
        copies = []
        for t in range(BLOCKS):
            copies += block_copies(
                ids_ref, t, (data_ref, data_other_ref), held, t, sems
            )
        for copy in copies:
            copy.start()
        for copy in copies:
            copy.wait()

    return call(
        kernel,
        [ids] + in_hbm([data, data_other]),
        [IN_SMEM, ANYWHERE, ANYWHERE],
        pltpu.VMEM((2 * rows, width // 2), data.dtype),
        IN_VMEM,
        [pltpu.SemaphoreType.DMA((2, BLOCKS))],
        0,
        rows * width * 4,
    )


def part_dots(start, groups, held, before, last):
    sizes = [g[0].shape[0] for g in groups]
    rows = sum(p.shape[1] for p in groups[0])
    block = groups[0][0].shape[2]
    both = held.shape[0]
    inner = both // 2
    parts = [p for g in groups for p in g]
    per = len(groups[0])
    height = rows // per
    spots = [(a, i) for a, size in enumerate(sizes) for i in range(size)]

    def kernel(*refs):
        pieces, (held_ref, *rest) = refs[: len(parts)], refs[len(parts) :]
        for p in range(per):
            here = pl.ds(p * height, height)
            total = None if before is None else rest[0][here]
            for t, (a, i) in enumerate(spots):
                part = lax.dot_general(
                    pieces[a * per + p][i],
                    held_ref[:, (start + t) * block : (start + t + 1) * block],
                    (((1,), (1,)), ((), ())),
                    preferred_element_type=jnp.float32,
                )
                total = part if total is None else total + part
            if last:
                rest[-2][here] = total[:, :inner]
                rest[-1][here] = total[:, inner:]
            else:
                rest[-1][here] = total

    ins = parts + [held] + ([] if before is None else [before])
    half = jax.ShapeDtypeStruct((rows, inner), jnp.float32)
    outs = [half, half] if last else [jax.ShapeDtypeStruct((rows, both), jnp.float32)]
    got = call(
        kernel,
        ins,
        [IN_VMEM] * len(ins),
        outs,
        [IN_VMEM] * len(outs),
        [],
        len(spots) * 2 * rows * both * block,
        len(spots) * block * 2 * (both + rows),
    )
    return got if len(got) > 1 else got[0]


def gathered_dots(noise, held, sq_data):
    half = noise.shape[0] // 2
    along = [hop(noise, -k, True) for k in OFFS] + [noise]
    top = jnp.stack([block[:half] for block in along])
    bottom = jnp.stack([block[half:] for block in along])
    top, bottom, sq_data = lax.optimization_barrier((top, bottom, sq_data))
    up_top, down_bottom = hop(top, -1, False), hop(bottom, 1, False)
    up_bottom, down_top = hop(bottom, -1, False), hop(top, 1, False)
    groups = [[block[None]] for block in along]
    dots = part_dots(0, groups, held, None, False)
    up_top, down_bottom, dots = lax.optimization_barrier((up_top, down_bottom, dots))
    far = [hop(up_top, -1, False), hop(down_bottom, 1, False)]
    groups = [[up_top, up_bottom], [down_top, down_bottom]]
    dots = part_dots(4, groups, held, dots, False)
    own, other = part_dots(12, [far], held, dots, True)
    return own + swap(other), sq_data


def part_sums(start, n, ins, ids, step=2):
    w_own, w_oth, data, data_other = ins
    rows, inner = w_own.shape
    dtype = data.dtype
    block = data.shape[1] // (2 * BLOCKS)
    half = rows // 2
    groups = len(start)

    def kernel(ids_ref, w_own_ref, w_oth_ref, data_ref, data_other_ref, *refs):
        outs, (weights, held, totals, in_sems, sems) = (
            refs[: 2 * groups],
            refs[2 * groups :],
        )
        into = []
        for a, first in enumerate(start):
            for i in range(n):
                into.append(
                    block_copies(
                        ids_ref,
                        first + i,
                        (data_ref, data_other_ref),
                        held,
                        a * n + i,
                        in_sems,
                    )
                )
                for copy in into[-1]:
                    copy.start()
        weights[:, :inner] = w_own_ref[...]
        weights[:, inner:] = w_oth_ref[...]
        out = []
        for a in range(groups):
            for i in range(0, n, step):
                spot = a * n + i
                for copies in into[spot : spot + step]:
                    for copy in copies:
                        copy.wait()
                total = jnp.dot(
                    weights[...],
                    held[:, spot * block : (spot + step) * block],
                    preferred_element_type=jnp.float32,
                ).astype(dtype)
                for j in range(step):
                    part = total[:, j * block : (j + 1) * block]
                    totals[2 * a, i + j] = part[:half]
                    totals[2 * a + 1, i + j] = part[half:]
            for p in range(2 * a, 2 * a + 2):
                out.append(pltpu.make_async_copy(totals.at[p], outs[p], sems.at[p]))
                out[-1].start()
        for copy in out:
            copy.wait()

    return call(
        kernel,
        [ids, w_own, w_oth] + in_hbm([data, data_other]),
        [IN_SMEM, IN_VMEM, IN_VMEM, ANYWHERE, ANYWHERE],
        [jax.ShapeDtypeStruct((n, half, block), dtype)] * (2 * groups),
        [ANYWHERE] * (2 * groups),
        [
            pltpu.VMEM((rows, 2 * inner), dtype),
            pltpu.VMEM((2 * inner, groups * n * block), dtype),
            pltpu.VMEM((2 * groups, n, half, block), dtype),
            pltpu.SemaphoreType.DMA((2, groups * n)),
            pltpu.SemaphoreType.DMA((2 * groups,)),
        ],
        groups * n * 4 * rows * inner * block,
        groups * n * 2 * block * (2 * inner + rows),
    )


def added(first, others):
    total = first.astype(jnp.float32)
    for other in others:
        total += other.astype(jnp.float32)
    return total


def scattered_sums(ins, ids, row_part):
    top, bottom = part_sums([12], 4, ins, ids)
    weights, top, bottom = lax.optimization_barrier((ins[0], top, bottom))
    ins = (weights,) + ins[1:]
    top, bottom = hop(top, 1, False), hop(bottom, -1, False)
    up_top, up_bottom, down_top, down_bottom = part_sums([4, 8], 4, ins, ids)
    weights, up_bottom, down_top = lax.optimization_barrier(
        (weights, up_bottom, down_top)
    )
    ins = (weights,) + ins[1:]
    tops, bottoms = [hop(down_top, -1, False)], [hop(up_bottom, 1, False)]
    near_top, near_bottom = part_sums([0], 4, ins, ids)
    tops.append(hop(added(up_top, [top]).astype(top.dtype), 1, False))
    bottoms.append(hop(added(down_bottom, [bottom]).astype(top.dtype), -1, False))
    totals = []
    for a in range(3):
        total = [
            added(near_top[a], [got[a] for got in tops]),
            added(near_bottom[a], [got[a] for got in bottoms]),
        ]
        totals.append(jnp.concatenate(total).astype(top.dtype))
    row_part, *totals = lax.optimization_barrier((row_part, *totals))
    sums = [hop(total, k, True) for total, k in zip(totals, OFFS)]
    row_sum = jnp.sum(to_all_dp(row_part), axis=0)
    row_sum, near_top = lax.optimization_barrier((row_sum, near_top))
    total = [
        added(near_top[3], [got[3] for got in tops]),
        added(near_bottom[3], [got[3] for got in bottoms]),
    ]
    return added(jnp.concatenate(total), sums), row_sum


def body(noise_latents, data_latents):
    width = data_latents.shape[1]
    place = lax.axis_index("dp")
    core = place % 2
    z = (place // 2) % SIDE
    y = place // (2 * SIDE)
    ids = block_ids(y, z, core)
    data_other = swap(data_latents)
    held = held_blocks(ids, data_latents, data_other)
    noise_f = noise_latents.astype(jnp.float32)
    sx_part = jnp.sum(noise_f * noise_f, axis=1)
    data_f = data_latents.astype(jnp.float32)
    sq_data = jnp.sum(data_f * data_f, axis=1)
    dots, sq_data = gathered_dots(noise_latents, held, sq_data)
    scale = 1.0 / (width * EPS)
    twice = dots * (2.0 * scale)
    sy = sq_data * scale
    sx = None
    g = jnp.zeros_like(sy)
    for step in range(ITERS):
        local = lse(twice + (g - sy)[None, :], 1)
        if sx is None:
            got = to_all_dp(jnp.stack([local, sx_part]))
            sx = jnp.sum(got[:, 1], axis=0) * scale
            got = got[:, 0]
        else:
            got = to_all_dp(local)
        f = sx - lse(got, 0)
        local = lse(twice + (f - sx)[:, None], 0)
        g = sy - lse(to_all_noise(local), 0)
    coupling = jnp.exp(twice + (f - sx)[:, None] + (g - sy)[None, :])
    weights = coupling.astype(jnp.bfloat16)
    total, row_sum = scattered_sums(
        (weights, swap(weights), data_latents, data_other),
        ids,
        jnp.sum(coupling, axis=1),
    )
    return (total / row_sum[:, None]).astype(jnp.bfloat16)


def solution(mesh):
    return jax.shard_map(
        body,
        mesh=mesh,
        in_specs=(P("noise", "dp"), P("dp", None)),
        out_specs=P("noise", "dp"),
        check_vma=False,
    )
```

time: 284 us -> 171 us (0.60)
  waiting for transfers between devices: 169 us -> 37.9 us
  starting transfers between devices: 10.4 us -> 42.6 us
  matrix products: 31.4 us -> 0 us
  Pallas kernels: 0 us -> 27.6 us
  between operations: 13.5 us -> 0.42 us
  other arithmetic: 13.1 us -> 16 us
    reduce_scatter x1 -> x0, waiting for transfers between devices: 89.5 us -> none  [body(): lax.psum_scatter(lax.dot_general(data_latents, coupling.astype(jnp.bfloat...]
    all_gather x1 -> x0, waiting for transfers between devices: 66.7 us -> none  [body(): piece = lax.all_gather(noise_latents, 'dp', axis=1, tiled=True)]
    dot_general x2 -> x0, matrix products: 31.4 us -> none  [the longest x1 17.4 us: body(): lax.dot_general(piece, data_latents, (((1,), (1,)), ((), ())), preferred_...]
    ppermute x0 -> x21, waiting for transfers between devices: none -> 30 us  [the longest x18 26.7 us: hop(): return lax.ppermute(values, 'dp', pairs)]
    ppermute x0 -> x21, starting transfers between devices: none -> 28.4 us  [the longest x18 28.1 us: hop(): return lax.ppermute(values, 'dp', pairs)]
    pallas_call x0 -> x7, Pallas kernels: none -> 27.6 us  [call(): pl.pallas_call(kernel, in_specs=in_specs, out_specs=out_specs, out_shape=...]
    ppermute x9, waiting for transfers between devices: 12.1 us -> 7.81 us  [to_all_noise(): lax.ppermute(values, 'noise', [(i, (i + k) % n) for i in range(n)])]
    ppermute x9, starting transfers between devices: 10.4 us -> 14.2 us  [to_all_noise(): lax.ppermute(values, 'noise', [(i, (i + k) % n) for i in range(n)])]
  transfers between devices with their start and end apart: 11 -> 30, of which waited for: 10 -> 18; matrix products, arithmetic and copies ran while one was open for 3% -> 6% of each run, Pallas kernels for 0% -> 13%
where the time goes in v5:
time: 171 us; the launch traced here: 170 us
  blocking collectives  44.8 us (26%)
  starting transfers between devices  42.6 us (25%)
  waiting for transfers between devices  37.9 us (22%)
  Pallas kernels  27.6 us (16%)
  other arithmetic  16 us (9%)
    all_to_all x4, blocking collectives, to_all_dp(): lax.all_to_all(jnp.broadcast_to(values[None], (n,) + values.shape), 'dp',...  44.8 us
    ppermute x18, starting transfers between devices, hop(): return lax.ppermute(values, 'dp', pairs)  28.1 us
    pallas_call x7, Pallas kernels, call(): pl.pallas_call(kernel, in_specs=in_specs, out_specs=out_specs, out_shape=...  27.6 us
    ppermute x18, waiting for transfers between devices, hop(): return lax.ppermute(values, 'dp', pairs)  26.7 us
    ppermute x9, starting transfers between devices, to_all_noise(): lax.ppermute(values, 'noise', [(i, (i + k) % n) for i in range(n)])  14.2 us
    ppermute x9, waiting for transfers between devices, to_all_noise(): lax.ppermute(values, 'noise', [(i, (i + k) % n) for i in range(n)])  7.81 us
    reduce_sum x1, other arithmetic, body(): sq_data = jnp.sum(data_f * data_f, axis=1)  7.14 us
  transfers between devices with their start and end apart: 30, of which 18 were waited for; matrix products, arithmetic and copies ran while one was open for 6% of the time, Pallas kernels for 13%

profile of v5, /device:TPU:0, one launch (start us, length us, event | category | flops | bytes accessed | tf_op | source)
XLA Modules:
  0.0 169.9 jit_solution(7305597809148297485)
XLA Ops:
  0.0 2.1 %collective-permute-start.2 = (bf16[384,512]{1,0:T(8,128)(2,1)}, bf16[384,512]{1,0:T(8,128)(2,1)S(1)}, u32[]{:S(2)}, u32[]{:S(2)}) collective-permute-start(bf16[384,512]{1,0:T(8,128)(2,1)} %param.2), channel_id=1, source_target_pairs={{0,8},{4,36},{8,16},{12,44},{16,24},{20,52},{24,0},{28,60},{32,40}... | collective-permute-start | bytes 1179656 | tf_op jit(solution)/shard_map/ppermute | solution.py:31
  2.1 3.6 %collective-permute-start = (bf16[384,512]{1,0:T(8,128)(2,1)}, bf16[384,512]{1,0:T(8,128)(2,1)S(1)}, u32[]{:S(2)}, u32[]{:S(2)}) collective-permute-start(bf16[384,512]{1,0:T(8,128)(2,1)} %param.2), channel_id=1, source_target_pairs={{0,16},{4,68},{8,24},{12,76},{16,0},{20,84},{24,8},{28,92},{32,48}... | collective-permute-start | bytes 1179656 | tf_op jit(solution)/shard_map/ppermute | solution.py:31
  6.7 7.1 %multiply_reduce_fusion = f32[384]{0:T(512)S(1)} fusion(bf16[384,16384]{1,0:T(8,128)(2,1)} %data_ref.7), kind=kLoop, calls=%fused_computation | loop fusion | flops 18873984 | bytes 12584448 | tf_op jit(solution)/shard_map/reduce_sum | solution.py:314
  13.8 2.0 %collective-permute-done = bf16[384,512]{1,0:T(8,128)(2,1)S(1)} collective-permute-done((bf16[384,512]{1,0:T(8,128)(2,1)}, bf16[384,512]{1,0:T(8,128)(2,1)S(1)}, u32[]{:S(2)}, u32[]{:S(2)}) %collective-permute-start) | collective-permute-done | bytes 393248 | tf_op jit(solution)/shard_map/ppermute | solution.py:31
  17.3 3.0 %collective-permute-start.3 = (bf16[4,192,512]{2,1,0:T(8,128)(2,1)}, bf16[4,192,512]{2,1,0:T(8,128)(2,1)S(1)}, u32[]{:S(2)}, u32[]{:S(2)}) collective-permute-start(bf16[4,192,512]{2,1,0:T(8,128)(2,1)} %get-tuple-element.33), channel_id=1, source_target_pairs={{0,96},{4,28},{8,104},{12,4},{16,112},{20,12},{24,120},{28,20},{32... | collective-permute-start | bytes 2359304 | tf_op jit(solution)/shard_map/ppermute | solution.py:31
  20.4 3.2 %collective-permute-start.8 = (bf16[4,192,512]{2,1,0:T(8,128)(2,1)}, bf16[4,192,512]{2,1,0:T(8,128)(2,1)}, u32[]{:S(2)}, u32[]{:S(2)}) collective-permute-start(bf16[4,192,512]{2,1,0:T(8,128)(2,1)} %get-tuple-element.34), channel_id=1, source_target_pairs={{0,96},{4,28},{8,104},{12,4},{16,112},{20,12},{24,120},{28,20},{32... | collective-permute-start | bytes 2359304 | tf_op jit(solution)/shard_map/ppermute | solution.py:31
  23.7 5.6 %shard_map.28.refs_4_.refs_2_ = bf16[768,8192]{1,0:T(8,128)(2,1)S(1)} custom-call(s32[16]{0:T(128)S(1)} %stack.153.ids_ref, bf16[384,16384]{1,0:T(8,128)(2,1)} %data_ref.7, bf16[384,16384]{1,0:T(8,128)(2,1)} %collective-permute-done.5.data_other_ref), custom_call_target="tpu_custom_call" | custom-call | bytes 25165824 | tf_op jit(solution)/shard_map/pallas_call | solution.py:67
  30.8 3.0 %collective-permute-done.4.refs_3_ = bf16[4,192,512]{2,1,0:T(8,128)(2,1)S(1)} collective-permute-done((bf16[4,192,512]{2,1,0:T(8,128)(2,1)}, bf16[4,192,512]{2,1,0:T(8,128)(2,1)S(1)}, u32[]{:S(2)}, u32[]{:S(2)}) %collective-permute-start.4) | collective-permute-done | bytes 786464 | tf_op jit(solution)/shard_map/ppermute | solution.py:31
  35.8 2.8 %collective-permute-done.8.refs_1_ = bf16[4,192,512]{2,1,0:T(8,128)(2,1)} collective-permute-done((bf16[4,192,512]{2,1,0:T(8,128)(2,1)}, bf16[4,192,512]{2,1,0:T(8,128)(2,1)}, u32[]{:S(2)}, u32[]{:S(2)}) %collective-permute-start.8) | collective-permute-done | bytes 786464 | tf_op jit(solution)/shard_map/ppermute | solution.py:31
  38.6 3.7 %collective-permute-done.9.refs_2_ = bf16[4,192,512]{2,1,0:T(8,128)(2,1)} collective-permute-done((bf16[4,192,512]{2,1,0:T(8,128)(2,1)}, bf16[4,192,512]{2,1,0:T(8,128)(2,1)}, u32[]{:S(2)}, u32[]{:S(2)}) %collective-permute-start.9) | collective-permute-done | bytes 786464 | tf_op jit(solution)/shard_map/ppermute | solution.py:31
  42.3 5.6 %shard_map.30.refs_3_ = f32[384,768]{1,0:T(8,128)S(1)} custom-call(bf16[4,192,512]{2,1,0:T(8,128)(2,1)S(1)} %collective-permute-done.3.refs_0_, bf16[4,192,512]{2,1,0:T(8,128)(2,1)} %collective-permute-done.8.refs_1_, bf16[4,192,512]{2,1,0:T(8,128)(2,1)} %collective-permute-done.9.refs_2_, bf16[4,192,512]{2,1,0:T(8,128)(2,1)S(1)} %collective-permute-done.4.refs_3_, ...), custom_call_target="tpu_custom_call" | custom-call | flops 2415919104 | bytes 9437184 | tf_op jit(solution)/shard_map/pallas_call | solution.py:67
  47.9 2.7 %collective-permute-done.7.refs_1_ = bf16[4,192,512]{2,1,0:T(8,128)(2,1)S(1)} collective-permute-done((bf16[4,192,512]{2,1,0:T(8,128)(2,1)S(1)}, bf16[4,192,512]{2,1,0:T(8,128)(2,1)S(1)}, u32[]{:S(2)}, u32[]{:S(2)}) %collective-permute-start.7) | collective-permute-done | bytes 786464 | tf_op jit(solution)/shard_map/ppermute | solution.py:31
  50.6 2.2 %shard_map.31 = (f32[384,384]{1,0:T(8,128)S(1)}, f32[384,384]{1,0:T(8,128)S(1)}) custom-call(bf16[4,192,512]{2,1,0:T(8,128)(2,1)S(1)} %collective-permute-done.6.refs_0_, bf16[4,192,512]{2,1,0:T(8,128)(2,1)S(1)} %collective-permute-done.7.refs_1_, bf16[768,8192]{1,0:T(8,128)(2,1)S(1)} %shard_map.28.refs_4_.refs_2_, f32[384,768]{1,0:T(8,128)S(1)} %shard_map.30.refs_3_), custom_call_target="tpu_custom_call" | custom-call | flops 1207959552 | bytes 4718592 | tf_op jit(solution)/shard_map/pallas_call | solution.py:67
  53.3 1.8 %collective-permute-done.10 = f32[384,384]{1,0:T(8,128)S(1)} collective-permute-done((f32[384,384]{1,0:T(8,128)S(1)}, f32[384,384]{1,0:T(8,128)S(1)}, u32[]{:S(2)}, u32[]{:S(2)}) %collective-permute-start.10) | collective-permute-done | bytes 589856 | tf_op jit(solution)/shard_map/ppermute | solution.py:20
  55.6 11.6 %all_to_all.29 = f32[32,2,384]{2,1,0:T(2,128)S(1)} all-to-all(f32[32,2,384]{2,1,0:T(2,128)S(1)} %broadcast_in_dim.23), channel_id=1, replica_groups=mesh['dp'=32,'noise'=4] {'dp'}, dimensions={0} | all-to-all | bytes 196608 | tf_op jit(solution)/shard_map/all_to_all | solution.py:51
  69.2 2.7 %collective-permute-start.12 = (f32[384]{0:T(512)S(1)}, f32[384]{0:T(512)S(1)}, u32[]{:S(2)}, u32[]{:S(2)}) collective-permute-start(f32[384]{0:T(512)S(1)} %log_add_fusion.4), channel_id=1, source_target_pairs={{0,2},{1,3},{2,0},{3,1},{4,6},{5,7},{6,4},{7,5},{8,10},{9,11},{10,... | collective-permute-start | bytes 4616 | tf_op jit(solution)/shard_map/ppermute | solution.py:61
  76.0 10.9 %all_to_all.30 = f32[32,1,384]{2,1,0:T(1,128)S(1)} all-to-all(f32[32,1,384]{2,1,0:T(1,128)S(1)} %broadcast_in_dim.24), channel_id=1, replica_groups=mesh['dp'=32,'noise'=4] {'dp'}, dimensions={0} | all-to-all | bytes 98304 | tf_op jit(solution)/shard_map/all_to_all | solution.py:51
  87.7 3.8 %collective-permute-start.15 = (f32[384]{0:T(512)S(1)}, f32[384]{0:T(512)S(1)}, u32[]{:S(2)}, u32[]{:S(2)}) collective-permute-start(f32[384]{0:T(512)S(1)} %log_add_fusion.2), channel_id=1, source_target_pairs={{0,2},{1,3},{2,0},{3,1},{4,6},{5,7},{6,4},{7,5},{8,10},{9,11},{10,... | collective-permute-start | bytes 4616 | tf_op jit(solution)/shard_map/ppermute | solution.py:61
  93.1 2.0 %collective-permute-done.16 = f32[384]{0:T(512)S(1)} collective-permute-done((f32[384]{0:T(512)S(1)}, f32[384]{0:T(512)S(1)}, u32[]{:S(2)}, u32[]{:S(2)}) %collective-permute-start.16) | collective-permute-done | bytes 1568 | tf_op jit(solution)/shard_map/ppermute | solution.py:61
  95.7 10.8 %all_to_all.31 = f32[32,1,384]{2,1,0:T(1,128)S(1)} all-to-all(f32[32,1,384]{2,1,0:T(1,128)S(1)} %broadcast_in_dim.25), channel_id=1, replica_groups=mesh['dp'=32,'noise'=4] {'dp'}, dimensions={0} | all-to-all | bytes 98304 | tf_op jit(solution)/shard_map/all_to_all | solution.py:51
  107.0 2.7 %collective-permute-start.18 = (f32[384]{0:T(512)S(1)}, f32[384]{0:T(512)S(1)}, u32[]{:S(2)}, u32[]{:S(2)}) collective-permute-start(f32[384]{0:T(512)S(1)} %log_add_fusion), channel_id=1, source_target_pairs={{0,2},{1,3},{2,0},{3,1},{4,6},{5,7},{6,4},{7,5},{8,10},{9,11},{10,... | collective-permute-start | bytes 4616 | tf_op jit(solution)/shard_map/ppermute | solution.py:61
  115.3 3.7 %shard_map.32 = (bf16[4,192,512]{2,1,0:T(8,128)(2,1)S(1)}, bf16[4,192,512]{2,1,0:T(8,128)(2,1)S(1)}) custom-call(s32[16]{0:T(128)S(1)} %stack.153.ids_ref, bf16[384,384]{1,0:T(8,128)(2,1)S(1)} %get-tuple-element.46.w_own_ref, bf16[384,384]{1,0:T(8,128)(2,1)S(1)} %collective-permute-done.20.w_oth_ref, bf16[384,16384]{1,0:T(8,128)(2,1)} %data_ref.7, ...), custom_call_target="tpu_custom_call" | custom-call | flops 1207959552 | bytes 4718592 | tf_op jit(solution)/shard_map/pallas_call | solution.py:67
  119.6 2.6 %collective-permute-start.25 = (bf16[4,192,512]{2,1,0:T(8,128)(2,1)S(1)}, bf16[4,192,512]{2,1,0:T(8,128)(2,1)S(1)}, u32[]{:S(2)}, u32[]{:S(2)}) collective-permute-start(bf16[4,192,512]{2,1,0:T(8,128)(2,1)S(1)} %get-tuple-element.54), channel_id=1, source_target_pairs={{0,96},{4,28},{8,104},{12,4},{16,112},{20,12},{24,120},{28,20},{32... | collective-permute-start | bytes 2359304 | tf_op jit(solution)/shard_map/ppermute | solution.py:31
  122.3 5.4 %shard_map.33 = (bf16[4,192,512]{2,1,0:T(8,128)(2,1)S(1)}, bf16[4,192,512]{2,1,0:T(8,128)(2,1)S(1)}, bf16[4,192,512]{2,1,0:T(8,128)(2,1)S(1)}, bf16[4,192,512]{2,1,0:T(8,128)(2,1)S(1)}) custom-call(s32[16]{0:T(128)S(1)} %stack.153.ids_ref, bf16[384,384]{1,0:T(8,128)(2,1)S(1)} %get-tuple-element.46.w_own_ref, ...), custom_call_target="tpu_custom_call" | custom-call | flops 2415919104 | bytes 9437184 | tf_op jit(solution)/shard_map/pallas_call | solution.py:67
  127.8 2.0 %collective-permute-start.24 = (bf16[4,192,512]{2,1,0:T(8,128)(2,1)S(1)}, bf16[4,192,512]{2,1,0:T(8,128)(2,1)S(1)}, u32[]{:S(2)}, u32[]{:S(2)}) collective-permute-start(bf16[4,192,512]{2,1,0:T(8,128)(2,1)S(1)} %get-tuple-element.52), channel_id=1, source_target_pairs={{0,32},{4,12},{8,40},{12,20},{16,48},{20,28},{24,56},{28,4},{32,64... | collective-permute-start | bytes 2359304 | tf_op jit(solution)/shard_map/ppermute | solution.py:31
  129.8 2.4 %collective-permute-done.22 = bf16[4,192,512]{2,1,0:T(8,128)(2,1)S(1)} collective-permute-done((bf16[4,192,512]{2,1,0:T(8,128)(2,1)S(1)}, bf16[4,192,512]{2,1,0:T(8,128)(2,1)S(1)}, u32[]{:S(2)}, u32[]{:S(2)}) %collective-permute-start.22) | collective-permute-done | bytes 786464 | tf_op jit(solution)/shard_map/ppermute | solution.py:31
  132.8 3.3 %collective-permute-start.26 = (bf16[4,192,512]{2,1,0:T(8,128)(2,1)S(1)}, bf16[4,192,512]{2,1,0:T(8,128)(2,1)S(1)}, u32[]{:S(2)}, u32[]{:S(2)}) collective-permute-start(bf16[4,192,512]{2,1,0:T(8,128)(2,1)S(1)} %add_convert_fusion), channel_id=1, source_target_pairs={{0,96},{4,28},{8,104},{12,4},{16,112},{20,12},{24,120},{28,20},{32... | collective-permute-start | bytes 2359304 | tf_op jit(solution)/shard_map/ppermute | solution.py:31
  136.0 3.7 %shard_map.34 = (bf16[4,192,512]{2,1,0:T(8,128)(2,1)S(1)}, bf16[4,192,512]{2,1,0:T(8,128)(2,1)S(1)}) custom-call(s32[16]{0:T(128)S(1)} %stack.153.ids_ref, bf16[384,384]{1,0:T(8,128)(2,1)S(1)} %get-tuple-element.46.w_own_ref, bf16[384,384]{1,0:T(8,128)(2,1)S(1)} %collective-permute-done.20.w_oth_ref, bf16[384,16384]{1,0:T(8,128)(2,1)} %data_ref.7, ...), custom_call_target="tpu_custom_call" | custom-call | flops 1207959552 | bytes 4718592 | tf_op jit(solution)/shard_map/pallas_call | solution.py:67
  140.2 9.5 %collective-permute-done.23 = bf16[4,192,512]{2,1,0:T(8,128)(2,1)S(1)} collective-permute-done((bf16[4,192,512]{2,1,0:T(8,128)(2,1)S(1)}, bf16[4,192,512]{2,1,0:T(8,128)(2,1)S(1)}, u32[]{:S(2)}, u32[]{:S(2)}) %collective-permute-start.23) | collective-permute-done | bytes 786464 | tf_op jit(solution)/shard_map/ppermute | solution.py:31
  152.8 2.3 %collective-permute-start.29 = (bf16[384,512]{1,0:T(8,128)(2,1)S(1)}, bf16[384,512]{1,0:T(8,128)(2,1)}, u32[]{:S(2)}, u32[]{:S(2)}) collective-permute-start(bf16[384,512]{1,0:T(8,128)(2,1)S(1)} %pad_maximum_fusion.4), channel_id=1, source_target_pairs={{0,24},{4,100},{8,0},{12,108},{16,8},{20,116},{24,16},{28,124},{32... | collective-permute-start | bytes 1179656 | tf_op jit(solution)/shard_map/ppermute | solution.py:31
  155.2 11.6 %all_to_all.32 = f32[32,1,384]{2,1,0:T(1,128)S(1)} all-to-all(f32[32,1,384]{2,1,0:T(1,128)S(1)} %broadcast_in_dim.26), channel_id=1, replica_groups=mesh['dp'=32,'noise'=4] {'dp'}, dimensions={0} | all-to-all | bytes 98304 | tf_op jit(solution)/shard_map/all_to_all | solution.py:51
  168.0 1.9 %fusion.3 = bf16[384,512]{1,0:T(8,128)(2,1)} fusion(bf16[384,512]{1,0:T(8,128)(2,1)} %collective-permute-done.29, bf16[384,512]{1,0:T(8,128)(2,1)S(1)} %collective-permute-done.28, bf16[384,512]{1,0:T(8,128)(2,1)S(1)} %collective-permute-done.27, f32[192,512]{1,0:T(8,128)S(1)} %get-tuple-element.65, f32[192,512]{1,0:T(8,128)S(1)} %add_bitcast_fusion.1, ...), kind=kLoop, calls=%fused_computation.10 | loop fusion | flops 1769472 | bytes 2360832 | tf_op jit(solution)/shard_map/convert_element_type | solution.py:339
  (120 shorter events, 28.1 us)
Async XLA Ops:
  0.0 13.8 %copy-start = (bf16[384,512]{1,0:T(8,128)(2,1)S(1)}, bf16[384,512]{1,0:T(8,128)(2,1)}, u32[]{:S(2)}) copy-start(bf16[384,512]{1,0:T(8,128)(2,1)} %param.2) | copy-start | bytes 1179652
  0.0 23.7 %collective-permute-start.5 = (bf16[384,16384]{1,0:T(8,128)(2,1)}, bf16[384,16384]{1,0:T(8,128)(2,1)}, u32[]{:S(2)}, u32[]{:S(2)}) collective-permute-start(bf16[384,16384]{1,0:T(8,128)(2,1)} %data_ref.7), channel_id=1, source_target_pairs={{0,4},{4,0},{8,12},{12,8},{16,20},{20,16},{24,28},{28,24},{32,36},... | collective-permute-start | bytes 37748744 | tf_op jit(solution)/shard_map/ppermute | solution.py:20
  0.0 15.9 %collective-permute-start.2 = (bf16[384,512]{1,0:T(8,128)(2,1)}, bf16[384,512]{1,0:T(8,128)(2,1)S(1)}, u32[]{:S(2)}, u32[]{:S(2)}) collective-permute-start(bf16[384,512]{1,0:T(8,128)(2,1)} %param.2), channel_id=1, source_target_pairs={{0,8},{4,36},{8,16},{12,44},{16,24},{20,52},{24,0},{28,60},{32,40}... | collective-permute-start | bytes 1179656 | tf_op jit(solution)/shard_map/ppermute | solution.py:31
  2.1 13.8 %collective-permute-start = (bf16[384,512]{1,0:T(8,128)(2,1)}, bf16[384,512]{1,0:T(8,128)(2,1)S(1)}, u32[]{:S(2)}, u32[]{:S(2)}) collective-permute-start(bf16[384,512]{1,0:T(8,128)(2,1)} %param.2), channel_id=1, source_target_pairs={{0,16},{4,68},{8,24},{12,76},{16,0},{20,84},{24,8},{28,92},{32,48}... | collective-permute-start | bytes 1179656 | tf_op jit(solution)/shard_map/ppermute | solution.py:31
  5.7 10.2 %collective-permute-start.1 = (bf16[384,512]{1,0:T(8,128)(2,1)}, bf16[384,512]{1,0:T(8,128)(2,1)S(1)}, u32[]{:S(2)}, u32[]{:S(2)}) collective-permute-start(bf16[384,512]{1,0:T(8,128)(2,1)} %param.2), channel_id=1, source_target_pairs={{0,24},{4,100},{8,0},{12,108},{16,8},{20,116},{24,16},{28,124},{32... | collective-permute-start | bytes 1179656 | tf_op jit(solution)/shard_map/ppermute | solution.py:31
  17.3 13.4 %collective-permute-start.3 = (bf16[4,192,512]{2,1,0:T(8,128)(2,1)}, bf16[4,192,512]{2,1,0:T(8,128)(2,1)S(1)}, u32[]{:S(2)}, u32[]{:S(2)}) collective-permute-start(bf16[4,192,512]{2,1,0:T(8,128)(2,1)} %get-tuple-element.33), channel_id=1, source_target_pairs={{0,96},{4,28},{8,104},{12,4},{16,112},{20,12},{24,120},{28,20},{32... | collective-permute-start | bytes 2359304 | tf_op jit(solution)/shard_map/ppermute | solution.py:31
  20.4 13.4 %collective-permute-start.4 = (bf16[4,192,512]{2,1,0:T(8,128)(2,1)}, bf16[4,192,512]{2,1,0:T(8,128)(2,1)S(1)}, u32[]{:S(2)}, u32[]{:S(2)}) collective-permute-start(bf16[4,192,512]{2,1,0:T(8,128)(2,1)} %get-tuple-element.34), channel_id=1, source_target_pairs={{0,32},{4,12},{8,40},{12,20},{16,48},{20,28},{24,56},{28,4},{32,64... | collective-permute-start | bytes 2359304 | tf_op jit(solution)/shard_map/ppermute | solution.py:31
  20.4 18.2 %collective-permute-start.8 = (bf16[4,192,512]{2,1,0:T(8,128)(2,1)}, bf16[4,192,512]{2,1,0:T(8,128)(2,1)}, u32[]{:S(2)}, u32[]{:S(2)}) collective-permute-start(bf16[4,192,512]{2,1,0:T(8,128)(2,1)} %get-tuple-element.34), channel_id=1, source_target_pairs={{0,96},{4,28},{8,104},{12,4},{16,112},{20,12},{24,120},{28,20},{32... | collective-permute-start | bytes 2359304 | tf_op jit(solution)/shard_map/ppermute | solution.py:31
  23.6 18.7 %collective-permute-start.9 = (bf16[4,192,512]{2,1,0:T(8,128)(2,1)}, bf16[4,192,512]{2,1,0:T(8,128)(2,1)}, u32[]{:S(2)}, u32[]{:S(2)}) collective-permute-start(bf16[4,192,512]{2,1,0:T(8,128)(2,1)} %get-tuple-element.33), channel_id=1, source_target_pairs={{0,32},{4,12},{8,40},{12,20},{16,48},{20,28},{24,56},{28,4},{32,64... | collective-permute-start | bytes 2359304 | tf_op jit(solution)/shard_map/ppermute | solution.py:31
  33.8 14.1 %collective-permute-start.6 = (bf16[4,192,512]{2,1,0:T(8,128)(2,1)S(1)}, bf16[4,192,512]{2,1,0:T(8,128)(2,1)S(1)}, u32[]{:S(2)}, u32[]{:S(2)}) collective-permute-start(bf16[4,192,512]{2,1,0:T(8,128)(2,1)S(1)} %collective-permute-done.3.refs_0_), channel_id=1, source_target_pairs={{0,96},{4,28},{8,104},{12,4},{16,112},{20,12},{24,120},{28,20},{32... | collective-permute-start | bytes 2359304 | tf_op jit(solution)/shard_map/ppermute | solution.py:31
  34.1 16.5 %collective-permute-start.7 = (bf16[4,192,512]{2,1,0:T(8,128)(2,1)S(1)}, bf16[4,192,512]{2,1,0:T(8,128)(2,1)S(1)}, u32[]{:S(2)}, u32[]{:S(2)}) collective-permute-start(bf16[4,192,512]{2,1,0:T(8,128)(2,1)S(1)} %collective-permute-done.4.refs_3_), channel_id=1, source_target_pairs={{0,32},{4,12},{8,40},{12,20},{16,48},{20,28},{24,56},{28,4},{32,64... | collective-permute-start | bytes 2359304 | tf_op jit(solution)/shard_map/ppermute | solution.py:31
  52.8 2.3 %collective-permute-start.10 = (f32[384,384]{1,0:T(8,128)S(1)}, f32[384,384]{1,0:T(8,128)S(1)}, u32[]{:S(2)}, u32[]{:S(2)}) collective-permute-start(f32[384,384]{1,0:T(8,128)S(1)} %get-tuple-element.39), channel_id=1, source_target_pairs={{0,4},{4,0},{8,12},{12,8},{16,20},{20,16},{24,28},{28,24},{32,36},... | collective-permute-start | bytes 1769480 | tf_op jit(solution)/shard_map/ppermute | solution.py:20
  67.6 5.7 %collective-permute-start.11 = (f32[384]{0:T(512)S(1)}, f32[384]{0:T(512)S(1)}, u32[]{:S(2)}, u32[]{:S(2)}) collective-permute-start(f32[384]{0:T(512)S(1)} %log_add_fusion.4), channel_id=1, source_target_pairs={{0,1},{1,2},{2,3},{3,0},{4,5},{5,6},{6,7},{7,4},{8,9},{9,10},{10,1... | collective-permute-start | bytes 4616 | tf_op jit(solution)/shard_map/ppermute | solution.py:61
  69.2 5.1 %collective-permute-start.12 = (f32[384]{0:T(512)S(1)}, f32[384]{0:T(512)S(1)}, u32[]{:S(2)}, u32[]{:S(2)}) collective-permute-start(f32[384]{0:T(512)S(1)} %log_add_fusion.4), channel_id=1, source_target_pairs={{0,2},{1,3},{2,0},{3,1},{4,6},{5,7},{6,4},{7,5},{8,10},{9,11},{10,... | collective-permute-start | bytes 4616 | tf_op jit(solution)/shard_map/ppermute | solution.py:61
  71.9 3.6 %collective-permute-start.13 = (f32[384]{0:T(512)S(1)}, f32[384]{0:T(512)S(1)}, u32[]{:S(2)}, u32[]{:S(2)}) collective-permute-start(f32[384]{0:T(512)S(1)} %log_add_fusion.4), channel_id=1, source_target_pairs={{0,3},{1,0},{2,1},{3,2},{4,7},{5,4},{6,5},{7,6},{8,11},{9,8},{10,9... | collective-permute-start | bytes 4616 | tf_op jit(solution)/shard_map/ppermute | solution.py:61
  87.4 4.9 %collective-permute-start.14 = (f32[384]{0:T(512)S(1)}, f32[384]{0:T(512)S(1)}, u32[]{:S(2)}, u32[]{:S(2)}) collective-permute-start(f32[384]{0:T(512)S(1)} %log_add_fusion.2), channel_id=1, source_target_pairs={{0,1},{1,2},{2,3},{3,0},{4,5},{5,6},{6,7},{7,4},{8,9},{9,10},{10,1... | collective-permute-start | bytes 4616 | tf_op jit(solution)/shard_map/ppermute | solution.py:61
  87.7 5.4 %collective-permute-start.15 = (f32[384]{0:T(512)S(1)}, f32[384]{0:T(512)S(1)}, u32[]{:S(2)}, u32[]{:S(2)}) collective-permute-start(f32[384]{0:T(512)S(1)} %log_add_fusion.2), channel_id=1, source_target_pairs={{0,2},{1,3},{2,0},{3,1},{4,6},{5,7},{6,4},{7,5},{8,10},{9,11},{10,... | collective-permute-start | bytes 4616 | tf_op jit(solution)/shard_map/ppermute | solution.py:61
  91.5 3.6 %collective-permute-start.16 = (f32[384]{0:T(512)S(1)}, f32[384]{0:T(512)S(1)}, u32[]{:S(2)}, u32[]{:S(2)}) collective-permute-start(f32[384]{0:T(512)S(1)} %log_add_fusion.2), channel_id=1, source_target_pairs={{0,3},{1,0},{2,1},{3,2},{4,7},{5,4},{6,5},{7,6},{8,11},{9,8},{10,9... | collective-permute-start | bytes 4616 | tf_op jit(solution)/shard_map/ppermute | solution.py:61
  106.9 4.9 %collective-permute-start.17 = (f32[384]{0:T(512)S(1)}, f32[384]{0:T(512)S(1)}, u32[]{:S(2)}, u32[]{:S(2)}) collective-permute-start(f32[384]{0:T(512)S(1)} %log_add_fusion), channel_id=1, source_target_pairs={{0,1},{1,2},{2,3},{3,0},{4,5},{5,6},{6,7},{7,4},{8,9},{9,10},{10,1... | collective-permute-start | bytes 4616 | tf_op jit(solution)/shard_map/ppermute | solution.py:61
  107.0 5.2 %collective-permute-start.18 = (f32[384]{0:T(512)S(1)}, f32[384]{0:T(512)S(1)}, u32[]{:S(2)}, u32[]{:S(2)}) collective-permute-start(f32[384]{0:T(512)S(1)} %log_add_fusion), channel_id=1, source_target_pairs={{0,2},{1,3},{2,0},{3,1},{4,6},{5,7},{6,4},{7,5},{8,10},{9,11},{10,... | collective-permute-start | bytes 4616 | tf_op jit(solution)/shard_map/ppermute | solution.py:61
  109.7 3.6 %collective-permute-start.19 = (f32[384]{0:T(512)S(1)}, f32[384]{0:T(512)S(1)}, u32[]{:S(2)}, u32[]{:S(2)}) collective-permute-start(f32[384]{0:T(512)S(1)} %log_add_fusion), channel_id=1, source_target_pairs={{0,3},{1,0},{2,1},{3,2},{4,7},{5,4},{6,5},{7,6},{8,11},{9,8},{10,9... | collective-permute-start | bytes 4616 | tf_op jit(solution)/shard_map/ppermute | solution.py:61
  113.6 1.7 collective-permute-start.20
  119.0 13.3 %collective-permute-start.22 = (bf16[4,192,512]{2,1,0:T(8,128)(2,1)S(1)}, bf16[4,192,512]{2,1,0:T(8,128)(2,1)S(1)}, u32[]{:S(2)}, u32[]{:S(2)}) collective-permute-start(bf16[4,192,512]{2,1,0:T(8,128)(2,1)S(1)} %get-tuple-element.50), channel_id=1, source_target_pairs={{0,32},{4,12},{8,40},{12,20},{16,48},{20,28},{24,56},{28,4},{32,64... | collective-permute-start | bytes 2359304 | tf_op jit(solution)/shard_map/ppermute | solution.py:31
  119.6 12.9 %collective-permute-start.25 = (bf16[4,192,512]{2,1,0:T(8,128)(2,1)S(1)}, bf16[4,192,512]{2,1,0:T(8,128)(2,1)S(1)}, u32[]{:S(2)}, u32[]{:S(2)}) collective-permute-start(bf16[4,192,512]{2,1,0:T(8,128)(2,1)S(1)} %get-tuple-element.54), channel_id=1, source_target_pairs={{0,96},{4,28},{8,104},{12,4},{16,112},{20,12},{24,120},{28,20},{32... | collective-permute-start | bytes 2359304 | tf_op jit(solution)/shard_map/ppermute | solution.py:31
  127.7 12.5 %collective-permute-start.21 = (bf16[4,192,512]{2,1,0:T(8,128)(2,1)S(1)}, bf16[4,192,512]{2,1,0:T(8,128)(2,1)S(1)}, u32[]{:S(2)}, u32[]{:S(2)}) collective-permute-start(bf16[4,192,512]{2,1,0:T(8,128)(2,1)S(1)} %get-tuple-element.48), channel_id=1, source_target_pairs={{0,96},{4,28},{8,104},{12,4},{16,112},{20,12},{24,120},{28,20},{32... | collective-permute-start | bytes 2359304 | tf_op jit(solution)/shard_map/ppermute | solution.py:31
  127.8 22.2 %collective-permute-start.24 = (bf16[4,192,512]{2,1,0:T(8,128)(2,1)S(1)}, bf16[4,192,512]{2,1,0:T(8,128)(2,1)S(1)}, u32[]{:S(2)}, u32[]{:S(2)}) collective-permute-start(bf16[4,192,512]{2,1,0:T(8,128)(2,1)S(1)} %get-tuple-element.52), channel_id=1, source_target_pairs={{0,32},{4,12},{8,40},{12,20},{16,48},{20,28},{24,56},{28,4},{32,64... | collective-permute-start | bytes 2359304 | tf_op jit(solution)/shard_map/ppermute | solution.py:31
  132.4 17.3 %collective-permute-start.23 = (bf16[4,192,512]{2,1,0:T(8,128)(2,1)S(1)}, bf16[4,192,512]{2,1,0:T(8,128)(2,1)S(1)}, u32[]{:S(2)}, u32[]{:S(2)}) collective-permute-start(bf16[4,192,512]{2,1,0:T(8,128)(2,1)S(1)} %add_convert_fusion.1), channel_id=1, source_target_pairs={{0,32},{4,12},{8,40},{12,20},{16,48},{20,28},{24,56},{28,4},{32,64... | collective-permute-start | bytes 2359304 | tf_op jit(solution)/shard_map/ppermute | solution.py:31
  132.8 17.2 %collective-permute-start.26 = (bf16[4,192,512]{2,1,0:T(8,128)(2,1)S(1)}, bf16[4,192,512]{2,1,0:T(8,128)(2,1)S(1)}, u32[]{:S(2)}, u32[]{:S(2)}) collective-permute-start(bf16[4,192,512]{2,1,0:T(8,128)(2,1)S(1)} %add_convert_fusion), channel_id=1, source_target_pairs={{0,96},{4,28},{8,104},{12,4},{16,112},{20,12},{24,120},{28,20},{32... | collective-permute-start | bytes 2359304 | tf_op jit(solution)/shard_map/ppermute | solution.py:31
  140.2 10.1 %copy-start.1 = (bf16[4,192,512]{2,1,0:T(8,128)(2,1)}, bf16[4,192,512]{2,1,0:T(8,128)(2,1)S(1)}, u32[]{:S(2)}) copy-start(bf16[4,192,512]{2,1,0:T(8,128)(2,1)S(1)} %collective-permute-done.21) | copy-start | bytes 2359300
  150.7 17.2 %collective-permute-start.27 = (bf16[384,512]{1,0:T(8,128)(2,1)S(1)}, bf16[384,512]{1,0:T(8,128)(2,1)S(1)}, u32[]{:S(2)}, u32[]{:S(2)}) collective-permute-start(bf16[384,512]{1,0:T(8,128)(2,1)S(1)} %pad_maximum_fusion.2), channel_id=1, source_target_pairs={{0,16},{4,68},{8,24},{12,76},{16,0},{20,84},{24,8},{28,92},{32,48}... | collective-permute-start | bytes 1179656 | tf_op jit(solution)/shard_map/ppermute | solution.py:31
  151.9 16.1 %collective-permute-start.28 = (bf16[384,512]{1,0:T(8,128)(2,1)S(1)}, bf16[384,512]{1,0:T(8,128)(2,1)S(1)}, u32[]{:S(2)}, u32[]{:S(2)}) collective-permute-start(bf16[384,512]{1,0:T(8,128)(2,1)S(1)} %pad_maximum_fusion.3), channel_id=1, source_target_pairs={{0,8},{4,36},{8,16},{12,44},{16,24},{20,52},{24,0},{28,60},{32,40}... | collective-permute-start | bytes 1179656 | tf_op jit(solution)/shard_map/ppermute | solution.py:31
  152.8 15.1 %collective-permute-start.29 = (bf16[384,512]{1,0:T(8,128)(2,1)S(1)}, bf16[384,512]{1,0:T(8,128)(2,1)}, u32[]{:S(2)}, u32[]{:S(2)}) collective-permute-start(bf16[384,512]{1,0:T(8,128)(2,1)S(1)} %pad_maximum_fusion.4), channel_id=1, source_target_pairs={{0,24},{4,100},{8,0},{12,108},{16,8},{20,116},{24,16},{28,124},{32... | collective-permute-start | bytes 1179656 | tf_op jit(solution)/shard_map/ppermute | solution.py:31
  (1 other events, 0.9 us)

commit v6 on v5

--- a/solution.py
+++ b/solution.py
@@ -10,6 +10,7 @@
 SIDE = 4
 OFFS = (2, 1, 3)
 BLOCKS = SIDE * SIDE
+EXTRA = 16
 VMEM_LIMIT = 24 * 1024 * 1024
 
 SPOTS = [(k, m) for k in (0, 1, 3, 2) for m in OFFS + (0,)]
@@ -199,7 +200,7 @@
     groups = len(start)
 
     def kernel(ids_ref, w_own_ref, w_oth_ref, data_ref, data_other_ref, *refs):
-        outs, (weights, held, totals, in_sems, sems) = (
+        outs, (weights, held, tops, bottoms, in_sems, sems) = (
             refs[: 2 * groups],
             refs[2 * groups :],
         )
@@ -220,8 +221,18 @@
                     copy.start()
         weights[:, :inner] = w_own_ref[...]
         weights[:, inner:] = w_oth_ref[...]
+        ones = jnp.ones((EXTRA, 2 * inner), dtype)
+        row_sums = lax.dot_general(
+            ones,
+            weights[...],
+            (((1,), (1,)), ((), ())),
+            preferred_element_type=jnp.float32,
+        ).astype(dtype)
         out = []
         for a in range(groups):
+            for i in range(n):
+                tops[a, i, half:, :rows] = row_sums
+                tops[a, i, half:, rows:] = jnp.zeros((EXTRA, block - rows), dtype)
             for i in range(0, n, step):
                 spot = a * n + i
                 for copies in into[spot : spot + step]:
@@ -234,10 +245,13 @@
                 ).astype(dtype)
                 for j in range(step):
                     part = total[:, j * block : (j + 1) * block]
-                    totals[2 * a, i + j] = part[:half]
-                    totals[2 * a + 1, i + j] = part[half:]
-            for p in range(2 * a, 2 * a + 2):
-                out.append(pltpu.make_async_copy(totals.at[p], outs[p], sems.at[p]))
+                    tops[a, i + j, :half] = part[:half]
+                    bottoms[a, i + j] = part[half:]
+            for p, held_part in enumerate((tops, bottoms)):
+                to = 2 * a + p
+                out.append(
+                    pltpu.make_async_copy(held_part.at[a], outs[to], sems.at[to])
+                )
                 out[-1].start()
         for copy in out:
             copy.wait()
@@ -246,12 +260,17 @@
         kernel,
         [ids, w_own, w_oth] + in_hbm([data, data_other]),
         [IN_SMEM, IN_VMEM, IN_VMEM, ANYWHERE, ANYWHERE],
-        [jax.ShapeDtypeStruct((n, half, block), dtype)] * (2 * groups),
+        [
+            jax.ShapeDtypeStruct((n, half + EXTRA, block), dtype),
+            jax.ShapeDtypeStruct((n, half, block), dtype),
+        ]
+        * groups,
         [ANYWHERE] * (2 * groups),
         [
             pltpu.VMEM((rows, 2 * inner), dtype),
             pltpu.VMEM((2 * inner, groups * n * block), dtype),
-            pltpu.VMEM((2 * groups, n, half, block), dtype),
+            pltpu.VMEM((groups, n, half + EXTRA, block), dtype),
+            pltpu.VMEM((groups, n, half, block), dtype),
             pltpu.SemaphoreType.DMA((2, groups * n)),
             pltpu.SemaphoreType.DMA((2 * groups,)),
         ],
@@ -267,7 +286,7 @@
     return total
 
 
-def scattered_sums(ins, ids, row_part):
+def scattered_sums(ins, ids):
     top, bottom = part_sums([12], 4, ins, ids)
     weights, top, bottom = lax.optimization_barrier((ins[0], top, bottom))
     ins = (weights,) + ins[1:]
@@ -288,15 +307,17 @@
             added(near_bottom[a], [got[a] for got in bottoms]),
         ]
         totals.append(jnp.concatenate(total).astype(top.dtype))
-    row_part, *totals = lax.optimization_barrier((row_part, *totals))
-    sums = [hop(total, k, True) for total, k in zip(totals, OFFS)]
-    row_sum = jnp.sum(to_all_dp(row_part), axis=0)
-    row_sum, near_top = lax.optimization_barrier((row_sum, near_top))
+    last = [hop(total, k, True) for total, k in zip(totals, OFFS)]
     total = [
         added(near_top[3], [got[3] for got in tops]),
         added(near_bottom[3], [got[3] for got in bottoms]),
     ]
-    return added(jnp.concatenate(total), sums), row_sum
+    total = added(jnp.concatenate(total), last)
+    rows = total.shape[0] - EXTRA
+    half = rows // 2
+    row_sums = total[half, :rows]
+    means = jnp.concatenate([total[:half], total[half + EXTRA :]])
+    return means / row_sums[:, None]
 
 
 def body(noise_latents, data_latents):
@@ -331,12 +352,10 @@
         g = sy - lse(to_all_noise(local), 0)
     coupling = jnp.exp(twice + (f - sx)[:, None] + (g - sy)[None, :])
     weights = coupling.astype(jnp.bfloat16)
-    total, row_sum = scattered_sums(
-        (weights, swap(weights), data_latents, data_other),
-        ids,
-        jnp.sum(coupling, axis=1),
-    )
-    return (total / row_sum[:, None]).astype(jnp.bfloat16)
+    means = scattered_sums(
+        (weights, swap(weights), data_latents, data_other), ids
+    )
+    return means.astype(jnp.bfloat16)
 
 
 def solution(mesh):

time: 171 us -> 167 us (0.977)
  waiting for transfers between devices: 37.9 us -> 49.9 us
  blocking collectives: 44.8 us -> 33.4 us
  starting transfers between devices: 42.6 us -> 40.4 us
  other arithmetic: 16 us -> 14 us
    ppermute x18, waiting for transfers between devices: 26.7 us -> 38.7 us  [hop(): return lax.ppermute(values, 'dp', pairs)]
    all_to_all x4 -> x3, blocking collectives: 44.8 us -> 33.4 us  [to_all_dp(): lax.all_to_all(jnp.broadcast_to(values[None], (n,) + values.shape), 'dp',...]
    ppermute x18, starting transfers between devices: 28.1 us -> 25.9 us  [hop(): return lax.ppermute(values, 'dp', pairs)]
  transfers between devices with their start and end apart: 30 -> 30, of which waited for: 18 -> 22; matrix products, arithmetic and copies ran while one was open for 6% -> 6% of each run, Pallas kernels for 13% -> 13%
where the time goes in v6:
time: 167 us
  waiting for transfers between devices  49.9 us (30%)
  starting transfers between devices  40.4 us (24%)
  blocking collectives  33.4 us (20%)
  Pallas kernels  28.3 us (17%)
  other arithmetic  14 us (8%)
    ppermute x18, waiting for transfers between devices, hop(): return lax.ppermute(values, 'dp', pairs)  38.7 us
    all_to_all x3, blocking collectives, to_all_dp(): lax.all_to_all(jnp.broadcast_to(values[None], (n,) + values.shape), 'dp',...  33.4 us
    pallas_call x7, Pallas kernels, call(): pl.pallas_call(kernel, in_specs=in_specs, out_specs=out_specs, out_shape=...  28.3 us
    ppermute x18, starting transfers between devices, hop(): return lax.ppermute(values, 'dp', pairs)  25.9 us
    ppermute x9, starting transfers between devices, to_all_noise(): lax.ppermute(values, 'noise', [(i, (i + k) % n) for i in range(n)])  14.2 us
    ppermute x9, waiting for transfers between devices, to_all_noise(): lax.ppermute(values, 'noise', [(i, (i + k) % n) for i in range(n)])  7.81 us
    reduce_sum x1, other arithmetic, body(): sq_data = jnp.sum(data_f * data_f, axis=1)  7.14 us
    ppermute x3, waiting for transfers between devices, swap(): return lax.ppermute(values, 'dp', [(i, i ^ 1) for i in range(n)])  3.39 us
  transfers between devices with their start and end apart: 30, of which 22 were waited for; matrix products, arithmetic and copies ran while one was open for 6% of the time, Pallas kernels for 13%

profile of v6, /device:TPU:0, one launch (start us, length us, event | category | flops | bytes accessed | tf_op | source)
XLA Modules:
  0.0 166.8 jit_solution(10991190680957545673)
XLA Ops:
  0.0 4.0 %collective-permute-start = (bf16[384,512]{1,0:T(8,128)(2,1)}, bf16[384,512]{1,0:T(8,128)(2,1)S(1)}, u32[]{:S(2)}, u32[]{:S(2)}) collective-permute-start(bf16[384,512]{1,0:T(8,128)(2,1)} %param.2), channel_id=1, source_target_pairs={{0,16},{4,68},{8,24},{12,76},{16,0},{20,84},{24,8},{28,92},{32,48}... | collective-permute-start | bytes 1179656 | tf_op jit(solution)/shard_map/ppermute | solution.py:32
  6.1 7.1 %multiply_reduce_fusion = f32[384]{0:T(512)S(1)} fusion(bf16[384,16384]{1,0:T(8,128)(2,1)} %data_ref.7), kind=kLoop, calls=%fused_computation | loop fusion | flops 18873984 | bytes 12584448 | tf_op jit(solution)/shard_map/reduce_sum | solution.py:335
  13.3 2.0 %collective-permute-done.1 = bf16[384,512]{1,0:T(8,128)(2,1)S(1)} collective-permute-done((bf16[384,512]{1,0:T(8,128)(2,1)}, bf16[384,512]{1,0:T(8,128)(2,1)S(1)}, u32[]{:S(2)}, u32[]{:S(2)}) %collective-permute-start.1) | collective-permute-done | bytes 393248 | tf_op jit(solution)/shard_map/ppermute | solution.py:32
  16.8 3.0 %collective-permute-start.3 = (bf16[4,192,512]{2,1,0:T(8,128)(2,1)}, bf16[4,192,512]{2,1,0:T(8,128)(2,1)S(1)}, u32[]{:S(2)}, u32[]{:S(2)}) collective-permute-start(bf16[4,192,512]{2,1,0:T(8,128)(2,1)} %get-tuple-element.27), channel_id=1, source_target_pairs={{0,96},{4,28},{8,104},{12,4},{16,112},{20,12},{24,120},{28,20},{32... | collective-permute-start | bytes 2359304 | tf_op jit(solution)/shard_map/ppermute | solution.py:32
  19.8 3.2 %collective-permute-start.8 = (bf16[4,192,512]{2,1,0:T(8,128)(2,1)}, bf16[4,192,512]{2,1,0:T(8,128)(2,1)}, u32[]{:S(2)}, u32[]{:S(2)}) collective-permute-start(bf16[4,192,512]{2,1,0:T(8,128)(2,1)} %get-tuple-element.28), channel_id=1, source_target_pairs={{0,96},{4,28},{8,104},{12,4},{16,112},{20,12},{24,120},{28,20},{32... | collective-permute-start | bytes 2359304 | tf_op jit(solution)/shard_map/ppermute | solution.py:32
  23.1 5.6 %shard_map.28.refs_4_.refs_2_ = bf16[768,8192]{1,0:T(8,128)(2,1)S(1)} custom-call(s32[16]{0:T(128)S(1)} %stack.143.ids_ref, bf16[384,16384]{1,0:T(8,128)(2,1)} %data_ref.7, bf16[384,16384]{1,0:T(8,128)(2,1)} %collective-permute-done.5.data_other_ref), custom_call_target="tpu_custom_call" | custom-call | bytes 25165824 | tf_op jit(solution)/shard_map/pallas_call | solution.py:68
  30.2 3.0 %collective-permute-done.4.refs_3_ = bf16[4,192,512]{2,1,0:T(8,128)(2,1)S(1)} collective-permute-done((bf16[4,192,512]{2,1,0:T(8,128)(2,1)}, bf16[4,192,512]{2,1,0:T(8,128)(2,1)S(1)}, u32[]{:S(2)}, u32[]{:S(2)}) %collective-permute-start.4) | collective-permute-done | bytes 786464 | tf_op jit(solution)/shard_map/ppermute | solution.py:32
  35.2 2.8 %collective-permute-done.8.refs_1_ = bf16[4,192,512]{2,1,0:T(8,128)(2,1)} collective-permute-done((bf16[4,192,512]{2,1,0:T(8,128)(2,1)}, bf16[4,192,512]{2,1,0:T(8,128)(2,1)}, u32[]{:S(2)}, u32[]{:S(2)}) %collective-permute-start.8) | collective-permute-done | bytes 786464 | tf_op jit(solution)/shard_map/ppermute | solution.py:32
  38.0 3.7 %collective-permute-done.9.refs_2_ = bf16[4,192,512]{2,1,0:T(8,128)(2,1)} collective-permute-done((bf16[4,192,512]{2,1,0:T(8,128)(2,1)}, bf16[4,192,512]{2,1,0:T(8,128)(2,1)}, u32[]{:S(2)}, u32[]{:S(2)}) %collective-permute-start.9) | collective-permute-done | bytes 786464 | tf_op jit(solution)/shard_map/ppermute | solution.py:32
  41.7 5.6 %shard_map.30.refs_3_ = f32[384,768]{1,0:T(8,128)S(1)} custom-call(bf16[4,192,512]{2,1,0:T(8,128)(2,1)S(1)} %collective-permute-done.3.refs_0_, bf16[4,192,512]{2,1,0:T(8,128)(2,1)} %collective-permute-done.8.refs_1_, bf16[4,192,512]{2,1,0:T(8,128)(2,1)} %collective-permute-done.9.refs_2_, bf16[4,192,512]{2,1,0:T(8,128)(2,1)S(1)} %collective-permute-done.4.refs_3_, ...), custom_call_target="tpu_custom_call" | custom-call | flops 2415919104 | bytes 9437184 | tf_op jit(solution)/shard_map/pallas_call | solution.py:68
  47.3 2.7 %collective-permute-done.7.refs_1_ = bf16[4,192,512]{2,1,0:T(8,128)(2,1)S(1)} collective-permute-done((bf16[4,192,512]{2,1,0:T(8,128)(2,1)S(1)}, bf16[4,192,512]{2,1,0:T(8,128)(2,1)S(1)}, u32[]{:S(2)}, u32[]{:S(2)}) %collective-permute-start.7) | collective-permute-done | bytes 786464 | tf_op jit(solution)/shard_map/ppermute | solution.py:32
  50.0 2.2 %shard_map.31 = (f32[384,384]{1,0:T(8,128)S(1)}, f32[384,384]{1,0:T(8,128)S(1)}) custom-call(bf16[4,192,512]{2,1,0:T(8,128)(2,1)S(1)} %collective-permute-done.6.refs_0_, bf16[4,192,512]{2,1,0:T(8,128)(2,1)S(1)} %collective-permute-done.7.refs_1_, bf16[768,8192]{1,0:T(8,128)(2,1)S(1)} %shard_map.28.refs_4_.refs_2_, f32[384,768]{1,0:T(8,128)S(1)} %shard_map.30.refs_3_), custom_call_target="tpu_custom_call" | custom-call | flops 1207959552 | bytes 4718592 | tf_op jit(solution)/shard_map/pallas_call | solution.py:68
  52.7 1.8 %collective-permute-done.10 = f32[384,384]{1,0:T(8,128)S(1)} collective-permute-done((f32[384,384]{1,0:T(8,128)S(1)}, f32[384,384]{1,0:T(8,128)S(1)}, u32[]{:S(2)}, u32[]{:S(2)}) %collective-permute-start.10) | collective-permute-done | bytes 589856 | tf_op jit(solution)/shard_map/ppermute | solution.py:21
  55.0 11.7 %all_to_all.23 = f32[32,2,384]{2,1,0:T(2,128)S(1)} all-to-all(f32[32,2,384]{2,1,0:T(2,128)S(1)} %broadcast_in_dim.21), channel_id=1, replica_groups=mesh['dp'=32,'noise'=4] {'dp'}, dimensions={0} | all-to-all | bytes 196608 | tf_op jit(solution)/shard_map/all_to_all | solution.py:52
  68.8 2.7 %collective-permute-start.12 = (f32[384]{0:T(512)S(1)}, f32[384]{0:T(512)S(1)}, u32[]{:S(2)}, u32[]{:S(2)}) collective-permute-start(f32[384]{0:T(512)S(1)} %log_add_fusion.4), channel_id=1, source_target_pairs={{0,2},{1,3},{2,0},{3,1},{4,6},{5,7},{6,4},{7,5},{8,10},{9,11},{10,... | collective-permute-start | bytes 4616 | tf_op jit(solution)/shard_map/ppermute | solution.py:62
  75.6 10.9 %all_to_all.24 = f32[32,1,384]{2,1,0:T(1,128)S(1)} all-to-all(f32[32,1,384]{2,1,0:T(1,128)S(1)} %broadcast_in_dim.22), channel_id=1, replica_groups=mesh['dp'=32,'noise'=4] {'dp'}, dimensions={0} | all-to-all | bytes 98304 | tf_op jit(solution)/shard_map/all_to_all | solution.py:52
  87.3 3.8 %collective-permute-start.15 = (f32[384]{0:T(512)S(1)}, f32[384]{0:T(512)S(1)}, u32[]{:S(2)}, u32[]{:S(2)}) collective-permute-start(f32[384]{0:T(512)S(1)} %log_add_fusion.2), channel_id=1, source_target_pairs={{0,2},{1,3},{2,0},{3,1},{4,6},{5,7},{6,4},{7,5},{8,10},{9,11},{10,... | collective-permute-start | bytes 4616 | tf_op jit(solution)/shard_map/ppermute | solution.py:62
  92.7 2.0 %collective-permute-done.16 = f32[384]{0:T(512)S(1)} collective-permute-done((f32[384]{0:T(512)S(1)}, f32[384]{0:T(512)S(1)}, u32[]{:S(2)}, u32[]{:S(2)}) %collective-permute-start.16) | collective-permute-done | bytes 1568 | tf_op jit(solution)/shard_map/ppermute | solution.py:62
  95.2 10.8 %all_to_all.25 = f32[32,1,384]{2,1,0:T(1,128)S(1)} all-to-all(f32[32,1,384]{2,1,0:T(1,128)S(1)} %broadcast_in_dim.23), channel_id=1, replica_groups=mesh['dp'=32,'noise'=4] {'dp'}, dimensions={0} | all-to-all | bytes 98304 | tf_op jit(solution)/shard_map/all_to_all | solution.py:52
  106.6 2.7 %collective-permute-start.18 = (f32[384]{0:T(512)S(1)}, f32[384]{0:T(512)S(1)}, u32[]{:S(2)}, u32[]{:S(2)}) collective-permute-start(f32[384]{0:T(512)S(1)} %log_add_fusion), channel_id=1, source_target_pairs={{0,2},{1,3},{2,0},{3,1},{4,6},{5,7},{6,4},{7,5},{8,10},{9,11},{10,... | collective-permute-start | bytes 4616 | tf_op jit(solution)/shard_map/ppermute | solution.py:62
  114.7 3.9 %shard_map.32 = (bf16[4,208,512]{2,1,0:T(8,128)(2,1)S(1)}, bf16[4,192,512]{2,1,0:T(8,128)(2,1)S(1)}) custom-call(s32[16]{0:T(128)S(1)} %stack.143.ids_ref, bf16[384,384]{1,0:T(8,128)(2,1)S(1)} %exponential_convert_fusion.w_own_ref, bf16[384,384]{1,0:T(8,128)(2,1)S(1)} %collective-permute-done.20.w_oth_ref, bf16[384,16384]{1,0:T(8,128)(2,1)} %data_ref.7, ...), custom_call_target="tpu_custom_call" | custom-call | flops 1207959552 | bytes 4718592 | tf_op jit(solution)/shard_map/pallas_call | solution.py:68
  120.7 5.7 %shard_map.33 = (bf16[4,208,512]{2,1,0:T(8,128)(2,1)S(1)}, bf16[4,192,512]{2,1,0:T(8,128)(2,1)S(1)}, bf16[4,208,512]{2,1,0:T(8,128)(2,1)S(1)}, bf16[4,192,512]{2,1,0:T(8,128)(2,1)S(1)}) custom-call(s32[16]{0:T(128)S(1)} %stack.143.ids_ref, bf16[384,384]{1,0:T(8,128)(2,1)S(1)} %exponential_convert_fusion.w_own_ref, ...), custom_call_target="tpu_custom_call" | custom-call | flops 2415919104 | bytes 9437184 | tf_op jit(solution)/shard_map/pallas_call | solution.py:68
  126.5 2.4 %collective-permute-start.21 = (bf16[4,208,512]{2,1,0:T(8,128)(2,1)S(1)}, bf16[4,208,512]{2,1,0:T(8,128)(2,1)S(1)}, u32[]{:S(2)}, u32[]{:S(2)}) collective-permute-start(bf16[4,208,512]{2,1,0:T(8,128)(2,1)S(1)} %get-tuple-element.42), channel_id=1, source_target_pairs={{0,96},{4,28},{8,104},{12,4},{16,112},{20,12},{24,120},{28,20},{32... | collective-permute-start | bytes 2555912 | tf_op jit(solution)/shard_map/ppermute | solution.py:32
  128.9 1.8 %collective-permute-done.25 = bf16[4,192,512]{2,1,0:T(8,128)(2,1)S(1)} collective-permute-done((bf16[4,192,512]{2,1,0:T(8,128)(2,1)S(1)}, bf16[4,192,512]{2,1,0:T(8,128)(2,1)S(1)}, u32[]{:S(2)}, u32[]{:S(2)}) %collective-permute-start.25) | collective-permute-done | bytes 786464 | tf_op jit(solution)/shard_map/ppermute | solution.py:32
  130.9 2.4 %collective-permute-start.26 = (bf16[4,192,512]{2,1,0:T(8,128)(2,1)S(1)}, bf16[4,192,512]{2,1,0:T(8,128)(2,1)S(1)}, u32[]{:S(2)}, u32[]{:S(2)}) collective-permute-start(bf16[4,192,512]{2,1,0:T(8,128)(2,1)S(1)} %add_convert_fusion.1), channel_id=1, source_target_pairs={{0,96},{4,28},{8,104},{12,4},{16,112},{20,12},{24,120},{28,20},{32... | collective-permute-start | bytes 2359304 | tf_op jit(solution)/shard_map/ppermute | solution.py:32
  134.1 3.9 %shard_map.34 = (bf16[4,208,512]{2,1,0:T(8,128)(2,1)S(1)}, bf16[4,192,512]{2,1,0:T(8,128)(2,1)S(1)}) custom-call(s32[16]{0:T(128)S(1)} %stack.143.ids_ref, bf16[384,384]{1,0:T(8,128)(2,1)S(1)} %exponential_convert_fusion.w_own_ref, bf16[384,384]{1,0:T(8,128)(2,1)S(1)} %collective-permute-done.20.w_oth_ref, bf16[384,16384]{1,0:T(8,128)(2,1)} %data_ref.7, ...), custom_call_target="tpu_custom_call" | custom-call | flops 1207959552 | bytes 4718592 | tf_op jit(solution)/shard_map/pallas_call | solution.py:68
  138.0 4.2 %collective-permute-done.24 = bf16[4,192,512]{2,1,0:T(8,128)(2,1)S(1)} collective-permute-done((bf16[4,192,512]{2,1,0:T(8,128)(2,1)S(1)}, bf16[4,192,512]{2,1,0:T(8,128)(2,1)S(1)}, u32[]{:S(2)}, u32[]{:S(2)}) %collective-permute-start.24) | collective-permute-done | bytes 786464 | tf_op jit(solution)/shard_map/ppermute | solution.py:32
  142.2 6.1 %collective-permute-done.26 = bf16[4,192,512]{2,1,0:T(8,128)(2,1)S(1)} collective-permute-done((bf16[4,192,512]{2,1,0:T(8,128)(2,1)S(1)}, bf16[4,192,512]{2,1,0:T(8,128)(2,1)S(1)}, u32[]{:S(2)}, u32[]{:S(2)}) %collective-permute-start.26) | collective-permute-done | bytes 786464 | tf_op jit(solution)/shard_map/ppermute | solution.py:32
  148.6 2.7 %collective-permute-done.23 = bf16[4,208,512]{2,1,0:T(8,128)(2,1)S(1)} collective-permute-done((bf16[4,208,512]{2,1,0:T(8,128)(2,1)S(1)}, bf16[4,208,512]{2,1,0:T(8,128)(2,1)S(1)}, u32[]{:S(2)}, u32[]{:S(2)}) %collective-permute-start.23) | collective-permute-done | bytes 852000 | tf_op jit(solution)/shard_map/ppermute | solution.py:32
  153.9 2.4 %collective-permute-start.29 = (bf16[400,512]{1,0:T(8,128)(2,1)S(1)}, bf16[400,512]{1,0:T(8,128)(2,1)S(1)}, u32[]{:S(2)}, u32[]{:S(2)}) collective-permute-start(bf16[400,512]{1,0:T(8,128)(2,1)S(1)} %pad_maximum_fusion.4), channel_id=1, source_target_pairs={{0,24},{4,100},{8,0},{12,108},{16,8},{20,116},{24,16},{28,124},{32... | collective-permute-start | bytes 1228808 | tf_op jit(solution)/shard_map/ppermute | solution.py:32
  156.3 5.0 %collective-permute-done.27 = bf16[400,512]{1,0:T(8,128)(2,1)S(1)} collective-permute-done((bf16[400,512]{1,0:T(8,128)(2,1)S(1)}, bf16[400,512]{1,0:T(8,128)(2,1)S(1)}, u32[]{:S(2)}, u32[]{:S(2)}) %collective-permute-start.27) | collective-permute-done | bytes 409632 | tf_op jit(solution)/shard_map/ppermute | solution.py:32
  161.3 4.3 %collective-permute-done.28 = bf16[400,512]{1,0:T(8,128)(2,1)S(1)} collective-permute-done((bf16[400,512]{1,0:T(8,128)(2,1)S(1)}, bf16[400,512]{1,0:T(8,128)(2,1)S(1)}, u32[]{:S(2)}, u32[]{:S(2)}) %collective-permute-start.28) | collective-permute-done | bytes 409632 | tf_op jit(solution)/shard_map/ppermute | solution.py:32
  (115 shorter events, 30.2 us)
Async XLA Ops:
  0.0 13.2 %copy-start = (bf16[384,512]{1,0:T(8,128)(2,1)S(1)}, bf16[384,512]{1,0:T(8,128)(2,1)}, u32[]{:S(2)}) copy-start(bf16[384,512]{1,0:T(8,128)(2,1)} %param.2) | copy-start | bytes 1179652
  0.0 23.1 %collective-permute-start.5 = (bf16[384,16384]{1,0:T(8,128)(2,1)}, bf16[384,16384]{1,0:T(8,128)(2,1)}, u32[]{:S(2)}, u32[]{:S(2)}) collective-permute-start(bf16[384,16384]{1,0:T(8,128)(2,1)} %data_ref.7), channel_id=1, source_target_pairs={{0,4},{4,0},{8,12},{12,8},{16,20},{20,16},{24,28},{28,24},{32,36},... | collective-permute-start | bytes 37748744 | tf_op jit(solution)/shard_map/ppermute | solution.py:21
  0.0 13.2 %collective-permute-start = (bf16[384,512]{1,0:T(8,128)(2,1)}, bf16[384,512]{1,0:T(8,128)(2,1)S(1)}, u32[]{:S(2)}, u32[]{:S(2)}) collective-permute-start(bf16[384,512]{1,0:T(8,128)(2,1)} %param.2), channel_id=1, source_target_pairs={{0,16},{4,68},{8,24},{12,76},{16,0},{20,84},{24,8},{28,92},{32,48}... | collective-permute-start | bytes 1179656 | tf_op jit(solution)/shard_map/ppermute | solution.py:32
  4.0 11.2 %collective-permute-start.1 = (bf16[384,512]{1,0:T(8,128)(2,1)}, bf16[384,512]{1,0:T(8,128)(2,1)S(1)}, u32[]{:S(2)}, u32[]{:S(2)}) collective-permute-start(bf16[384,512]{1,0:T(8,128)(2,1)} %param.2), channel_id=1, source_target_pairs={{0,24},{4,100},{8,0},{12,108},{16,8},{20,116},{24,16},{28,124},{32... | collective-permute-start | bytes 1179656 | tf_op jit(solution)/shard_map/ppermute | solution.py:32
  4.8 10.6 %collective-permute-start.2 = (bf16[384,512]{1,0:T(8,128)(2,1)}, bf16[384,512]{1,0:T(8,128)(2,1)S(1)}, u32[]{:S(2)}, u32[]{:S(2)}) collective-permute-start(bf16[384,512]{1,0:T(8,128)(2,1)} %param.2), channel_id=1, source_target_pairs={{0,8},{4,36},{8,16},{12,44},{16,24},{20,52},{24,0},{28,60},{32,40}... | collective-permute-start | bytes 1179656 | tf_op jit(solution)/shard_map/ppermute | solution.py:32
  16.8 13.4 %collective-permute-start.3 = (bf16[4,192,512]{2,1,0:T(8,128)(2,1)}, bf16[4,192,512]{2,1,0:T(8,128)(2,1)S(1)}, u32[]{:S(2)}, u32[]{:S(2)}) collective-permute-start(bf16[4,192,512]{2,1,0:T(8,128)(2,1)} %get-tuple-element.27), channel_id=1, source_target_pairs={{0,96},{4,28},{8,104},{12,4},{16,112},{20,12},{24,120},{28,20},{32... | collective-permute-start | bytes 2359304 | tf_op jit(solution)/shard_map/ppermute | solution.py:32
  19.8 13.4 %collective-permute-start.4 = (bf16[4,192,512]{2,1,0:T(8,128)(2,1)}, bf16[4,192,512]{2,1,0:T(8,128)(2,1)S(1)}, u32[]{:S(2)}, u32[]{:S(2)}) collective-permute-start(bf16[4,192,512]{2,1,0:T(8,128)(2,1)} %get-tuple-element.28), channel_id=1, source_target_pairs={{0,32},{4,12},{8,40},{12,20},{16,48},{20,28},{24,56},{28,4},{32,64... | collective-permute-start | bytes 2359304 | tf_op jit(solution)/shard_map/ppermute | solution.py:32
  19.8 18.2 %collective-permute-start.8 = (bf16[4,192,512]{2,1,0:T(8,128)(2,1)}, bf16[4,192,512]{2,1,0:T(8,128)(2,1)}, u32[]{:S(2)}, u32[]{:S(2)}) collective-permute-start(bf16[4,192,512]{2,1,0:T(8,128)(2,1)} %get-tuple-element.28), channel_id=1, source_target_pairs={{0,96},{4,28},{8,104},{12,4},{16,112},{20,12},{24,120},{28,20},{32... | collective-permute-start | bytes 2359304 | tf_op jit(solution)/shard_map/ppermute | solution.py:32
  23.0 18.7 %collective-permute-start.9 = (bf16[4,192,512]{2,1,0:T(8,128)(2,1)}, bf16[4,192,512]{2,1,0:T(8,128)(2,1)}, u32[]{:S(2)}, u32[]{:S(2)}) collective-permute-start(bf16[4,192,512]{2,1,0:T(8,128)(2,1)} %get-tuple-element.27), channel_id=1, source_target_pairs={{0,32},{4,12},{8,40},{12,20},{16,48},{20,28},{24,56},{28,4},{32,64... | collective-permute-start | bytes 2359304 | tf_op jit(solution)/shard_map/ppermute | solution.py:32
  33.2 14.1 %collective-permute-start.6 = (bf16[4,192,512]{2,1,0:T(8,128)(2,1)S(1)}, bf16[4,192,512]{2,1,0:T(8,128)(2,1)S(1)}, u32[]{:S(2)}, u32[]{:S(2)}) collective-permute-start(bf16[4,192,512]{2,1,0:T(8,128)(2,1)S(1)} %collective-permute-done.3.refs_0_), channel_id=1, source_target_pairs={{0,96},{4,28},{8,104},{12,4},{16,112},{20,12},{24,120},{28,20},{32... | collective-permute-start | bytes 2359304 | tf_op jit(solution)/shard_map/ppermute | solution.py:32
  33.5 16.5 %collective-permute-start.7 = (bf16[4,192,512]{2,1,0:T(8,128)(2,1)S(1)}, bf16[4,192,512]{2,1,0:T(8,128)(2,1)S(1)}, u32[]{:S(2)}, u32[]{:S(2)}) collective-permute-start(bf16[4,192,512]{2,1,0:T(8,128)(2,1)S(1)} %collective-permute-done.4.refs_3_), channel_id=1, source_target_pairs={{0,32},{4,12},{8,40},{12,20},{16,48},{20,28},{24,56},{28,4},{32,64... | collective-permute-start | bytes 2359304 | tf_op jit(solution)/shard_map/ppermute | solution.py:32
  52.2 2.3 %collective-permute-start.10 = (f32[384,384]{1,0:T(8,128)S(1)}, f32[384,384]{1,0:T(8,128)S(1)}, u32[]{:S(2)}, u32[]{:S(2)}) collective-permute-start(f32[384,384]{1,0:T(8,128)S(1)} %get-tuple-element.33), channel_id=1, source_target_pairs={{0,4},{4,0},{8,12},{12,8},{16,20},{20,16},{24,28},{28,24},{32,36},... | collective-permute-start | bytes 1769480 | tf_op jit(solution)/shard_map/ppermute | solution.py:21
  67.2 5.7 %collective-permute-start.11 = (f32[384]{0:T(512)S(1)}, f32[384]{0:T(512)S(1)}, u32[]{:S(2)}, u32[]{:S(2)}) collective-permute-start(f32[384]{0:T(512)S(1)} %log_add_fusion.4), channel_id=1, source_target_pairs={{0,1},{1,2},{2,3},{3,0},{4,5},{5,6},{6,7},{7,4},{8,9},{9,10},{10,1... | collective-permute-start | bytes 4616 | tf_op jit(solution)/shard_map/ppermute | solution.py:62
  68.8 5.1 %collective-permute-start.12 = (f32[384]{0:T(512)S(1)}, f32[384]{0:T(512)S(1)}, u32[]{:S(2)}, u32[]{:S(2)}) collective-permute-start(f32[384]{0:T(512)S(1)} %log_add_fusion.4), channel_id=1, source_target_pairs={{0,2},{1,3},{2,0},{3,1},{4,6},{5,7},{6,4},{7,5},{8,10},{9,11},{10,... | collective-permute-start | bytes 4616 | tf_op jit(solution)/shard_map/ppermute | solution.py:62
  71.5 3.6 %collective-permute-start.13 = (f32[384]{0:T(512)S(1)}, f32[384]{0:T(512)S(1)}, u32[]{:S(2)}, u32[]{:S(2)}) collective-permute-start(f32[384]{0:T(512)S(1)} %log_add_fusion.4), channel_id=1, source_target_pairs={{0,3},{1,0},{2,1},{3,2},{4,7},{5,4},{6,5},{7,6},{8,11},{9,8},{10,9... | collective-permute-start | bytes 4616 | tf_op jit(solution)/shard_map/ppermute | solution.py:62
  86.9 4.9 %collective-permute-start.14 = (f32[384]{0:T(512)S(1)}, f32[384]{0:T(512)S(1)}, u32[]{:S(2)}, u32[]{:S(2)}) collective-permute-start(f32[384]{0:T(512)S(1)} %log_add_fusion.2), channel_id=1, source_target_pairs={{0,1},{1,2},{2,3},{3,0},{4,5},{5,6},{6,7},{7,4},{8,9},{9,10},{10,1... | collective-permute-start | bytes 4616 | tf_op jit(solution)/shard_map/ppermute | solution.py:62
  87.3 5.4 %collective-permute-start.15 = (f32[384]{0:T(512)S(1)}, f32[384]{0:T(512)S(1)}, u32[]{:S(2)}, u32[]{:S(2)}) collective-permute-start(f32[384]{0:T(512)S(1)} %log_add_fusion.2), channel_id=1, source_target_pairs={{0,2},{1,3},{2,0},{3,1},{4,6},{5,7},{6,4},{7,5},{8,10},{9,11},{10,... | collective-permute-start | bytes 4616 | tf_op jit(solution)/shard_map/ppermute | solution.py:62
  91.1 3.6 %collective-permute-start.16 = (f32[384]{0:T(512)S(1)}, f32[384]{0:T(512)S(1)}, u32[]{:S(2)}, u32[]{:S(2)}) collective-permute-start(f32[384]{0:T(512)S(1)} %log_add_fusion.2), channel_id=1, source_target_pairs={{0,3},{1,0},{2,1},{3,2},{4,7},{5,4},{6,5},{7,6},{8,11},{9,8},{10,9... | collective-permute-start | bytes 4616 | tf_op jit(solution)/shard_map/ppermute | solution.py:62
  106.5 4.9 %collective-permute-start.17 = (f32[384]{0:T(512)S(1)}, f32[384]{0:T(512)S(1)}, u32[]{:S(2)}, u32[]{:S(2)}) collective-permute-start(f32[384]{0:T(512)S(1)} %log_add_fusion), channel_id=1, source_target_pairs={{0,1},{1,2},{2,3},{3,0},{4,5},{5,6},{6,7},{7,4},{8,9},{9,10},{10,1... | collective-permute-start | bytes 4616 | tf_op jit(solution)/shard_map/ppermute | solution.py:62
  106.6 5.2 %collective-permute-start.18 = (f32[384]{0:T(512)S(1)}, f32[384]{0:T(512)S(1)}, u32[]{:S(2)}, u32[]{:S(2)}) collective-permute-start(f32[384]{0:T(512)S(1)} %log_add_fusion), channel_id=1, source_target_pairs={{0,2},{1,3},{2,0},{3,1},{4,6},{5,7},{6,4},{7,5},{8,10},{9,11},{10,... | collective-permute-start | bytes 4616 | tf_op jit(solution)/shard_map/ppermute | solution.py:62
  109.3 3.6 %collective-permute-start.19 = (f32[384]{0:T(512)S(1)}, f32[384]{0:T(512)S(1)}, u32[]{:S(2)}, u32[]{:S(2)}) collective-permute-start(f32[384]{0:T(512)S(1)} %log_add_fusion), channel_id=1, source_target_pairs={{0,3},{1,0},{2,1},{3,2},{4,7},{5,4},{6,5},{7,6},{8,11},{9,8},{10,9... | collective-permute-start | bytes 4616 | tf_op jit(solution)/shard_map/ppermute | solution.py:62
  113.1 1.7 collective-permute-start.20
  118.6 12.1 %collective-permute-start.25 = (bf16[4,192,512]{2,1,0:T(8,128)(2,1)S(1)}, bf16[4,192,512]{2,1,0:T(8,128)(2,1)S(1)}, u32[]{:S(2)}, u32[]{:S(2)}) collective-permute-start(bf16[4,192,512]{2,1,0:T(8,128)(2,1)S(1)} %get-tuple-element.48), channel_id=1, source_target_pairs={{0,96},{4,28},{8,104},{12,4},{16,112},{20,12},{24,120},{28,20},{32... | collective-permute-start | bytes 2359304 | tf_op jit(solution)/shard_map/ppermute | solution.py:32
  119.8 13.9 %collective-permute-start.22 = (bf16[4,208,512]{2,1,0:T(8,128)(2,1)S(1)}, bf16[4,208,512]{2,1,0:T(8,128)(2,1)S(1)}, u32[]{:S(2)}, u32[]{:S(2)}) collective-permute-start(bf16[4,208,512]{2,1,0:T(8,128)(2,1)S(1)} %get-tuple-element.44), channel_id=1, source_target_pairs={{0,32},{4,12},{8,40},{12,20},{16,48},{20,28},{24,56},{28,4},{32,64... | collective-permute-start | bytes 2555912 | tf_op jit(solution)/shard_map/ppermute | solution.py:32
  126.5 22.1 %collective-permute-start.21 = (bf16[4,208,512]{2,1,0:T(8,128)(2,1)S(1)}, bf16[4,208,512]{2,1,0:T(8,128)(2,1)S(1)}, u32[]{:S(2)}, u32[]{:S(2)}) collective-permute-start(bf16[4,208,512]{2,1,0:T(8,128)(2,1)S(1)} %get-tuple-element.42), channel_id=1, source_target_pairs={{0,96},{4,28},{8,104},{12,4},{16,112},{20,12},{24,120},{28,20},{32... | collective-permute-start | bytes 2555912 | tf_op jit(solution)/shard_map/ppermute | solution.py:32
  128.9 13.3 %collective-permute-start.24 = (bf16[4,192,512]{2,1,0:T(8,128)(2,1)S(1)}, bf16[4,192,512]{2,1,0:T(8,128)(2,1)S(1)}, u32[]{:S(2)}, u32[]{:S(2)}) collective-permute-start(bf16[4,192,512]{2,1,0:T(8,128)(2,1)S(1)} %get-tuple-element.46), channel_id=1, source_target_pairs={{0,32},{4,12},{8,40},{12,20},{16,48},{20,28},{24,56},{28,4},{32,64... | collective-permute-start | bytes 2359304 | tf_op jit(solution)/shard_map/ppermute | solution.py:32
  130.9 17.3 %collective-permute-start.26 = (bf16[4,192,512]{2,1,0:T(8,128)(2,1)S(1)}, bf16[4,192,512]{2,1,0:T(8,128)(2,1)S(1)}, u32[]{:S(2)}, u32[]{:S(2)}) collective-permute-start(bf16[4,192,512]{2,1,0:T(8,128)(2,1)S(1)} %add_convert_fusion.1), channel_id=1, source_target_pairs={{0,96},{4,28},{8,104},{12,4},{16,112},{20,12},{24,120},{28,20},{32... | collective-permute-start | bytes 2359304 | tf_op jit(solution)/shard_map/ppermute | solution.py:32
  134.0 17.3 %collective-permute-start.23 = (bf16[4,208,512]{2,1,0:T(8,128)(2,1)S(1)}, bf16[4,208,512]{2,1,0:T(8,128)(2,1)S(1)}, u32[]{:S(2)}, u32[]{:S(2)}) collective-permute-start(bf16[4,208,512]{2,1,0:T(8,128)(2,1)S(1)} %add_convert_fusion), channel_id=1, source_target_pairs={{0,32},{4,12},{8,40},{12,20},{16,48},{20,28},{24,56},{28,4},{32,64... | collective-permute-start | bytes 2555912 | tf_op jit(solution)/shard_map/ppermute | solution.py:32
  151.7 9.6 %collective-permute-start.27 = (bf16[400,512]{1,0:T(8,128)(2,1)S(1)}, bf16[400,512]{1,0:T(8,128)(2,1)S(1)}, u32[]{:S(2)}, u32[]{:S(2)}) collective-permute-start(bf16[400,512]{1,0:T(8,128)(2,1)S(1)} %pad_maximum_fusion.2), channel_id=1, source_target_pairs={{0,16},{4,68},{8,24},{12,76},{16,0},{20,84},{24,8},{28,92},{32,48}... | collective-permute-start | bytes 1228808 | tf_op jit(solution)/shard_map/ppermute | solution.py:32
  152.9 12.7 %collective-permute-start.28 = (bf16[400,512]{1,0:T(8,128)(2,1)S(1)}, bf16[400,512]{1,0:T(8,128)(2,1)S(1)}, u32[]{:S(2)}, u32[]{:S(2)}) collective-permute-start(bf16[400,512]{1,0:T(8,128)(2,1)S(1)} %pad_maximum_fusion.3), channel_id=1, source_target_pairs={{0,8},{4,36},{8,16},{12,44},{16,24},{20,52},{24,0},{28,60},{32,40}... | collective-permute-start | bytes 1228808 | tf_op jit(solution)/shard_map/ppermute | solution.py:32
  153.9 11.7 %collective-permute-start.29 = (bf16[400,512]{1,0:T(8,128)(2,1)S(1)}, bf16[400,512]{1,0:T(8,128)(2,1)S(1)}, u32[]{:S(2)}, u32[]{:S(2)}) collective-permute-start(bf16[400,512]{1,0:T(8,128)(2,1)S(1)} %pad_maximum_fusion.4), channel_id=1, source_target_pairs={{0,24},{4,100},{8,0},{12,108},{16,8},{20,116},{24,16},{28,124},{32... | collective-permute-start | bytes 1228808 | tf_op jit(solution)/shard_map/ppermute | solution.py:32

commit v7 on v6

--- a/solution.py
+++ b/solution.py
@@ -57,7 +57,7 @@
 def to_all_noise(values):
     n = lax.axis_size("noise")
     parts = [values]
-    for k in range(1, n):
+    for k in sorted(range(1, n), key=lambda k: -min(k, n - k)):
         parts.append(
             lax.ppermute(values, "noise", [(i, (i + k) % n) for i in range(n)])
         )
@@ -101,14 +101,15 @@
     ]
 
 
-def held_blocks(ids, data, data_other):
+def held_blocks(ids, start, n, data, data_other):
     rows, width = data.shape
+    block = width // (2 * BLOCKS)
 
     def kernel(ids_ref, data_ref, data_other_ref, held, sems):
         copies = []
-        for t in range(BLOCKS):
+        for t in range(n):
             copies += block_copies(
-                ids_ref, t, (data_ref, data_other_ref), held, t, sems
+                ids_ref, start + t, (data_ref, data_other_ref), held, t, sems
             )
         for copy in copies:
             copy.start()
@@ -119,11 +120,11 @@
         kernel,
         [ids] + in_hbm([data, data_other]),
         [IN_SMEM, ANYWHERE, ANYWHERE],
-        pltpu.VMEM((2 * rows, width // 2), data.dtype),
+        pltpu.VMEM((2 * rows, n * block), data.dtype),
         IN_VMEM,
-        [pltpu.SemaphoreType.DMA((2, BLOCKS))],
+        [pltpu.SemaphoreType.DMA((2, n))],
         0,
-        rows * width * 4,
+        n * rows * block * 8,
     )
 
 
@@ -191,34 +192,35 @@
     return own + swap(other), sq_data
 
 
-def part_sums(start, n, ins, ids, step=2):
+def part_sums(start, groups, ins, ids, ready=None, step=2):
     w_own, w_oth, data, data_other = ins
     rows, inner = w_own.shape
     dtype = data.dtype
     block = data.shape[1] // (2 * BLOCKS)
     half = rows // 2
-    groups = len(start)
-
-    def kernel(ids_ref, w_own_ref, w_oth_ref, data_ref, data_other_ref, *refs):
-        outs, (weights, held, tops, bottoms, in_sems, sems) = (
-            refs[: 2 * groups],
-            refs[2 * groups :],
+    ends = [sum(groups[: a + 1]) for a in range(len(groups))]
+    count = ends[-1]
+    sources = [data, data_other] if ready is None else [ready]
+
+    def kernel(ids_ref, w_own_ref, w_oth_ref, *refs):
+        refs, outs, scratch = (
+            refs[: len(sources)],
+            refs[len(sources) : len(sources) + 2 * len(groups)],
+            refs[len(sources) + 2 * len(groups) :],
         )
-        into = []
-        for a, first in enumerate(start):
-            for i in range(n):
-                into.append(
-                    block_copies(
-                        ids_ref,
-                        first + i,
-                        (data_ref, data_other_ref),
-                        held,
-                        a * n + i,
-                        in_sems,
-                    )
-                )
-                for copy in into[-1]:
+        weights, tops, bottoms, sems, *scratch = scratch
+        into = [[]] * count
+        if ready is None:
+            held, in_sems = scratch
+            into = [
+                block_copies(ids_ref, start + spot, refs, held, spot, in_sems)
+                for spot in range(count)
+            ]
+            for copies in into:
+                for copy in copies:
                     copy.start()
+        else:
+            (held,) = refs
         weights[:, :inner] = w_own_ref[...]
         weights[:, inner:] = w_oth_ref[...]
         ones = jnp.ones((EXTRA, 2 * inner), dtype)
@@ -228,54 +230,62 @@
             (((1,), (1,)), ((), ())),
             preferred_element_type=jnp.float32,
         ).astype(dtype)
+        for spot in range(count):
+            tops[spot, half:, :rows] = row_sums
+            tops[spot, half:, rows:] = jnp.zeros((EXTRA, block - rows), dtype)
         out = []
-        for a in range(groups):
-            for i in range(n):
-                tops[a, i, half:, :rows] = row_sums
-                tops[a, i, half:, rows:] = jnp.zeros((EXTRA, block - rows), dtype)
-            for i in range(0, n, step):
-                spot = a * n + i
-                for copies in into[spot : spot + step]:
-                    for copy in copies:
-                        copy.wait()
-                total = jnp.dot(
-                    weights[...],
-                    held[:, spot * block : (spot + step) * block],
-                    preferred_element_type=jnp.float32,
-                ).astype(dtype)
-                for j in range(step):
-                    part = total[:, j * block : (j + 1) * block]
-                    tops[a, i + j, :half] = part[:half]
-                    bottoms[a, i + j] = part[half:]
-            for p, held_part in enumerate((tops, bottoms)):
-                to = 2 * a + p
-                out.append(
-                    pltpu.make_async_copy(held_part.at[a], outs[to], sems.at[to])
-                )
-                out[-1].start()
+        for spot in range(0, count, step):
+            stop = spot + step
+            for copies in into[spot:stop]:
+                for copy in copies:
+                    copy.wait()
+            total = jnp.dot(
+                weights[...],
+                held[:, spot * block : stop * block],
+                preferred_element_type=jnp.float32,
+            ).astype(dtype)
+            for j in range(step):
+                part = total[:, j * block : (j + 1) * block]
+                tops[spot + j, :half] = part[:half]
+                bottoms[spot + j] = part[half:]
+            for a, n in enumerate(groups):
+                if not spot < ends[a] <= stop:
+                    continue
+                for p, source in enumerate((tops, bottoms)):
+                    to = 2 * a + p
+                    out.append(
+                        pltpu.make_async_copy(
+                            source.at[pl.ds(ends[a] - n, n)], outs[to], sems.at[to]
+                        )
+                    )
+                    out[-1].start()
         for copy in out:
             copy.wait()
 
+    shapes = []
+    for n in groups:
+        shapes.append(jax.ShapeDtypeStruct((n, half + EXTRA, block), dtype))
+        shapes.append(jax.ShapeDtypeStruct((n, half, block), dtype))
+    scratch = [
+        pltpu.VMEM((rows, 2 * inner), dtype),
+        pltpu.VMEM((count, half + EXTRA, block), dtype),
+        pltpu.VMEM((count, half, block), dtype),
+        pltpu.SemaphoreType.DMA((2 * len(groups),)),
+    ]
+    if ready is None:
+        scratch.append(pltpu.VMEM((2 * inner, count * block), dtype))
+        scratch.append(pltpu.SemaphoreType.DMA((2, count)))
+        sources = in_hbm(sources)
     return call(
         kernel,
-        [ids, w_own, w_oth] + in_hbm([data, data_other]),
-        [IN_SMEM, IN_VMEM, IN_VMEM, ANYWHERE, ANYWHERE],
-        [
-            jax.ShapeDtypeStruct((n, half + EXTRA, block), dtype),
-            jax.ShapeDtypeStruct((n, half, block), dtype),
-        ]
-        * groups,
-        [ANYWHERE] * (2 * groups),
-        [
-            pltpu.VMEM((rows, 2 * inner), dtype),
-            pltpu.VMEM((2 * inner, groups * n * block), dtype),
-            pltpu.VMEM((groups, n, half + EXTRA, block), dtype),
-            pltpu.VMEM((groups, n, half, block), dtype),
-            pltpu.SemaphoreType.DMA((2, groups * n)),
-            pltpu.SemaphoreType.DMA((2 * groups,)),
-        ],
-        groups * n * 4 * rows * inner * block,
-        groups * n * 2 * block * (2 * inner + rows),
+        [ids, w_own, w_oth] + sources,
+        [IN_SMEM, IN_VMEM, IN_VMEM]
+        + ([ANYWHERE] * 2 if ready is None else [IN_VMEM]),
+        shapes,
+        [ANYWHERE] * len(shapes),
+        scratch,
+        count * 4 * rows * inner * block,
+        count * 2 * block * (2 * inner + rows),
     )
 
 
@@ -286,33 +296,38 @@
     return total
 
 
-def scattered_sums(ins, ids):
-    top, bottom = part_sums([12], 4, ins, ids)
+def scattered_sums(ins, ids, ready):
+    top, bottom = part_sums(12, [4], ins, ids, ready)
     weights, top, bottom = lax.optimization_barrier((ins[0], top, bottom))
     ins = (weights,) + ins[1:]
     top, bottom = hop(top, 1, False), hop(bottom, -1, False)
-    up_top, up_bottom, down_top, down_bottom = part_sums([4, 8], 4, ins, ids)
-    weights, up_bottom, down_top = lax.optimization_barrier(
-        (weights, up_bottom, down_top)
-    )
+    parts = part_sums(4, [3, 1, 3, 1], ins, ids)
+    up_top, up_bottom, up_own_top, up_own_bottom, *parts = parts
+    down_top, down_bottom, down_own_top, down_own_bottom = parts
+    tops, bottoms = [hop(down_top, -1, False)], [hop(up_bottom, 1, False)]
+    dtype = top.dtype
+    up_top = added(up_top, [top[:3]]).astype(dtype)
+    down_bottom = added(down_bottom, [bottom[:3]]).astype(dtype)
+    weights, up_top, down_bottom = lax.optimization_barrier(
+        (weights, up_top, down_bottom)
+    )
+    tops.append(hop(up_top, 1, False))
+    bottoms.append(hop(down_bottom, -1, False))
     ins = (weights,) + ins[1:]
-    tops, bottoms = [hop(down_top, -1, False)], [hop(up_bottom, 1, False)]
-    near_top, near_bottom = part_sums([0], 4, ins, ids)
-    tops.append(hop(added(up_top, [top]).astype(top.dtype), 1, False))
-    bottoms.append(hop(added(down_bottom, [bottom]).astype(top.dtype), -1, False))
-    totals = []
-    for a in range(3):
+    near_top, near_bottom = part_sums(0, [4], ins, ids)
+    up_own_top = added(up_own_top[0], [top[3]]).astype(dtype)
+    down_own_bottom = added(down_own_bottom[0], [bottom[3]]).astype(dtype)
+    last = [
+        hop(jnp.concatenate([up_own_top, up_own_bottom[0]]), 1, False),
+        hop(jnp.concatenate([down_own_top[0], down_own_bottom]), -1, False),
+    ]
+    for a, k in enumerate(OFFS):
         total = [
             added(near_top[a], [got[a] for got in tops]),
             added(near_bottom[a], [got[a] for got in bottoms]),
         ]
-        totals.append(jnp.concatenate(total).astype(top.dtype))
-    last = [hop(total, k, True) for total, k in zip(totals, OFFS)]
-    total = [
-        added(near_top[3], [got[3] for got in tops]),
-        added(near_bottom[3], [got[3] for got in bottoms]),
-    ]
-    total = added(jnp.concatenate(total), last)
+        last.append(hop(jnp.concatenate(total).astype(dtype), k, True))
+    total = added(jnp.concatenate([near_top[3], near_bottom[3]]), last)
     rows = total.shape[0] - EXTRA
     half = rows // 2
     row_sums = total[half, :rows]
@@ -328,7 +343,7 @@
     y = place // (2 * SIDE)
     ids = block_ids(y, z, core)
     data_other = swap(data_latents)
-    held = held_blocks(ids, data_latents, data_other)
+    held = held_blocks(ids, 0, BLOCKS, data_latents, data_other)
     noise_f = noise_latents.astype(jnp.float32)
     sx_part = jnp.sum(noise_f * noise_f, axis=1)
     data_f = data_latents.astype(jnp.float32)
@@ -349,11 +364,14 @@
             got = to_all_dp(local)
         f = sx - lse(got, 0)
         local = lse(twice + (f - sx)[:, None], 0)
+        if step == ITERS - 1:
+            local, ids = lax.optimization_barrier((local, ids))
         g = sy - lse(to_all_noise(local), 0)
     coupling = jnp.exp(twice + (f - sx)[:, None] + (g - sy)[None, :])
     weights = coupling.astype(jnp.bfloat16)
+    ready = held_blocks(ids, 12, 4, data_latents, data_other)
     means = scattered_sums(
-        (weights, swap(weights), data_latents, data_other), ids
+        (weights, swap(weights), data_latents, data_other), ids, ready
     )
     return means.astype(jnp.bfloat16)
 

time: 167 us -> 164 us (0.982)
  waiting for transfers between devices: 49.9 us -> 42.3 us
  starting transfers between devices: 40.4 us -> 42.6 us
  Pallas kernels: 28.3 us -> 30.5 us
    ppermute x18 -> x20, waiting for transfers between devices: 38.7 us -> 33.6 us  [hop(): return lax.ppermute(values, 'dp', pairs)]
    pallas_call x7 -> x8, Pallas kernels: 28.3 us -> 30.5 us  [call(): pl.pallas_call(kernel, in_specs=in_specs, out_specs=out_specs, out_shape=...]
    ppermute x18 -> x20, starting transfers between devices: 25.9 us -> 27.2 us  [hop(): return lax.ppermute(values, 'dp', pairs)]
  transfers between devices with their start and end apart: 30 -> 32, of which waited for: 22 -> 21; matrix products, arithmetic and copies ran while one was open for 6% -> 6% of each run, Pallas kernels for 13% -> 16%
where the time goes in v7:
time: 164 us; the launch traced here: 163 us
  starting transfers between devices  42.6 us (26%)
  waiting for transfers between devices  42.3 us (26%)
  blocking collectives  33.2 us (20%)
  Pallas kernels  30.5 us (19%)
  other arithmetic  13.9 us (8%)
    ppermute x20, waiting for transfers between devices, hop(): return lax.ppermute(values, 'dp', pairs)  33.6 us
    all_to_all x3, blocking collectives, to_all_dp(): lax.all_to_all(jnp.broadcast_to(values[None], (n,) + values.shape), 'dp',...  33.2 us
    pallas_call x8, Pallas kernels, call(): pl.pallas_call(kernel, in_specs=in_specs, out_specs=out_specs, out_shape=...  30.5 us
    ppermute x20, starting transfers between devices, hop(): return lax.ppermute(values, 'dp', pairs)  27.2 us
    ppermute x9, starting transfers between devices, to_all_noise(): lax.ppermute(values, 'noise', [(i, (i + k) % n) for i in range(n)])  15.1 us
    reduce_sum x1, other arithmetic, body(): sq_data = jnp.sum(data_f * data_f, axis=1)  7.14 us
    ppermute x9, waiting for transfers between devices, to_all_noise(): lax.ppermute(values, 'noise', [(i, (i + k) % n) for i in range(n)])  6.85 us
  transfers between devices with their start and end apart: 32, of which 21 were waited for; matrix products, arithmetic and copies ran while one was open for 6% of the time, Pallas kernels for 16%

profile of v7, /device:TPU:0, one launch (start us, length us, event | category | flops | bytes accessed | tf_op | source)
XLA Modules:
  0.0 163.4 jit_solution(15161928664568921440)
XLA Ops:
  0.0 2.1 %collective-permute-start.2 = (bf16[384,512]{1,0:T(8,128)(2,1)}, bf16[384,512]{1,0:T(8,128)(2,1)S(1)}, u32[]{:S(2)}, u32[]{:S(2)}) collective-permute-start(bf16[384,512]{1,0:T(8,128)(2,1)} %param.2), channel_id=1, source_target_pairs={{0,8},{4,36},{8,16},{12,44},{16,24},{20,52},{24,0},{28,60},{32,40}... | collective-permute-start | bytes 1179656 | tf_op jit(solution)/shard_map/ppermute | solution.py:32
  2.1 3.6 %collective-permute-start = (bf16[384,512]{1,0:T(8,128)(2,1)}, bf16[384,512]{1,0:T(8,128)(2,1)S(1)}, u32[]{:S(2)}, u32[]{:S(2)}) collective-permute-start(bf16[384,512]{1,0:T(8,128)(2,1)} %param.2), channel_id=1, source_target_pairs={{0,16},{4,68},{8,24},{12,76},{16,0},{20,84},{24,8},{28,92},{32,48}... | collective-permute-start | bytes 1179656 | tf_op jit(solution)/shard_map/ppermute | solution.py:32
  6.7 7.1 %multiply_reduce_fusion = f32[384]{0:T(512)S(1)} fusion(bf16[384,16384]{1,0:T(8,128)(2,1)} %refs_0_.3), kind=kLoop, calls=%fused_computation | loop fusion | flops 18873984 | bytes 12584448 | tf_op jit(solution)/shard_map/reduce_sum | solution.py:350
  13.8 2.0 %collective-permute-done = bf16[384,512]{1,0:T(8,128)(2,1)S(1)} collective-permute-done((bf16[384,512]{1,0:T(8,128)(2,1)}, bf16[384,512]{1,0:T(8,128)(2,1)S(1)}, u32[]{:S(2)}, u32[]{:S(2)}) %collective-permute-start) | collective-permute-done | bytes 393248 | tf_op jit(solution)/shard_map/ppermute | solution.py:32
  17.3 3.0 %collective-permute-start.3 = (bf16[4,192,512]{2,1,0:T(8,128)(2,1)}, bf16[4,192,512]{2,1,0:T(8,128)(2,1)S(1)}, u32[]{:S(2)}, u32[]{:S(2)}) collective-permute-start(bf16[4,192,512]{2,1,0:T(8,128)(2,1)} %get-tuple-element.33), channel_id=1, source_target_pairs={{0,96},{4,28},{8,104},{12,4},{16,112},{20,12},{24,120},{28,20},{32... | collective-permute-start | bytes 2359304 | tf_op jit(solution)/shard_map/ppermute | solution.py:32
  20.4 3.2 %collective-permute-start.8 = (bf16[4,192,512]{2,1,0:T(8,128)(2,1)}, bf16[4,192,512]{2,1,0:T(8,128)(2,1)}, u32[]{:S(2)}, u32[]{:S(2)}) collective-permute-start(bf16[4,192,512]{2,1,0:T(8,128)(2,1)} %get-tuple-element.34), channel_id=1, source_target_pairs={{0,96},{4,28},{8,104},{12,4},{16,112},{20,12},{24,120},{28,20},{32... | collective-permute-start | bytes 2359304 | tf_op jit(solution)/shard_map/ppermute | solution.py:32
  23.7 5.6 %shard_map.28.refs_4_.refs_2_ = bf16[768,8192]{1,0:T(8,128)(2,1)S(1)} custom-call(s32[16]{0:T(128)S(1)} %stack.155.ids_ref, bf16[384,16384]{1,0:T(8,128)(2,1)} %refs_0_.3, bf16[384,16384]{1,0:T(8,128)(2,1)} %collective-permute-done.5.data_other_ref.refs_1_), custom_call_target="tpu_custom_call" | custom-call | bytes 25165824 | tf_op jit(solution)/shard_map/pallas_call | solution.py:68
  30.8 3.0 %collective-permute-done.4.refs_3_ = bf16[4,192,512]{2,1,0:T(8,128)(2,1)S(1)} collective-permute-done((bf16[4,192,512]{2,1,0:T(8,128)(2,1)}, bf16[4,192,512]{2,1,0:T(8,128)(2,1)S(1)}, u32[]{:S(2)}, u32[]{:S(2)}) %collective-permute-start.4) | collective-permute-done | bytes 786464 | tf_op jit(solution)/shard_map/ppermute | solution.py:32
  35.8 2.8 %collective-permute-done.8.refs_1_ = bf16[4,192,512]{2,1,0:T(8,128)(2,1)} collective-permute-done((bf16[4,192,512]{2,1,0:T(8,128)(2,1)}, bf16[4,192,512]{2,1,0:T(8,128)(2,1)}, u32[]{:S(2)}, u32[]{:S(2)}) %collective-permute-start.8) | collective-permute-done | bytes 786464 | tf_op jit(solution)/shard_map/ppermute | solution.py:32
  38.6 3.7 %collective-permute-done.9.refs_2_ = bf16[4,192,512]{2,1,0:T(8,128)(2,1)} collective-permute-done((bf16[4,192,512]{2,1,0:T(8,128)(2,1)}, bf16[4,192,512]{2,1,0:T(8,128)(2,1)}, u32[]{:S(2)}, u32[]{:S(2)}) %collective-permute-start.9) | collective-permute-done | bytes 786464 | tf_op jit(solution)/shard_map/ppermute | solution.py:32
  42.3 5.6 %shard_map.30.refs_3_ = f32[384,768]{1,0:T(8,128)S(1)} custom-call(bf16[4,192,512]{2,1,0:T(8,128)(2,1)S(1)} %collective-permute-done.3.refs_0_, bf16[4,192,512]{2,1,0:T(8,128)(2,1)} %collective-permute-done.8.refs_1_, bf16[4,192,512]{2,1,0:T(8,128)(2,1)} %collective-permute-done.9.refs_2_, bf16[4,192,512]{2,1,0:T(8,128)(2,1)S(1)} %collective-permute-done.4.refs_3_, ...), custom_call_target="tpu_custom_call" | custom-call | flops 2415919104 | bytes 9437184 | tf_op jit(solution)/shard_map/pallas_call | solution.py:68
  47.9 2.7 %collective-permute-done.7.refs_1_ = bf16[4,192,512]{2,1,0:T(8,128)(2,1)S(1)} collective-permute-done((bf16[4,192,512]{2,1,0:T(8,128)(2,1)S(1)}, bf16[4,192,512]{2,1,0:T(8,128)(2,1)S(1)}, u32[]{:S(2)}, u32[]{:S(2)}) %collective-permute-start.7) | collective-permute-done | bytes 786464 | tf_op jit(solution)/shard_map/ppermute | solution.py:32
  50.6 2.2 %shard_map.31 = (f32[384,384]{1,0:T(8,128)S(1)}, f32[384,384]{1,0:T(8,128)S(1)}) custom-call(bf16[4,192,512]{2,1,0:T(8,128)(2,1)S(1)} %collective-permute-done.6.refs_0_, bf16[4,192,512]{2,1,0:T(8,128)(2,1)S(1)} %collective-permute-done.7.refs_1_, bf16[768,8192]{1,0:T(8,128)(2,1)S(1)} %shard_map.28.refs_4_.refs_2_, f32[384,768]{1,0:T(8,128)S(1)} %shard_map.30.refs_3_), custom_call_target="tpu_custom_call" | custom-call | flops 1207959552 | bytes 4718592 | tf_op jit(solution)/shard_map/pallas_call | solution.py:68
  53.3 1.8 %collective-permute-done.10 = f32[384,384]{1,0:T(8,128)S(1)} collective-permute-done((f32[384,384]{1,0:T(8,128)S(1)}, f32[384,384]{1,0:T(8,128)S(1)}, u32[]{:S(2)}, u32[]{:S(2)}) %collective-permute-start.10) | collective-permute-done | bytes 589856 | tf_op jit(solution)/shard_map/ppermute | solution.py:21
  55.6 11.6 %all_to_all.23 = f32[32,2,384]{2,1,0:T(2,128)S(1)} all-to-all(f32[32,2,384]{2,1,0:T(2,128)S(1)} %broadcast_in_dim.21), channel_id=1, replica_groups=mesh['dp'=32,'noise'=4] {'dp'}, dimensions={0} | all-to-all | bytes 196608 | tf_op jit(solution)/shard_map/all_to_all | solution.py:52
  67.6 3.1 %collective-permute-start.11 = (f32[384]{0:T(512)S(1)}, f32[384]{0:T(512)S(1)}, u32[]{:S(2)}, u32[]{:S(2)}) collective-permute-start(f32[384]{0:T(512)S(1)} %log_add_fusion.4), channel_id=1, source_target_pairs={{0,2},{1,3},{2,0},{3,1},{4,6},{5,7},{6,4},{7,5},{8,10},{9,11},{10,... | collective-permute-start | bytes 4616 | tf_op jit(solution)/shard_map/ppermute | solution.py:62
  71.3 2.6 %collective-permute-start.13 = (f32[384]{0:T(512)S(1)}, f32[384]{0:T(512)S(1)}, u32[]{:S(2)}, u32[]{:S(2)}) collective-permute-start(f32[384]{0:T(512)S(1)} %log_add_fusion.4), channel_id=1, source_target_pairs={{0,3},{1,0},{2,1},{3,2},{4,7},{5,4},{6,5},{7,6},{8,11},{9,8},{10,9... | collective-permute-start | bytes 4616 | tf_op jit(solution)/shard_map/ppermute | solution.py:62
  76.1 10.9 %all_to_all.24 = f32[32,1,384]{2,1,0:T(1,128)S(1)} all-to-all(f32[32,1,384]{2,1,0:T(1,128)S(1)} %broadcast_in_dim.22), channel_id=1, replica_groups=mesh['dp'=32,'noise'=4] {'dp'}, dimensions={0} | all-to-all | bytes 98304 | tf_op jit(solution)/shard_map/all_to_all | solution.py:52
  88.9 2.6 %collective-permute-start.15 = (f32[384]{0:T(512)S(1)}, f32[384]{0:T(512)S(1)}, u32[]{:S(2)}, u32[]{:S(2)}) collective-permute-start(f32[384]{0:T(512)S(1)} %log_add_fusion.2), channel_id=1, source_target_pairs={{0,1},{1,2},{2,3},{3,0},{4,5},{5,6},{6,7},{7,4},{8,9},{9,10},{10,1... | collective-permute-start | bytes 4616 | tf_op jit(solution)/shard_map/ppermute | solution.py:62
  95.7 10.8 %all_to_all.25 = f32[32,1,384]{2,1,0:T(1,128)S(1)} all-to-all(f32[32,1,384]{2,1,0:T(1,128)S(1)} %broadcast_in_dim.23), channel_id=1, replica_groups=mesh['dp'=32,'noise'=4] {'dp'}, dimensions={0} | all-to-all | bytes 98304 | tf_op jit(solution)/shard_map/all_to_all | solution.py:52
  107.7 2.0 %collective-permute-start.18 = (f32[384]{0:T(512)S(1)}, f32[384]{0:T(512)S(1)}, u32[]{:S(2)}, u32[]{:S(2)}) collective-permute-start(f32[384]{0:T(512)S(1)} %log_add_fusion), channel_id=1, source_target_pairs={{0,1},{1,2},{2,3},{3,0},{4,5},{5,6},{6,7},{7,4},{8,9},{9,10},{10,1... | collective-permute-start | bytes 4616 | tf_op jit(solution)/shard_map/ppermute | solution.py:62
  113.6 2.5 %shard_map.32.refs_0_ = bf16[768,2048]{1,0:T(8,128)(2,1)S(1)} custom-call(s32[16]{0:T(128)S(1)} %stack.155.ids_ref, bf16[384,16384]{1,0:T(8,128)(2,1)} %refs_0_.3, bf16[384,16384]{1,0:T(8,128)(2,1)} %collective-permute-done.5.data_other_ref.refs_1_), custom_call_target="tpu_custom_call" | custom-call | bytes 6291456 | tf_op jit(solution)/shard_map/pallas_call | solution.py:68
  116.1 2.3 %shard_map.33 = (bf16[4,208,512]{2,1,0:T(8,128)(2,1)S(1)}, bf16[4,192,512]{2,1,0:T(8,128)(2,1)S(1)}) custom-call(s32[16]{0:T(128)S(1)} %stack.155.ids_ref, bf16[384,384]{1,0:T(8,128)(2,1)S(1)} %exponential_convert_fusion.w_own_ref, bf16[384,384]{1,0:T(8,128)(2,1)S(1)} %collective-permute-done.20.w_oth_ref, bf16[768,2048]{1,0:T(8,128)(2,1)S(1)} %shard_map.32.refs_0_), custom_call_target="tpu_custom_call" | custom-call | flops 1207959552 | bytes 4718592 | tf_op jit(solution)/shard_map/pallas_call | solution.py:68
  120.5 7.0 %shard_map.34 = (bf16[3,208,512]{2,1,0:T(8,128)(2,1)S(1)}, bf16[3,192,512]{2,1,0:T(8,128)(2,1)S(1)}, bf16[1,208,512]{2,1,0:T(8,128)(2,1)S(1)}, bf16[1,192,512]{2...) custom-call(s32[16]{0:T(128)S(1)} %stack.155.ids_ref, ...), custom_call_target="tpu_custom_call" | custom-call | flops 2415919104 | bytes 9437184 | tf_op jit(solution)/shard_map/pallas_call | solution.py:68
  127.5 2.4 %collective-permute-start.25 = (bf16[3,208,512]{2,1,0:T(8,128)(2,1)S(1)}, bf16[3,208,512]{2,1,0:T(8,128)(2,1)S(1)}, u32[]{:S(2)}, u32[]{:S(2)}) collective-permute-start(bf16[3,208,512]{2,1,0:T(8,128)(2,1)S(1)} %get-tuple-element.57), channel_id=1, source_target_pairs={{0,96},{4,28},{8,104},{12,4},{16,112},{20,12},{24,120},{28,20},{32... | collective-permute-start | bytes 1916936 | tf_op jit(solution)/shard_map/ppermute | solution.py:32
  130.6 2.8 %collective-permute-done.21 = bf16[4,208,512]{2,1,0:T(8,128)(2,1)S(1)} collective-permute-done((bf16[4,208,512]{2,1,0:T(8,128)(2,1)S(1)}, bf16[4,208,512]{2,1,0:T(8,128)(2,1)S(1)}, u32[]{:S(2)}, u32[]{:S(2)}) %collective-permute-start.21) | collective-permute-done | bytes 852000 | tf_op jit(solution)/shard_map/ppermute | solution.py:32
  135.9 3.9 %shard_map.35 = (bf16[4,208,512]{2,1,0:T(8,128)(2,1)S(1)}, bf16[4,192,512]{2,1,0:T(8,128)(2,1)S(1)}) custom-call(s32[16]{0:T(128)S(1)} %stack.155.ids_ref, bf16[384,384]{1,0:T(8,128)(2,1)S(1)} %exponential_convert_fusion.w_own_ref, bf16[384,384]{1,0:T(8,128)(2,1)S(1)} %collective-permute-done.20.w_oth_ref, bf16[384,16384]{1,0:T(8,128)(2,1)} %refs_0_.3, ...), custom_call_target="tpu_custom_call" | custom-call | flops 1207959552 | bytes 4718592 | tf_op jit(solution)/shard_map/pallas_call | solution.py:68
  141.9 2.4 %collective-permute-done.28 = bf16[3,192,512]{2,1,0:T(8,128)(2,1)S(1)} collective-permute-done((bf16[3,192,512]{2,1,0:T(8,128)(2,1)S(1)}, bf16[3,192,512]{2,1,0:T(8,128)(2,1)S(1)}, u32[]{:S(2)}, u32[]{:S(2)}) %collective-permute-start.28) | collective-permute-done | bytes 589856 | tf_op jit(solution)/shard_map/ppermute | solution.py:32
  144.6 3.3 %collective-permute-done.26 = bf16[3,208,512]{2,1,0:T(8,128)(2,1)S(1)} collective-permute-done((bf16[3,208,512]{2,1,0:T(8,128)(2,1)S(1)}, bf16[3,208,512]{2,1,0:T(8,128)(2,1)S(1)}, u32[]{:S(2)}, u32[]{:S(2)}) %collective-permute-start.26) | collective-permute-done | bytes 639008 | tf_op jit(solution)/shard_map/ppermute | solution.py:32
  150.4 2.4 %collective-permute-start.31 = (bf16[400,512]{1,0:T(8,128)(2,1)S(1)}, bf16[400,512]{1,0:T(8,128)(2,1)S(1)}, u32[]{:S(2)}, u32[]{:S(2)}) collective-permute-start(bf16[400,512]{1,0:T(8,128)(2,1)S(1)} %pad_maximum_fusion.6), channel_id=1, source_target_pairs={{0,24},{4,100},{8,0},{12,108},{16,8},{20,116},{24,16},{28,124},{32... | collective-permute-start | bytes 1228808 | tf_op jit(solution)/shard_map/ppermute | solution.py:32
  152.9 4.7 %collective-permute-done.23 = bf16[400,512]{1,0:T(8,128)(2,1)S(1)} collective-permute-done((bf16[400,512]{1,0:T(8,128)(2,1)S(1)}, bf16[400,512]{1,0:T(8,128)(2,1)S(1)}, u32[]{:S(2)}, u32[]{:S(2)}) %collective-permute-start.23) | collective-permute-done | bytes 409632 | tf_op jit(solution)/shard_map/ppermute | solution.py:32
  157.8 4.3 %collective-permute-done.30 = bf16[400,512]{1,0:T(8,128)(2,1)S(1)} collective-permute-done((bf16[400,512]{1,0:T(8,128)(2,1)S(1)}, bf16[400,512]{1,0:T(8,128)(2,1)S(1)}, u32[]{:S(2)}, u32[]{:S(2)}) %collective-permute-start.30) | collective-permute-done | bytes 409632 | tf_op jit(solution)/shard_map/ppermute | solution.py:32
  (126 shorter events, 32.9 us)
Async XLA Ops:
  0.0 23.7 %collective-permute-start.5 = (bf16[384,16384]{1,0:T(8,128)(2,1)}, bf16[384,16384]{1,0:T(8,128)(2,1)}, u32[]{:S(2)}, u32[]{:S(2)}) collective-permute-start(bf16[384,16384]{1,0:T(8,128)(2,1)} %refs_0_.3), channel_id=1, source_target_pairs={{0,4},{4,0},{8,12},{12,8},{16,20},{20,16},{24,28},{28,24},{32,36},... | collective-permute-start | bytes 37748744 | tf_op jit(solution)/shard_map/ppermute | solution.py:21
  0.0 15.9 %collective-permute-start.2 = (bf16[384,512]{1,0:T(8,128)(2,1)}, bf16[384,512]{1,0:T(8,128)(2,1)S(1)}, u32[]{:S(2)}, u32[]{:S(2)}) collective-permute-start(bf16[384,512]{1,0:T(8,128)(2,1)} %param.2), channel_id=1, source_target_pairs={{0,8},{4,36},{8,16},{12,44},{16,24},{20,52},{24,0},{28,60},{32,40}... | collective-permute-start | bytes 1179656 | tf_op jit(solution)/shard_map/ppermute | solution.py:32
  2.1 13.8 %collective-permute-start = (bf16[384,512]{1,0:T(8,128)(2,1)}, bf16[384,512]{1,0:T(8,128)(2,1)S(1)}, u32[]{:S(2)}, u32[]{:S(2)}) collective-permute-start(bf16[384,512]{1,0:T(8,128)(2,1)} %param.2), channel_id=1, source_target_pairs={{0,16},{4,68},{8,24},{12,76},{16,0},{20,84},{24,8},{28,92},{32,48}... | collective-permute-start | bytes 1179656 | tf_op jit(solution)/shard_map/ppermute | solution.py:32
  5.7 10.2 %collective-permute-start.1 = (bf16[384,512]{1,0:T(8,128)(2,1)}, bf16[384,512]{1,0:T(8,128)(2,1)S(1)}, u32[]{:S(2)}, u32[]{:S(2)}) collective-permute-start(bf16[384,512]{1,0:T(8,128)(2,1)} %param.2), channel_id=1, source_target_pairs={{0,24},{4,100},{8,0},{12,108},{16,8},{20,116},{24,16},{28,124},{32... | collective-permute-start | bytes 1179656 | tf_op jit(solution)/shard_map/ppermute | solution.py:32
  17.3 13.4 %collective-permute-start.3 = (bf16[4,192,512]{2,1,0:T(8,128)(2,1)}, bf16[4,192,512]{2,1,0:T(8,128)(2,1)S(1)}, u32[]{:S(2)}, u32[]{:S(2)}) collective-permute-start(bf16[4,192,512]{2,1,0:T(8,128)(2,1)} %get-tuple-element.33), channel_id=1, source_target_pairs={{0,96},{4,28},{8,104},{12,4},{16,112},{20,12},{24,120},{28,20},{32... | collective-permute-start | bytes 2359304 | tf_op jit(solution)/shard_map/ppermute | solution.py:32
  20.4 13.4 %collective-permute-start.4 = (bf16[4,192,512]{2,1,0:T(8,128)(2,1)}, bf16[4,192,512]{2,1,0:T(8,128)(2,1)S(1)}, u32[]{:S(2)}, u32[]{:S(2)}) collective-permute-start(bf16[4,192,512]{2,1,0:T(8,128)(2,1)} %get-tuple-element.34), channel_id=1, source_target_pairs={{0,32},{4,12},{8,40},{12,20},{16,48},{20,28},{24,56},{28,4},{32,64... | collective-permute-start | bytes 2359304 | tf_op jit(solution)/shard_map/ppermute | solution.py:32
  20.4 18.2 %collective-permute-start.8 = (bf16[4,192,512]{2,1,0:T(8,128)(2,1)}, bf16[4,192,512]{2,1,0:T(8,128)(2,1)}, u32[]{:S(2)}, u32[]{:S(2)}) collective-permute-start(bf16[4,192,512]{2,1,0:T(8,128)(2,1)} %get-tuple-element.34), channel_id=1, source_target_pairs={{0,96},{4,28},{8,104},{12,4},{16,112},{20,12},{24,120},{28,20},{32... | collective-permute-start | bytes 2359304 | tf_op jit(solution)/shard_map/ppermute | solution.py:32
  23.6 18.7 %collective-permute-start.9 = (bf16[4,192,512]{2,1,0:T(8,128)(2,1)}, bf16[4,192,512]{2,1,0:T(8,128)(2,1)}, u32[]{:S(2)}, u32[]{:S(2)}) collective-permute-start(bf16[4,192,512]{2,1,0:T(8,128)(2,1)} %get-tuple-element.33), channel_id=1, source_target_pairs={{0,32},{4,12},{8,40},{12,20},{16,48},{20,28},{24,56},{28,4},{32,64... | collective-permute-start | bytes 2359304 | tf_op jit(solution)/shard_map/ppermute | solution.py:32
  33.8 14.1 %collective-permute-start.6 = (bf16[4,192,512]{2,1,0:T(8,128)(2,1)S(1)}, bf16[4,192,512]{2,1,0:T(8,128)(2,1)S(1)}, u32[]{:S(2)}, u32[]{:S(2)}) collective-permute-start(bf16[4,192,512]{2,1,0:T(8,128)(2,1)S(1)} %collective-permute-done.3.refs_0_), channel_id=1, source_target_pairs={{0,96},{4,28},{8,104},{12,4},{16,112},{20,12},{24,120},{28,20},{32... | collective-permute-start | bytes 2359304 | tf_op jit(solution)/shard_map/ppermute | solution.py:32
  34.1 16.5 %collective-permute-start.7 = (bf16[4,192,512]{2,1,0:T(8,128)(2,1)S(1)}, bf16[4,192,512]{2,1,0:T(8,128)(2,1)S(1)}, u32[]{:S(2)}, u32[]{:S(2)}) collective-permute-start(bf16[4,192,512]{2,1,0:T(8,128)(2,1)S(1)} %collective-permute-done.4.refs_3_), channel_id=1, source_target_pairs={{0,32},{4,12},{8,40},{12,20},{16,48},{20,28},{24,56},{28,4},{32,64... | collective-permute-start | bytes 2359304 | tf_op jit(solution)/shard_map/ppermute | solution.py:32
  52.8 2.3 %collective-permute-start.10 = (f32[384,384]{1,0:T(8,128)S(1)}, f32[384,384]{1,0:T(8,128)S(1)}, u32[]{:S(2)}, u32[]{:S(2)}) collective-permute-start(f32[384,384]{1,0:T(8,128)S(1)} %get-tuple-element.39), channel_id=1, source_target_pairs={{0,4},{4,0},{8,12},{12,8},{16,20},{20,16},{24,28},{28,24},{32,36},... | collective-permute-start | bytes 1769480 | tf_op jit(solution)/shard_map/ppermute | solution.py:21
  67.6 6.4 %collective-permute-start.11 = (f32[384]{0:T(512)S(1)}, f32[384]{0:T(512)S(1)}, u32[]{:S(2)}, u32[]{:S(2)}) collective-permute-start(f32[384]{0:T(512)S(1)} %log_add_fusion.4), channel_id=1, source_target_pairs={{0,2},{1,3},{2,0},{3,1},{4,6},{5,7},{6,4},{7,5},{8,10},{9,11},{10,... | collective-permute-start | bytes 4616 | tf_op jit(solution)/shard_map/ppermute | solution.py:62
  70.7 4.8 %collective-permute-start.12 = (f32[384]{0:T(512)S(1)}, f32[384]{0:T(512)S(1)}, u32[]{:S(2)}, u32[]{:S(2)}) collective-permute-start(f32[384]{0:T(512)S(1)} %log_add_fusion.4), channel_id=1, source_target_pairs={{0,1},{1,2},{2,3},{3,0},{4,5},{5,6},{6,7},{7,4},{8,9},{9,10},{10,1... | collective-permute-start | bytes 4616 | tf_op jit(solution)/shard_map/ppermute | solution.py:62
  71.3 4.2 %collective-permute-start.13 = (f32[384]{0:T(512)S(1)}, f32[384]{0:T(512)S(1)}, u32[]{:S(2)}, u32[]{:S(2)}) collective-permute-start(f32[384]{0:T(512)S(1)} %log_add_fusion.4), channel_id=1, source_target_pairs={{0,3},{1,0},{2,1},{3,2},{4,7},{5,4},{6,5},{7,6},{8,11},{9,8},{10,9... | collective-permute-start | bytes 4616 | tf_op jit(solution)/shard_map/ppermute | solution.py:62
  87.4 5.2 %collective-permute-start.14 = (f32[384]{0:T(512)S(1)}, f32[384]{0:T(512)S(1)}, u32[]{:S(2)}, u32[]{:S(2)}) collective-permute-start(f32[384]{0:T(512)S(1)} %log_add_fusion.2), channel_id=1, source_target_pairs={{0,2},{1,3},{2,0},{3,1},{4,6},{5,7},{6,4},{7,5},{8,10},{9,11},{10,... | collective-permute-start | bytes 4616 | tf_op jit(solution)/shard_map/ppermute | solution.py:62
  88.9 4.8 %collective-permute-start.15 = (f32[384]{0:T(512)S(1)}, f32[384]{0:T(512)S(1)}, u32[]{:S(2)}, u32[]{:S(2)}) collective-permute-start(f32[384]{0:T(512)S(1)} %log_add_fusion.2), channel_id=1, source_target_pairs={{0,1},{1,2},{2,3},{3,0},{4,5},{5,6},{6,7},{7,4},{8,9},{9,10},{10,1... | collective-permute-start | bytes 4616 | tf_op jit(solution)/shard_map/ppermute | solution.py:62
  91.6 3.6 %collective-permute-start.16 = (f32[384]{0:T(512)S(1)}, f32[384]{0:T(512)S(1)}, u32[]{:S(2)}, u32[]{:S(2)}) collective-permute-start(f32[384]{0:T(512)S(1)} %log_add_fusion.2), channel_id=1, source_target_pairs={{0,3},{1,0},{2,1},{3,2},{4,7},{5,4},{6,5},{7,6},{8,11},{9,8},{10,9... | collective-permute-start | bytes 4616 | tf_op jit(solution)/shard_map/ppermute | solution.py:62
  106.9 5.2 %collective-permute-start.17 = (f32[384]{0:T(512)S(1)}, f32[384]{0:T(512)S(1)}, u32[]{:S(2)}, u32[]{:S(2)}) collective-permute-start(f32[384]{0:T(512)S(1)} %log_add_fusion), channel_id=1, source_target_pairs={{0,2},{1,3},{2,0},{3,1},{4,6},{5,7},{6,4},{7,5},{8,10},{9,11},{10,... | collective-permute-start | bytes 4616 | tf_op jit(solution)/shard_map/ppermute | solution.py:62
  107.7 4.8 %collective-permute-start.18 = (f32[384]{0:T(512)S(1)}, f32[384]{0:T(512)S(1)}, u32[]{:S(2)}, u32[]{:S(2)}) collective-permute-start(f32[384]{0:T(512)S(1)} %log_add_fusion), channel_id=1, source_target_pairs={{0,1},{1,2},{2,3},{3,0},{4,5},{5,6},{6,7},{7,4},{8,9},{9,10},{10,1... | collective-permute-start | bytes 4616 | tf_op jit(solution)/shard_map/ppermute | solution.py:62
  109.7 3.6 %collective-permute-start.19 = (f32[384]{0:T(512)S(1)}, f32[384]{0:T(512)S(1)}, u32[]{:S(2)}, u32[]{:S(2)}) collective-permute-start(f32[384]{0:T(512)S(1)} %log_add_fusion), channel_id=1, source_target_pairs={{0,3},{1,0},{2,1},{3,2},{4,7},{5,4},{6,5},{7,6},{8,11},{9,8},{10,9... | collective-permute-start | bytes 4616 | tf_op jit(solution)/shard_map/ppermute | solution.py:62
  113.5 2.6 %collective-permute-start.20 = (bf16[384,384]{1,0:T(8,128)(2,1)S(1)}, bf16[384,384]{1,0:T(8,128)(2,1)S(1)}, u32[]{:S(2)}, u32[]{:S(2)}) collective-permute-start(bf16[384,384]{1,0:T(8,128)(2,1)S(1)} %exponential_convert_fusion.w_own_ref), channel_id=1, source_target_pairs={{0,4},{4,0},{8,12},{12,8},{16,20},{20,16},{24,28},{28,24},{32,36},... | collective-permute-start | bytes 884744 | tf_op jit(solution)/shard_map/ppermute | solution.py:21
  118.4 12.1 %collective-permute-start.22 = (bf16[4,192,512]{2,1,0:T(8,128)(2,1)S(1)}, bf16[4,192,512]{2,1,0:T(8,128)(2,1)S(1)}, u32[]{:S(2)}, u32[]{:S(2)}) collective-permute-start(bf16[4,192,512]{2,1,0:T(8,128)(2,1)S(1)} %get-tuple-element.49), channel_id=1, source_target_pairs={{0,96},{4,28},{8,104},{12,4},{16,112},{20,12},{24,120},{28,20},{32... | collective-permute-start | bytes 2359304 | tf_op jit(solution)/shard_map/ppermute | solution.py:32
  119.6 13.9 %collective-permute-start.21 = (bf16[4,208,512]{2,1,0:T(8,128)(2,1)S(1)}, bf16[4,208,512]{2,1,0:T(8,128)(2,1)S(1)}, u32[]{:S(2)}, u32[]{:S(2)}) collective-permute-start(bf16[4,208,512]{2,1,0:T(8,128)(2,1)S(1)} %get-tuple-element.47), channel_id=1, source_target_pairs={{0,32},{4,12},{8,40},{12,20},{16,48},{20,28},{24,56},{28,4},{32,64... | collective-permute-start | bytes 2555912 | tf_op jit(solution)/shard_map/ppermute | solution.py:32
  127.5 17.0 %collective-permute-start.25 = (bf16[3,208,512]{2,1,0:T(8,128)(2,1)S(1)}, bf16[3,208,512]{2,1,0:T(8,128)(2,1)S(1)}, u32[]{:S(2)}, u32[]{:S(2)}) collective-permute-start(bf16[3,208,512]{2,1,0:T(8,128)(2,1)S(1)} %get-tuple-element.57), channel_id=1, source_target_pairs={{0,96},{4,28},{8,104},{12,4},{16,112},{20,12},{24,120},{28,20},{32... | collective-permute-start | bytes 1916936 | tf_op jit(solution)/shard_map/ppermute | solution.py:32
  129.9 11.1 %collective-permute-start.27 = (bf16[3,192,512]{2,1,0:T(8,128)(2,1)S(1)}, bf16[3,192,512]{2,1,0:T(8,128)(2,1)S(1)}, u32[]{:S(2)}, u32[]{:S(2)}) collective-permute-start(bf16[3,192,512]{2,1,0:T(8,128)(2,1)S(1)} %get-tuple-element.59), channel_id=1, source_target_pairs={{0,32},{4,12},{8,40},{12,20},{16,48},{20,28},{24,56},{28,4},{32,64... | collective-permute-start | bytes 1769480 | tf_op jit(solution)/shard_map/ppermute | solution.py:32
  133.7 10.7 %collective-permute-start.28 = (bf16[3,192,512]{2,1,0:T(8,128)(2,1)S(1)}, bf16[3,192,512]{2,1,0:T(8,128)(2,1)S(1)}, u32[]{:S(2)}, u32[]{:S(2)}) collective-permute-start(bf16[3,192,512]{2,1,0:T(8,128)(2,1)S(1)} %add_convert_fusion.1), channel_id=1, source_target_pairs={{0,96},{4,28},{8,104},{12,4},{16,112},{20,12},{24,120},{28,20},{32... | collective-permute-start | bytes 1769480 | tf_op jit(solution)/shard_map/ppermute | solution.py:32
  133.8 19.1 %collective-permute-start.24 = (bf16[400,512]{1,0:T(8,128)(2,1)S(1)}, bf16[400,512]{1,0:T(8,128)(2,1)S(1)}, u32[]{:S(2)}, u32[]{:S(2)}) collective-permute-start(bf16[400,512]{1,0:T(8,128)(2,1)S(1)} %pad_maximum_fusion.3), channel_id=1, source_target_pairs={{0,96},{4,28},{8,104},{12,4},{16,112},{20,12},{24,120},{28,20},{32... | collective-permute-start | bytes 1228808 | tf_op jit(solution)/shard_map/ppermute | solution.py:32
  134.7 13.2 %collective-permute-start.26 = (bf16[3,208,512]{2,1,0:T(8,128)(2,1)S(1)}, bf16[3,208,512]{2,1,0:T(8,128)(2,1)S(1)}, u32[]{:S(2)}, u32[]{:S(2)}) collective-permute-start(bf16[3,208,512]{2,1,0:T(8,128)(2,1)S(1)} %add_convert_fusion), channel_id=1, source_target_pairs={{0,32},{4,12},{8,40},{12,20},{16,48},{20,28},{24,56},{28,4},{32,64... | collective-permute-start | bytes 1916936 | tf_op jit(solution)/shard_map/ppermute | solution.py:32
  141.0 16.5 %collective-permute-start.23 = (bf16[400,512]{1,0:T(8,128)(2,1)S(1)}, bf16[400,512]{1,0:T(8,128)(2,1)S(1)}, u32[]{:S(2)}, u32[]{:S(2)}) collective-permute-start(bf16[400,512]{1,0:T(8,128)(2,1)S(1)} %pad_maximum_fusion.2), channel_id=1, source_target_pairs={{0,32},{4,12},{8,40},{12,20},{16,48},{20,28},{24,56},{28,4},{32,64... | collective-permute-start | bytes 1228808 | tf_op jit(solution)/shard_map/ppermute | solution.py:32
  148.2 9.6 %collective-permute-start.29 = (bf16[400,512]{1,0:T(8,128)(2,1)S(1)}, bf16[400,512]{1,0:T(8,128)(2,1)S(1)}, u32[]{:S(2)}, u32[]{:S(2)}) collective-permute-start(bf16[400,512]{1,0:T(8,128)(2,1)S(1)} %pad_maximum_fusion.4), channel_id=1, source_target_pairs={{0,16},{4,68},{8,24},{12,76},{16,0},{20,84},{24,8},{28,92},{32,48}... | collective-permute-start | bytes 1228808 | tf_op jit(solution)/shard_map/ppermute | solution.py:32
  149.4 12.7 %collective-permute-start.30 = (bf16[400,512]{1,0:T(8,128)(2,1)S(1)}, bf16[400,512]{1,0:T(8,128)(2,1)S(1)}, u32[]{:S(2)}, u32[]{:S(2)}) collective-permute-start(bf16[400,512]{1,0:T(8,128)(2,1)S(1)} %pad_maximum_fusion.5), channel_id=1, source_target_pairs={{0,8},{4,36},{8,16},{12,44},{16,24},{20,52},{24,0},{28,60},{32,40}... | collective-permute-start | bytes 1228808 | tf_op jit(solution)/shard_map/ppermute | solution.py:32
  150.4 11.7 %collective-permute-start.31 = (bf16[400,512]{1,0:T(8,128)(2,1)S(1)}, bf16[400,512]{1,0:T(8,128)(2,1)S(1)}, u32[]{:S(2)}, u32[]{:S(2)}) collective-permute-start(bf16[400,512]{1,0:T(8,128)(2,1)S(1)} %pad_maximum_fusion.6), channel_id=1, source_target_pairs={{0,24},{4,100},{8,0},{12,108},{16,8},{20,116},{24,16},{28,124},{32... | collective-permute-start | bytes 1228808 | tf_op jit(solution)/shard_map/ppermute | solution.py:32
  (1 other events, 13.8 us)

commit v8 on v7

--- a/solution.py
+++ b/solution.py
@@ -11,7 +11,7 @@
 OFFS = (2, 1, 3)
 BLOCKS = SIDE * SIDE
 EXTRA = 16
-VMEM_LIMIT = 24 * 1024 * 1024
+VMEM_LIMIT = 14 * 1024 * 1024
 
 SPOTS = [(k, m) for k in (0, 1, 3, 2) for m in OFFS + (0,)]
 
@@ -105,7 +105,7 @@
     rows, width = data.shape
     block = width // (2 * BLOCKS)
 
-    def kernel(ids_ref, data_ref, data_other_ref, held, sems):
+    def kernel(ids_ref, data_ref, data_other_ref, held, mark, sems):
         copies = []
         for t in range(n):
             copies += block_copies(
@@ -113,6 +113,7 @@
             )
         for copy in copies:
             copy.start()
+        mark[...] = jnp.zeros_like(mark)
         for copy in copies:
             copy.wait()
 
@@ -120,76 +121,64 @@
         kernel,
         [ids] + in_hbm([data, data_other]),
         [IN_SMEM, ANYWHERE, ANYWHERE],
-        pltpu.VMEM((2 * rows, n * block), data.dtype),
-        IN_VMEM,
+        [
+            pltpu.VMEM((2 * rows, n * block), data.dtype),
+            jax.ShapeDtypeStruct((8, 128), jnp.float32),
+        ],
+        [IN_VMEM, IN_VMEM],
         [pltpu.SemaphoreType.DMA((2, n))],
         0,
         n * rows * block * 8,
     )
 
 
-def part_dots(start, groups, held, before, last):
-    sizes = [g[0].shape[0] for g in groups]
-    rows = sum(p.shape[1] for p in groups[0])
-    block = groups[0][0].shape[2]
+def part_dots(start, groups, held, before, side=None):
+    rows, block = groups[0].shape[1:]
     both = held.shape[0]
-    inner = both // 2
-    parts = [p for g in groups for p in g]
-    per = len(groups[0])
-    height = rows // per
-    spots = [(a, i) for a, size in enumerate(sizes) for i in range(size)]
+    mine = slice(0, both)
+    if side is not None:
+        mine = slice(side * both // 2, (side + 1) * both // 2)
+    width = mine.stop - mine.start
+    spots = [(a, i) for a, g in enumerate(groups) for i in range(g.shape[0])]
 
     def kernel(*refs):
-        pieces, (held_ref, *rest) = refs[: len(parts)], refs[len(parts) :]
-        for p in range(per):
-            here = pl.ds(p * height, height)
-            total = None if before is None else rest[0][here]
-            for t, (a, i) in enumerate(spots):
-                part = lax.dot_general(
-                    pieces[a * per + p][i],
-                    held_ref[:, (start + t) * block : (start + t + 1) * block],
-                    (((1,), (1,)), ((), ())),
-                    preferred_element_type=jnp.float32,
-                )
-                total = part if total is None else total + part
-            if last:
-                rest[-2][here] = total[:, :inner]
-                rest[-1][here] = total[:, inner:]
-            else:
-                rest[-1][here] = total
-
-    ins = parts + [held] + ([] if before is None else [before])
-    half = jax.ShapeDtypeStruct((rows, inner), jnp.float32)
-    outs = [half, half] if last else [jax.ShapeDtypeStruct((rows, both), jnp.float32)]
-    got = call(
+        pieces, (held_ref, *rest) = refs[: len(groups)], refs[len(groups) :]
+        total = None if before is None else rest[0][:, mine]
+        for t, (a, i) in enumerate(spots):
+            part = lax.dot_general(
+                pieces[a][i],
+                held_ref[mine, (start + t) * block : (start + t + 1) * block],
+                (((1,), (1,)), ((), ())),
+                preferred_element_type=jnp.float32,
+            )
+            total = part if total is None else total + part
+        rest[-1][...] = total
+
+    ins = groups + [held] + ([] if before is None else [before])
+    return call(
         kernel,
         ins,
         [IN_VMEM] * len(ins),
-        outs,
-        [IN_VMEM] * len(outs),
+        jax.ShapeDtypeStruct((rows, width), jnp.float32),
+        IN_VMEM,
         [],
-        len(spots) * 2 * rows * both * block,
-        len(spots) * block * 2 * (both + rows),
-    )
-    return got if len(got) > 1 else got[0]
+        len(spots) * 2 * rows * width * block,
+        len(spots) * block * 2 * (width + rows),
+    )
 
 
 def gathered_dots(noise, held, sq_data):
-    half = noise.shape[0] // 2
     along = [hop(noise, -k, True) for k in OFFS] + [noise]
-    top = jnp.stack([block[:half] for block in along])
-    bottom = jnp.stack([block[half:] for block in along])
-    top, bottom, sq_data = lax.optimization_barrier((top, bottom, sq_data))
-    up_top, down_bottom = hop(top, -1, False), hop(bottom, 1, False)
-    up_bottom, down_top = hop(bottom, -1, False), hop(top, 1, False)
-    groups = [[block[None]] for block in along]
-    dots = part_dots(0, groups, held, None, False)
-    up_top, down_bottom, dots = lax.optimization_barrier((up_top, down_bottom, dots))
-    far = [hop(up_top, -1, False), hop(down_bottom, 1, False)]
-    groups = [[up_top, up_bottom], [down_top, down_bottom]]
-    dots = part_dots(4, groups, held, dots, False)
-    own, other = part_dots(12, [far], held, dots, True)
-    return own + swap(other), sq_data
+    one, two = jnp.stack(along[:2]), jnp.stack(along[2:])
+    one, two, sq_data = lax.optimization_barrier((one, two, sq_data))
+    up_one, down_two = hop(one, -1, False), hop(two, 1, False)
+    up_two, down_one = hop(two, -1, False), hop(one, 1, False)
+    dots = part_dots(0, [one, two], held, None)
+    up_one, down_two, dots = lax.optimization_barrier((up_one, down_two, dots))
+    far = [hop(up_one, -1, False), hop(down_two, 1, False)]
+    dots = part_dots(4, [up_one, up_two, down_one, down_two], held, dots)
+    other = swap(part_dots(12, far, held, dots, 1))
+    return part_dots(12, far, held, dots, 0) + other, sq_data
 
 
 def part_sums(start, groups, ins, ids, ready=None, step=2):
@@ -200,7 +189,7 @@
     half = rows // 2
     ends = [sum(groups[: a + 1]) for a in range(len(groups))]
     count = ends[-1]
-    sources = [data, data_other] if ready is None else [ready]
+    sources = [data, data_other] if ready is None else ready
 
     def kernel(ids_ref, w_own_ref, w_oth_ref, *refs):
         refs, outs, scratch = (
@@ -220,7 +209,7 @@
                 for copy in copies:
                     copy.start()
         else:
-            (held,) = refs
+            held, _ = refs
         weights[:, :inner] = w_own_ref[...]
         weights[:, inner:] = w_oth_ref[...]
         ones = jnp.ones((EXTRA, 2 * inner), dtype)
@@ -280,7 +269,7 @@
         kernel,
         [ids, w_own, w_oth] + sources,
         [IN_SMEM, IN_VMEM, IN_VMEM]
-        + ([ANYWHERE] * 2 if ready is None else [IN_VMEM]),
+        + [ANYWHERE if ready is None else IN_VMEM] * 2,
         shapes,
         [ANYWHERE] * len(shapes),
         scratch,
@@ -343,7 +332,7 @@
     y = place // (2 * SIDE)
     ids = block_ids(y, z, core)
     data_other = swap(data_latents)
-    held = held_blocks(ids, 0, BLOCKS, data_latents, data_other)
+    held, _ = held_blocks(ids, 0, BLOCKS, data_latents, data_other)
     noise_f = noise_latents.astype(jnp.float32)
     sx_part = jnp.sum(noise_f * noise_f, axis=1)
     data_f = data_latents.astype(jnp.float32)
@@ -366,12 +355,15 @@
         local = lse(twice + (f - sx)[:, None], 0)
         if step == ITERS - 1:
             local, ids = lax.optimization_barrier((local, ids))
-        g = sy - lse(to_all_noise(local), 0)
+        got = to_all_noise(local)
+        if step == ITERS - 1:
+            ready, mark = held_blocks(ids, 12, 4, data_latents, data_other)
+            got, mark = lax.optimization_barrier((got, mark))
+        g = sy - lse(got, 0)
     coupling = jnp.exp(twice + (f - sx)[:, None] + (g - sy)[None, :])
     weights = coupling.astype(jnp.bfloat16)
-    ready = held_blocks(ids, 12, 4, data_latents, data_other)
     means = scattered_sums(
-        (weights, swap(weights), data_latents, data_other), ids, ready
+        (weights, swap(weights), data_latents, data_other), ids, [ready, mark]
     )
     return means.astype(jnp.bfloat16)
 

time: 164 us -> 161 us (0.982)
    ppermute x9, waiting for transfers between devices: 6.85 us -> 4.53 us  [to_all_noise(): lax.ppermute(values, 'noise', [(i, (i + k) % n) for i in range(n)])]
    pallas_call x8 -> x9, Pallas kernels: 30.5 us -> 29.3 us  [call(): pl.pallas_call(kernel, in_specs=in_specs, out_specs=out_specs, out_shape=...]
  transfers between devices with their start and end apart: 32 -> 32, of which waited for: 21 -> 19; matrix products, arithmetic and copies ran while one was open for 6% -> 5% of each run, Pallas kernels for 16% -> 16%
where the time goes in v8:
time: 161 us
  starting transfers between devices  42 us (26%)
  waiting for transfers between devices  41.3 us (26%)
  blocking collectives  33.4 us (21%)
  Pallas kernels  29.3 us (18%)
  other arithmetic  13.8 us (9%)
    ppermute x20, waiting for transfers between devices, hop(): return lax.ppermute(values, 'dp', pairs)  34.4 us
    all_to_all x3, blocking collectives, to_all_dp(): lax.all_to_all(jnp.broadcast_to(values[None], (n,) + values.shape), 'dp',...  33.4 us
    pallas_call x9, Pallas kernels, call(): pl.pallas_call(kernel, in_specs=in_specs, out_specs=out_specs, out_shape=...  29.3 us
    ppermute x20, starting transfers between devices, hop(): return lax.ppermute(values, 'dp', pairs)  26.6 us
    ppermute x9, starting transfers between devices, to_all_noise(): lax.ppermute(values, 'noise', [(i, (i + k) % n) for i in range(n)])  15.1 us
    reduce_sum x1, other arithmetic, body(): sq_data = jnp.sum(data_f * data_f, axis=1)  7.14 us
    ppermute x9, waiting for transfers between devices, to_all_noise(): lax.ppermute(values, 'noise', [(i, (i + k) % n) for i in range(n)])  4.53 us
  transfers between devices with their start and end apart: 32, of which 19 were waited for; matrix products, arithmetic and copies ran while one was open for 5% of the time, Pallas kernels for 16%

profile of v8, /device:TPU:0, one launch (start us, length us, event | category | flops | bytes accessed | tf_op | source)
XLA Modules:
  0.0 160.6 jit_solution(1280181195102002877)
XLA Ops:
  0.0 4.0 %collective-permute-start = (bf16[384,512]{1,0:T(8,128)(2,1)}, bf16[384,512]{1,0:T(8,128)(2,1)S(1)}, u32[]{:S(2)}, u32[]{:S(2)}) collective-permute-start(bf16[384,512]{1,0:T(8,128)(2,1)} %param.2), channel_id=1, source_target_pairs={{0,16},{4,68},{8,24},{12,76},{16,0},{20,84},{24,8},{28,92},{32,48}... | collective-permute-start | bytes 1179656 | tf_op jit(solution)/shard_map/ppermute | solution.py:32
  6.0 7.1 %multiply_reduce_fusion = f32[384]{0:T(512)S(1)} fusion(bf16[384,16384]{1,0:T(8,128)(2,1)} %refs_0_.3), kind=kLoop, calls=%fused_computation | loop fusion | flops 18873984 | bytes 12584448 | tf_op jit(solution)/shard_map/reduce_sum | solution.py:339
  13.1 2.1 %collective-permute-done.1 = bf16[384,512]{1,0:T(8,128)(2,1)S(1)} collective-permute-done((bf16[384,512]{1,0:T(8,128)(2,1)}, bf16[384,512]{1,0:T(8,128)(2,1)S(1)}, u32[]{:S(2)}, u32[]{:S(2)}) %collective-permute-start.1) | collective-permute-done | bytes 393248 | tf_op jit(solution)/shard_map/ppermute | solution.py:32
  15.4 3.1 %collective-permute-start.3 = (bf16[2,384,512]{2,1,0:T(8,128)(2,1)S(1)}, bf16[2,384,512]{2,1,0:T(8,128)(2,1)S(1)}, u32[]{:S(2)}, u32[]{:S(2)}) collective-permute-start(bf16[2,384,512]{2,1,0:T(8,128)(2,1)S(1)} %pad_maximum_fusion.refs_0_), channel_id=1, source_target_pairs={{0,96},{4,28},{8,104},{12,4},{16,112},{20,12},{24,120},{28,20},{32... | collective-permute-start | bytes 2359304 | tf_op jit(solution)/shard_map/ppermute | solution.py:32
  18.5 3.2 %collective-permute-start.8 = (bf16[2,384,512]{2,1,0:T(8,128)(2,1)S(1)}, bf16[2,384,512]{2,1,0:T(8,128)(2,1)}, u32[]{:S(2)}, u32[]{:S(2)}) collective-permute-start(bf16[2,384,512]{2,1,0:T(8,128)(2,1)S(1)} %pad_maximum_fusion.1.refs_1_), channel_id=1, source_target_pairs={{0,96},{4,28},{8,104},{12,4},{16,112},{20,12},{24,120},{28,20},{32... | collective-permute-start | bytes 2359304 | tf_op jit(solution)/shard_map/ppermute | solution.py:32
  21.8 6.2 %shard_map.28 = (bf16[768,8192]{1,0:T(8,128)(2,1)S(1)}, f32[8,128]{1,0:T(8,128)}) custom-call(s32[16]{0:T(128)S(1)} %stack.139.ids_ref, bf16[384,16384]{1,0:T(8,128)(2,1)} %refs_0_.3, bf16[384,16384]{1,0:T(8,128)(2,1)} %collective-permute-done.5.data_other_ref.refs_1_), custom_call_target="tpu_custom_call" | custom-call | bytes 25165824 | tf_op jit(solution)/shard_map/pallas_call | solution.py:68
  29.5 2.2 %collective-permute-done.4.refs_3_ = bf16[2,384,512]{2,1,0:T(8,128)(2,1)S(1)} collective-permute-done((bf16[2,384,512]{2,1,0:T(8,128)(2,1)S(1)}, bf16[2,384,512]{2,1,0:T(8,128)(2,1)S(1)}, u32[]{:S(2)}, u32[]{:S(2)}) %collective-permute-start.4) | collective-permute-done | bytes 786464 | tf_op jit(solution)/shard_map/ppermute | solution.py:32
  33.7 2.7 %collective-permute-done.8.refs_1_ = bf16[2,384,512]{2,1,0:T(8,128)(2,1)} collective-permute-done((bf16[2,384,512]{2,1,0:T(8,128)(2,1)S(1)}, bf16[2,384,512]{2,1,0:T(8,128)(2,1)}, u32[]{:S(2)}, u32[]{:S(2)}) %collective-permute-start.8) | collective-permute-done | bytes 786464 | tf_op jit(solution)/shard_map/ppermute | solution.py:32
  36.4 3.8 %collective-permute-done.9.refs_2_ = bf16[2,384,512]{2,1,0:T(8,128)(2,1)} collective-permute-done((bf16[2,384,512]{2,1,0:T(8,128)(2,1)S(1)}, bf16[2,384,512]{2,1,0:T(8,128)(2,1)}, u32[]{:S(2)}, u32[]{:S(2)}) %collective-permute-start.9) | collective-permute-done | bytes 786464 | tf_op jit(solution)/shard_map/ppermute | solution.py:32
  40.2 4.0 %shard_map.30.refs_3_ = f32[384,768]{1,0:T(8,128)S(1)} custom-call(bf16[2,384,512]{2,1,0:T(8,128)(2,1)S(1)} %collective-permute-done.3.refs_0_, bf16[2,384,512]{2,1,0:T(8,128)(2,1)} %collective-permute-done.8.refs_1_, bf16[2,384,512]{2,1,0:T(8,128)(2,1)} %collective-permute-done.9.refs_2_, bf16[2,384,512]{2,1,0:T(8,128)(2,1)S(1)} %collective-permute-done.4.refs_3_, ...), custom_call_target="tpu_custom_call" | custom-call | flops 2415919104 | bytes 9437184 | tf_op jit(solution)/shard_map/pallas_call | solution.py:68
  44.8 3.7 %collective-permute-done.7.refs_1_ = bf16[2,384,512]{2,1,0:T(8,128)(2,1)S(1)} collective-permute-done((bf16[2,384,512]{2,1,0:T(8,128)(2,1)S(1)}, bf16[2,384,512]{2,1,0:T(8,128)(2,1)S(1)}, u32[]{:S(2)}, u32[]{:S(2)}) %collective-permute-start.7) | collective-permute-done | bytes 786464 | tf_op jit(solution)/shard_map/ppermute | solution.py:32
  52.3 11.7 %all_to_all.23 = f32[32,2,384]{2,1,0:T(2,128)S(1)} all-to-all(f32[32,2,384]{2,1,0:T(2,128)S(1)} %broadcast_in_dim.9), channel_id=1, replica_groups=mesh['dp'=32,'noise'=4] {'dp'}, dimensions={0} | all-to-all | bytes 196608 | tf_op jit(solution)/shard_map/all_to_all | solution.py:52
  64.5 3.1 %collective-permute-start.11 = (f32[384]{0:T(512)S(1)}, f32[384]{0:T(512)S(1)}, u32[]{:S(2)}, u32[]{:S(2)}) collective-permute-start(f32[384]{0:T(512)S(1)} %log_add_fusion.4), channel_id=1, source_target_pairs={{0,2},{1,3},{2,0},{3,1},{4,6},{5,7},{6,4},{7,5},{8,10},{9,11},{10,... | collective-permute-start | bytes 4616 | tf_op jit(solution)/shard_map/ppermute | solution.py:62
  68.2 2.6 %collective-permute-start.13 = (f32[384]{0:T(512)S(1)}, f32[384]{0:T(512)S(1)}, u32[]{:S(2)}, u32[]{:S(2)}) collective-permute-start(f32[384]{0:T(512)S(1)} %log_add_fusion.4), channel_id=1, source_target_pairs={{0,3},{1,0},{2,1},{3,2},{4,7},{5,4},{6,5},{7,6},{8,11},{9,8},{10,9... | collective-permute-start | bytes 4616 | tf_op jit(solution)/shard_map/ppermute | solution.py:62
  70.8 1.5 collective-permute-done.12
  72.9 10.9 %all_to_all.24 = f32[32,1,384]{2,1,0:T(1,128)S(1)} all-to-all(f32[32,1,384]{2,1,0:T(1,128)S(1)} %broadcast_in_dim.10), channel_id=1, replica_groups=mesh['dp'=32,'noise'=4] {'dp'}, dimensions={0} | all-to-all | bytes 98304 | tf_op jit(solution)/shard_map/all_to_all | solution.py:52
  84.3 1.5 collective-permute-start.14
  85.8 2.6 %collective-permute-start.15 = (f32[384]{0:T(512)S(1)}, f32[384]{0:T(512)S(1)}, u32[]{:S(2)}, u32[]{:S(2)}) collective-permute-start(f32[384]{0:T(512)S(1)} %log_add_fusion.2), channel_id=1, source_target_pairs={{0,1},{1,2},{2,3},{3,0},{4,5},{5,6},{6,7},{7,4},{8,9},{9,10},{10,1... | collective-permute-start | bytes 4616 | tf_op jit(solution)/shard_map/ppermute | solution.py:62
  92.5 10.8 %all_to_all.25 = f32[32,1,384]{2,1,0:T(1,128)S(1)} all-to-all(f32[32,1,384]{2,1,0:T(1,128)S(1)} %broadcast_in_dim.11), channel_id=1, replica_groups=mesh['dp'=32,'noise'=4] {'dp'}, dimensions={0} | all-to-all | bytes 98304 | tf_op jit(solution)/shard_map/all_to_all | solution.py:52
  104.6 2.0 %collective-permute-start.18 = (f32[384]{0:T(512)S(1)}, f32[384]{0:T(512)S(1)}, u32[]{:S(2)}, u32[]{:S(2)}) collective-permute-start(f32[384]{0:T(512)S(1)} %log_add_fusion), channel_id=1, source_target_pairs={{0,1},{1,2},{2,3},{3,0},{4,5},{5,6},{6,7},{7,4},{8,9},{9,10},{10,1... | collective-permute-start | bytes 4616 | tf_op jit(solution)/shard_map/ppermute | solution.py:62
  107.8 2.5 %shard_map.33 = (bf16[768,2048]{1,0:T(8,128)(2,1)S(1)}, f32[8,128]{1,0:T(8,128)S(1)}) custom-call(s32[16]{0:T(128)S(1)} %stack.139.ids_ref, bf16[384,16384]{1,0:T(8,128)(2,1)} %refs_0_.3, bf16[384,16384]{1,0:T(8,128)(2,1)} %collective-permute-done.5.data_other_ref.refs_1_), custom_call_target="tpu_custom_call" | custom-call | bytes 6291456 | tf_op jit(solution)/shard_map/pallas_call | solution.py:68
  111.8 1.6 collective-permute-done.20.w_oth_ref
  113.3 2.3 %shard_map.34 = (bf16[4,208,512]{2,1,0:T(8,128)(2,1)S(1)}, bf16[4,192,512]{2,1,0:T(8,128)(2,1)S(1)}) custom-call(s32[16]{0:T(128)S(1)} %stack.139.ids_ref, bf16[384,384]{1,0:T(8,128)(2,1)S(1)} %exponential_convert_fusion.w_own_ref, bf16[384,384]{1,0:T(8,128)(2,1)S(1)} %collective-permute-done.20.w_oth_ref, bf16[768,2048]{1,0:T(8,128)(2,1)S(1)} %get-tuple-element.47.refs_0_, ...), custom_call_target="tpu_custom_call" | custom-call | flops 1207959552 | bytes 4718592 | tf_op jit(solution)/shard_map/pallas_call | solution.py:68
  117.7 7.1 %shard_map.35 = (bf16[3,208,512]{2,1,0:T(8,128)(2,1)S(1)}, bf16[3,192,512]{2,1,0:T(8,128)(2,1)S(1)}, bf16[1,208,512]{2,1,0:T(8,128)(2,1)S(1)}, bf16[1,192,512]{2...) custom-call(s32[16]{0:T(128)S(1)} %stack.139.ids_ref, ...), custom_call_target="tpu_custom_call" | custom-call | flops 2415919104 | bytes 9437184 | tf_op jit(solution)/shard_map/pallas_call | solution.py:68
  124.8 2.4 %collective-permute-start.25 = (bf16[3,208,512]{2,1,0:T(8,128)(2,1)S(1)}, bf16[3,208,512]{2,1,0:T(8,128)(2,1)S(1)}, u32[]{:S(2)}, u32[]{:S(2)}) collective-permute-start(bf16[3,208,512]{2,1,0:T(8,128)(2,1)S(1)} %get-tuple-element.63), channel_id=1, source_target_pairs={{0,96},{4,28},{8,104},{12,4},{16,112},{20,12},{24,120},{28,20},{32... | collective-permute-start | bytes 1916936 | tf_op jit(solution)/shard_map/ppermute | solution.py:32
  127.9 2.8 %collective-permute-done.21 = bf16[4,208,512]{2,1,0:T(8,128)(2,1)S(1)} collective-permute-done((bf16[4,208,512]{2,1,0:T(8,128)(2,1)S(1)}, bf16[4,208,512]{2,1,0:T(8,128)(2,1)S(1)}, u32[]{:S(2)}, u32[]{:S(2)}) %collective-permute-start.21) | collective-permute-done | bytes 852000 | tf_op jit(solution)/shard_map/ppermute | solution.py:32
  133.2 3.9 %shard_map.36 = (bf16[4,208,512]{2,1,0:T(8,128)(2,1)S(1)}, bf16[4,192,512]{2,1,0:T(8,128)(2,1)S(1)}) custom-call(s32[16]{0:T(128)S(1)} %stack.139.ids_ref, bf16[384,384]{1,0:T(8,128)(2,1)S(1)} %exponential_convert_fusion.w_own_ref, bf16[384,384]{1,0:T(8,128)(2,1)S(1)} %collective-permute-done.20.w_oth_ref, bf16[384,16384]{1,0:T(8,128)(2,1)} %refs_0_.3, ...), custom_call_target="tpu_custom_call" | custom-call | flops 1207959552 | bytes 4718592 | tf_op jit(solution)/shard_map/pallas_call | solution.py:68
  139.2 2.4 %collective-permute-done.28 = bf16[3,192,512]{2,1,0:T(8,128)(2,1)S(1)} collective-permute-done((bf16[3,192,512]{2,1,0:T(8,128)(2,1)S(1)}, bf16[3,192,512]{2,1,0:T(8,128)(2,1)S(1)}, u32[]{:S(2)}, u32[]{:S(2)}) %collective-permute-start.28) | collective-permute-done | bytes 589856 | tf_op jit(solution)/shard_map/ppermute | solution.py:32
  141.8 3.3 %collective-permute-done.26 = bf16[3,208,512]{2,1,0:T(8,128)(2,1)S(1)} collective-permute-done((bf16[3,208,512]{2,1,0:T(8,128)(2,1)S(1)}, bf16[3,208,512]{2,1,0:T(8,128)(2,1)S(1)}, u32[]{:S(2)}, u32[]{:S(2)}) %collective-permute-start.26) | collective-permute-done | bytes 639008 | tf_op jit(solution)/shard_map/ppermute | solution.py:32
  147.7 2.4 %collective-permute-start.31 = (bf16[400,512]{1,0:T(8,128)(2,1)S(1)}, bf16[400,512]{1,0:T(8,128)(2,1)S(1)}, u32[]{:S(2)}, u32[]{:S(2)}) collective-permute-start(bf16[400,512]{1,0:T(8,128)(2,1)S(1)} %pad_maximum_fusion.6), channel_id=1, source_target_pairs={{0,24},{4,100},{8,0},{12,108},{16,8},{20,116},{24,16},{28,124},{32... | collective-permute-start | bytes 1228808 | tf_op jit(solution)/shard_map/ppermute | solution.py:32
  150.1 5.1 %collective-permute-done.23 = bf16[400,512]{1,0:T(8,128)(2,1)S(1)} collective-permute-done((bf16[400,512]{1,0:T(8,128)(2,1)S(1)}, bf16[400,512]{1,0:T(8,128)(2,1)S(1)}, u32[]{:S(2)}, u32[]{:S(2)}) %collective-permute-start.23) | collective-permute-done | bytes 409632 | tf_op jit(solution)/shard_map/ppermute | solution.py:32
  155.2 4.2 %collective-permute-done.30 = bf16[400,512]{1,0:T(8,128)(2,1)S(1)} collective-permute-done((bf16[400,512]{1,0:T(8,128)(2,1)S(1)}, bf16[400,512]{1,0:T(8,128)(2,1)S(1)}, u32[]{:S(2)}, u32[]{:S(2)}) %collective-permute-start.30) | collective-permute-done | bytes 409632 | tf_op jit(solution)/shard_map/ppermute | solution.py:32
  (127 shorter events, 31.5 us)
Async XLA Ops:
  0.0 21.8 %collective-permute-start.5 = (bf16[384,16384]{1,0:T(8,128)(2,1)}, bf16[384,16384]{1,0:T(8,128)(2,1)}, u32[]{:S(2)}, u32[]{:S(2)}) collective-permute-start(bf16[384,16384]{1,0:T(8,128)(2,1)} %refs_0_.3), channel_id=1, source_target_pairs={{0,4},{4,0},{8,12},{12,8},{16,20},{20,16},{24,28},{28,24},{32,36},... | collective-permute-start | bytes 37748744 | tf_op jit(solution)/shard_map/ppermute | solution.py:21
  0.0 13.1 %collective-permute-start = (bf16[384,512]{1,0:T(8,128)(2,1)}, bf16[384,512]{1,0:T(8,128)(2,1)S(1)}, u32[]{:S(2)}, u32[]{:S(2)}) collective-permute-start(bf16[384,512]{1,0:T(8,128)(2,1)} %param.2), channel_id=1, source_target_pairs={{0,16},{4,68},{8,24},{12,76},{16,0},{20,84},{24,8},{28,92},{32,48}... | collective-permute-start | bytes 1179656 | tf_op jit(solution)/shard_map/ppermute | solution.py:32
  4.0 11.2 %collective-permute-start.1 = (bf16[384,512]{1,0:T(8,128)(2,1)}, bf16[384,512]{1,0:T(8,128)(2,1)S(1)}, u32[]{:S(2)}, u32[]{:S(2)}) collective-permute-start(bf16[384,512]{1,0:T(8,128)(2,1)} %param.2), channel_id=1, source_target_pairs={{0,24},{4,100},{8,0},{12,108},{16,8},{20,116},{24,16},{28,124},{32... | collective-permute-start | bytes 1179656 | tf_op jit(solution)/shard_map/ppermute | solution.py:32
  4.7 10.6 %collective-permute-start.2 = (bf16[384,512]{1,0:T(8,128)(2,1)}, bf16[384,512]{1,0:T(8,128)(2,1)S(1)}, u32[]{:S(2)}, u32[]{:S(2)}) collective-permute-start(bf16[384,512]{1,0:T(8,128)(2,1)} %param.2), channel_id=1, source_target_pairs={{0,8},{4,36},{8,16},{12,44},{16,24},{20,52},{24,0},{28,60},{32,40}... | collective-permute-start | bytes 1179656 | tf_op jit(solution)/shard_map/ppermute | solution.py:32
  15.4 14.1 %collective-permute-start.3 = (bf16[2,384,512]{2,1,0:T(8,128)(2,1)S(1)}, bf16[2,384,512]{2,1,0:T(8,128)(2,1)S(1)}, u32[]{:S(2)}, u32[]{:S(2)}) collective-permute-start(bf16[2,384,512]{2,1,0:T(8,128)(2,1)S(1)} %pad_maximum_fusion.refs_0_), channel_id=1, source_target_pairs={{0,96},{4,28},{8,104},{12,4},{16,112},{20,12},{24,120},{28,20},{32... | collective-permute-start | bytes 2359304 | tf_op jit(solution)/shard_map/ppermute | solution.py:32
  18.5 13.2 %collective-permute-start.4 = (bf16[2,384,512]{2,1,0:T(8,128)(2,1)S(1)}, bf16[2,384,512]{2,1,0:T(8,128)(2,1)S(1)}, u32[]{:S(2)}, u32[]{:S(2)}) collective-permute-start(bf16[2,384,512]{2,1,0:T(8,128)(2,1)S(1)} %pad_maximum_fusion.1.refs_1_), channel_id=1, source_target_pairs={{0,32},{4,12},{8,40},{12,20},{16,48},{20,28},{24,56},{28,4},{32,64... | collective-permute-start | bytes 2359304 | tf_op jit(solution)/shard_map/ppermute | solution.py:32
  18.5 17.9 %collective-permute-start.8 = (bf16[2,384,512]{2,1,0:T(8,128)(2,1)S(1)}, bf16[2,384,512]{2,1,0:T(8,128)(2,1)}, u32[]{:S(2)}, u32[]{:S(2)}) collective-permute-start(bf16[2,384,512]{2,1,0:T(8,128)(2,1)S(1)} %pad_maximum_fusion.1.refs_1_), channel_id=1, source_target_pairs={{0,96},{4,28},{8,104},{12,4},{16,112},{20,12},{24,120},{28,20},{32... | collective-permute-start | bytes 2359304 | tf_op jit(solution)/shard_map/ppermute | solution.py:32
  21.7 18.5 %collective-permute-start.9 = (bf16[2,384,512]{2,1,0:T(8,128)(2,1)S(1)}, bf16[2,384,512]{2,1,0:T(8,128)(2,1)}, u32[]{:S(2)}, u32[]{:S(2)}) collective-permute-start(bf16[2,384,512]{2,1,0:T(8,128)(2,1)S(1)} %pad_maximum_fusion.refs_0_), channel_id=1, source_target_pairs={{0,32},{4,12},{8,40},{12,20},{16,48},{20,28},{24,56},{28,4},{32,64... | collective-permute-start | bytes 2359304 | tf_op jit(solution)/shard_map/ppermute | solution.py:32
  31.7 13.2 %collective-permute-start.6 = (bf16[2,384,512]{2,1,0:T(8,128)(2,1)S(1)}, bf16[2,384,512]{2,1,0:T(8,128)(2,1)S(1)}, u32[]{:S(2)}, u32[]{:S(2)}) collective-permute-start(bf16[2,384,512]{2,1,0:T(8,128)(2,1)S(1)} %collective-permute-done.3.refs_0_), channel_id=1, source_target_pairs={{0,96},{4,28},{8,104},{12,4},{16,112},{20,12},{24,120},{28,20},{32... | collective-permute-start | bytes 2359304 | tf_op jit(solution)/shard_map/ppermute | solution.py:32
  32.8 15.7 %collective-permute-start.7 = (bf16[2,384,512]{2,1,0:T(8,128)(2,1)S(1)}, bf16[2,384,512]{2,1,0:T(8,128)(2,1)S(1)}, u32[]{:S(2)}, u32[]{:S(2)}) collective-permute-start(bf16[2,384,512]{2,1,0:T(8,128)(2,1)S(1)} %collective-permute-done.4.refs_3_), channel_id=1, source_target_pairs={{0,32},{4,12},{8,40},{12,20},{16,48},{20,28},{24,56},{28,4},{32,64... | collective-permute-start | bytes 2359304 | tf_op jit(solution)/shard_map/ppermute | solution.py:32
  49.5 2.3 %collective-permute-start.10 = (f32[384,384]{1,0:T(8,128)S(1)}, f32[384,384]{1,0:T(8,128)S(1)}, u32[]{:S(2)}, u32[]{:S(2)}) collective-permute-start(f32[384,384]{1,0:T(8,128)S(1)} %shard_map.32), channel_id=1, source_target_pairs={{0,4},{4,0},{8,12},{12,8},{16,20},{20,16},{24,28},{28,24},{32,36},... | collective-permute-start | bytes 1769480 | tf_op jit(solution)/shard_map/ppermute | solution.py:21
  64.5 6.3 %collective-permute-start.11 = (f32[384]{0:T(512)S(1)}, f32[384]{0:T(512)S(1)}, u32[]{:S(2)}, u32[]{:S(2)}) collective-permute-start(f32[384]{0:T(512)S(1)} %log_add_fusion.4), channel_id=1, source_target_pairs={{0,2},{1,3},{2,0},{3,1},{4,6},{5,7},{6,4},{7,5},{8,10},{9,11},{10,... | collective-permute-start | bytes 4616 | tf_op jit(solution)/shard_map/ppermute | solution.py:62
  67.6 4.8 %collective-permute-start.12 = (f32[384]{0:T(512)S(1)}, f32[384]{0:T(512)S(1)}, u32[]{:S(2)}, u32[]{:S(2)}) collective-permute-start(f32[384]{0:T(512)S(1)} %log_add_fusion.4), channel_id=1, source_target_pairs={{0,1},{1,2},{2,3},{3,0},{4,5},{5,6},{6,7},{7,4},{8,9},{9,10},{10,1... | collective-permute-start | bytes 4616 | tf_op jit(solution)/shard_map/ppermute | solution.py:62
  68.2 4.2 %collective-permute-start.13 = (f32[384]{0:T(512)S(1)}, f32[384]{0:T(512)S(1)}, u32[]{:S(2)}, u32[]{:S(2)}) collective-permute-start(f32[384]{0:T(512)S(1)} %log_add_fusion.4), channel_id=1, source_target_pairs={{0,3},{1,0},{2,1},{3,2},{4,7},{5,4},{6,5},{7,6},{8,11},{9,8},{10,9... | collective-permute-start | bytes 4616 | tf_op jit(solution)/shard_map/ppermute | solution.py:62
  84.3 5.2 %collective-permute-start.14 = (f32[384]{0:T(512)S(1)}, f32[384]{0:T(512)S(1)}, u32[]{:S(2)}, u32[]{:S(2)}) collective-permute-start(f32[384]{0:T(512)S(1)} %log_add_fusion.2), channel_id=1, source_target_pairs={{0,2},{1,3},{2,0},{3,1},{4,6},{5,7},{6,4},{7,5},{8,10},{9,11},{10,... | collective-permute-start | bytes 4616 | tf_op jit(solution)/shard_map/ppermute | solution.py:62
  85.8 4.8 %collective-permute-start.15 = (f32[384]{0:T(512)S(1)}, f32[384]{0:T(512)S(1)}, u32[]{:S(2)}, u32[]{:S(2)}) collective-permute-start(f32[384]{0:T(512)S(1)} %log_add_fusion.2), channel_id=1, source_target_pairs={{0,1},{1,2},{2,3},{3,0},{4,5},{5,6},{6,7},{7,4},{8,9},{9,10},{10,1... | collective-permute-start | bytes 4616 | tf_op jit(solution)/shard_map/ppermute | solution.py:62
  88.4 3.6 %collective-permute-start.16 = (f32[384]{0:T(512)S(1)}, f32[384]{0:T(512)S(1)}, u32[]{:S(2)}, u32[]{:S(2)}) collective-permute-start(f32[384]{0:T(512)S(1)} %log_add_fusion.2), channel_id=1, source_target_pairs={{0,3},{1,0},{2,1},{3,2},{4,7},{5,4},{6,5},{7,6},{8,11},{9,8},{10,9... | collective-permute-start | bytes 4616 | tf_op jit(solution)/shard_map/ppermute | solution.py:62
  103.8 6.5 %collective-permute-start.17 = (f32[384]{0:T(512)S(1)}, f32[384]{0:T(512)S(1)}, u32[]{:S(2)}, u32[]{:S(2)}) collective-permute-start(f32[384]{0:T(512)S(1)} %log_add_fusion), channel_id=1, source_target_pairs={{0,2},{1,3},{2,0},{3,1},{4,6},{5,7},{6,4},{7,5},{8,10},{9,11},{10,... | collective-permute-start | bytes 4616 | tf_op jit(solution)/shard_map/ppermute | solution.py:62
  104.6 5.7 %collective-permute-start.18 = (f32[384]{0:T(512)S(1)}, f32[384]{0:T(512)S(1)}, u32[]{:S(2)}, u32[]{:S(2)}) collective-permute-start(f32[384]{0:T(512)S(1)} %log_add_fusion), channel_id=1, source_target_pairs={{0,1},{1,2},{2,3},{3,0},{4,5},{5,6},{6,7},{7,4},{8,9},{9,10},{10,1... | collective-permute-start | bytes 4616 | tf_op jit(solution)/shard_map/ppermute | solution.py:62
  106.6 3.8 %collective-permute-start.19 = (f32[384]{0:T(512)S(1)}, f32[384]{0:T(512)S(1)}, u32[]{:S(2)}, u32[]{:S(2)}) collective-permute-start(f32[384]{0:T(512)S(1)} %log_add_fusion), channel_id=1, source_target_pairs={{0,3},{1,0},{2,1},{3,2},{4,7},{5,4},{6,5},{7,6},{8,11},{9,8},{10,9... | collective-permute-start | bytes 4616 | tf_op jit(solution)/shard_map/ppermute | solution.py:62
  111.7 1.7 %collective-permute-start.20 = (bf16[384,384]{1,0:T(8,128)(2,1)S(1)}, bf16[384,384]{1,0:T(8,128)(2,1)S(1)}, u32[]{:S(2)}, u32[]{:S(2)}) collective-permute-start(bf16[384,384]{1,0:T(8,128)(2,1)S(1)} %exponential_convert_fusion.w_own_ref), channel_id=1, source_target_pairs={{0,4},{4,0},{8,12},{12,8},{16,20},{20,16},{24,28},{28,24},{32,36},... | collective-permute-start | bytes 884744 | tf_op jit(solution)/shard_map/ppermute | solution.py:21
  115.6 12.1 %collective-permute-start.22 = (bf16[4,192,512]{2,1,0:T(8,128)(2,1)S(1)}, bf16[4,192,512]{2,1,0:T(8,128)(2,1)S(1)}, u32[]{:S(2)}, u32[]{:S(2)}) collective-permute-start(bf16[4,192,512]{2,1,0:T(8,128)(2,1)S(1)} %get-tuple-element.55), channel_id=1, source_target_pairs={{0,96},{4,28},{8,104},{12,4},{16,112},{20,12},{24,120},{28,20},{32... | collective-permute-start | bytes 2359304 | tf_op jit(solution)/shard_map/ppermute | solution.py:32
  116.8 13.9 %collective-permute-start.21 = (bf16[4,208,512]{2,1,0:T(8,128)(2,1)S(1)}, bf16[4,208,512]{2,1,0:T(8,128)(2,1)S(1)}, u32[]{:S(2)}, u32[]{:S(2)}) collective-permute-start(bf16[4,208,512]{2,1,0:T(8,128)(2,1)S(1)} %get-tuple-element.53), channel_id=1, source_target_pairs={{0,32},{4,12},{8,40},{12,20},{16,48},{20,28},{24,56},{28,4},{32,64... | collective-permute-start | bytes 2555912 | tf_op jit(solution)/shard_map/ppermute | solution.py:32
  124.8 17.0 %collective-permute-start.25 = (bf16[3,208,512]{2,1,0:T(8,128)(2,1)S(1)}, bf16[3,208,512]{2,1,0:T(8,128)(2,1)S(1)}, u32[]{:S(2)}, u32[]{:S(2)}) collective-permute-start(bf16[3,208,512]{2,1,0:T(8,128)(2,1)S(1)} %get-tuple-element.63), channel_id=1, source_target_pairs={{0,96},{4,28},{8,104},{12,4},{16,112},{20,12},{24,120},{28,20},{32... | collective-permute-start | bytes 1916936 | tf_op jit(solution)/shard_map/ppermute | solution.py:32
  127.2 11.1 %collective-permute-start.27 = (bf16[3,192,512]{2,1,0:T(8,128)(2,1)S(1)}, bf16[3,192,512]{2,1,0:T(8,128)(2,1)S(1)}, u32[]{:S(2)}, u32[]{:S(2)}) collective-permute-start(bf16[3,192,512]{2,1,0:T(8,128)(2,1)S(1)} %get-tuple-element.65), channel_id=1, source_target_pairs={{0,32},{4,12},{8,40},{12,20},{16,48},{20,28},{24,56},{28,4},{32,64... | collective-permute-start | bytes 1769480 | tf_op jit(solution)/shard_map/ppermute | solution.py:32
  130.9 10.7 %collective-permute-start.28 = (bf16[3,192,512]{2,1,0:T(8,128)(2,1)S(1)}, bf16[3,192,512]{2,1,0:T(8,128)(2,1)S(1)}, u32[]{:S(2)}, u32[]{:S(2)}) collective-permute-start(bf16[3,192,512]{2,1,0:T(8,128)(2,1)S(1)} %add_convert_fusion.1), channel_id=1, source_target_pairs={{0,96},{4,28},{8,104},{12,4},{16,112},{20,12},{24,120},{28,20},{32... | collective-permute-start | bytes 1769480 | tf_op jit(solution)/shard_map/ppermute | solution.py:32
  131.0 19.1 %collective-permute-start.24 = (bf16[400,512]{1,0:T(8,128)(2,1)S(1)}, bf16[400,512]{1,0:T(8,128)(2,1)S(1)}, u32[]{:S(2)}, u32[]{:S(2)}) collective-permute-start(bf16[400,512]{1,0:T(8,128)(2,1)S(1)} %pad_maximum_fusion.3), channel_id=1, source_target_pairs={{0,96},{4,28},{8,104},{12,4},{16,112},{20,12},{24,120},{28,20},{32... | collective-permute-start | bytes 1228808 | tf_op jit(solution)/shard_map/ppermute | solution.py:32
  132.0 13.2 %collective-permute-start.26 = (bf16[3,208,512]{2,1,0:T(8,128)(2,1)S(1)}, bf16[3,208,512]{2,1,0:T(8,128)(2,1)S(1)}, u32[]{:S(2)}, u32[]{:S(2)}) collective-permute-start(bf16[3,208,512]{2,1,0:T(8,128)(2,1)S(1)} %add_convert_fusion), channel_id=1, source_target_pairs={{0,32},{4,12},{8,40},{12,20},{16,48},{20,28},{24,56},{28,4},{32,64... | collective-permute-start | bytes 1916936 | tf_op jit(solution)/shard_map/ppermute | solution.py:32
  138.3 16.9 %collective-permute-start.23 = (bf16[400,512]{1,0:T(8,128)(2,1)S(1)}, bf16[400,512]{1,0:T(8,128)(2,1)S(1)}, u32[]{:S(2)}, u32[]{:S(2)}) collective-permute-start(bf16[400,512]{1,0:T(8,128)(2,1)S(1)} %pad_maximum_fusion.2), channel_id=1, source_target_pairs={{0,32},{4,12},{8,40},{12,20},{16,48},{20,28},{24,56},{28,4},{32,64... | collective-permute-start | bytes 1228808 | tf_op jit(solution)/shard_map/ppermute | solution.py:32
  145.4 9.8 %collective-permute-start.29 = (bf16[400,512]{1,0:T(8,128)(2,1)S(1)}, bf16[400,512]{1,0:T(8,128)(2,1)S(1)}, u32[]{:S(2)}, u32[]{:S(2)}) collective-permute-start(bf16[400,512]{1,0:T(8,128)(2,1)S(1)} %pad_maximum_fusion.4), channel_id=1, source_target_pairs={{0,16},{4,68},{8,24},{12,76},{16,0},{20,84},{24,8},{28,92},{32,48}... | collective-permute-start | bytes 1228808 | tf_op jit(solution)/shard_map/ppermute | solution.py:32
  146.7 12.7 %collective-permute-start.30 = (bf16[400,512]{1,0:T(8,128)(2,1)S(1)}, bf16[400,512]{1,0:T(8,128)(2,1)S(1)}, u32[]{:S(2)}, u32[]{:S(2)}) collective-permute-start(bf16[400,512]{1,0:T(8,128)(2,1)S(1)} %pad_maximum_fusion.5), channel_id=1, source_target_pairs={{0,8},{4,36},{8,16},{12,44},{16,24},{20,52},{24,0},{28,60},{32,40}... | collective-permute-start | bytes 1228808 | tf_op jit(solution)/shard_map/ppermute | solution.py:32
  147.7 11.7 %collective-permute-start.31 = (bf16[400,512]{1,0:T(8,128)(2,1)S(1)}, bf16[400,512]{1,0:T(8,128)(2,1)S(1)}, u32[]{:S(2)}, u32[]{:S(2)}) collective-permute-start(bf16[400,512]{1,0:T(8,128)(2,1)S(1)} %pad_maximum_fusion.6), channel_id=1, source_target_pairs={{0,24},{4,100},{8,0},{12,108},{16,8},{20,116},{24,16},{28,124},{32... | collective-permute-start | bytes 1228808 | tf_op jit(solution)/shard_map/ppermute | solution.py:32
  (2 other events, 54.0 us)

commit v9 on v8

--- a/solution.py
+++ b/solution.py
@@ -352,7 +352,10 @@
         else:
             got = to_all_dp(local)
         f = sx - lse(got, 0)
-        local = lse(twice + (f - sx)[:, None], 0)
+        scores = twice + (f - sx)[:, None]
+        if step == ITERS - 1:
+            scores = lax.optimization_barrier(scores)
+        local = lse(scores, 0)
         if step == ITERS - 1:
             local, ids = lax.optimization_barrier((local, ids))
         got = to_all_noise(local)
@@ -360,7 +363,7 @@
             ready, mark = held_blocks(ids, 12, 4, data_latents, data_other)
             got, mark = lax.optimization_barrier((got, mark))
         g = sy - lse(got, 0)
-    coupling = jnp.exp(twice + (f - sx)[:, None] + (g - sy)[None, :])
+    coupling = jnp.exp(scores + (g - sy)[None, :])
     weights = coupling.astype(jnp.bfloat16)
     means = scattered_sums(
         (weights, swap(weights), data_latents, data_other), ids, [ready, mark]

time: 161 us -> 161 us (level)
  no operation moved by 1% of the time
where the time goes in v9:
time: 161 us
  starting transfers between devices  42 us (26%)
  waiting for transfers between devices  41.3 us (26%)
  blocking collectives  33.4 us (21%)
  Pallas kernels  29.3 us (18%)
  other arithmetic  13.7 us (9%)
    ppermute x20, waiting for transfers between devices, hop(): return lax.ppermute(values, 'dp', pairs)  34.4 us
    all_to_all x3, blocking collectives, to_all_dp(): lax.all_to_all(jnp.broadcast_to(values[None], (n,) + values.shape), 'dp',...  33.4 us
    pallas_call x9, Pallas kernels, call(): pl.pallas_call(kernel, in_specs=in_specs, out_specs=out_specs, out_shape=...  29.3 us
    ppermute x20, starting transfers between devices, hop(): return lax.ppermute(values, 'dp', pairs)  26.6 us
    ppermute x9, starting transfers between devices, to_all_noise(): lax.ppermute(values, 'noise', [(i, (i + k) % n) for i in range(n)])  15.1 us
    reduce_sum x1, other arithmetic, body(): sq_data = jnp.sum(data_f * data_f, axis=1)  7.14 us
    ppermute x9, waiting for transfers between devices, to_all_noise(): lax.ppermute(values, 'noise', [(i, (i + k) % n) for i in range(n)])  4.53 us
  transfers between devices with their start and end apart: 32, of which 19 were waited for; matrix products, arithmetic and copies ran while one was open for 5% of the time, Pallas kernels for 16%

profile of v9, /device:TPU:0, one launch (start us, length us, event | category | flops | bytes accessed | tf_op | source)
XLA Modules:
  0.0 160.5 jit_solution(8214060368820365998)
XLA Ops:
  0.0 4.0 %collective-permute-start = (bf16[384,512]{1,0:T(8,128)(2,1)}, bf16[384,512]{1,0:T(8,128)(2,1)S(1)}, u32[]{:S(2)}, u32[]{:S(2)}) collective-permute-start(bf16[384,512]{1,0:T(8,128)(2,1)} %param.2), channel_id=1, source_target_pairs={{0,16},{4,68},{8,24},{12,76},{16,0},{20,84},{24,8},{28,92},{32,48}... | collective-permute-start | bytes 1179656 | tf_op jit(solution)/shard_map/ppermute | solution.py:32
  6.0 7.1 %multiply_reduce_fusion = f32[384]{0:T(512)S(1)} fusion(bf16[384,16384]{1,0:T(8,128)(2,1)} %refs_0_.3), kind=kLoop, calls=%fused_computation | loop fusion | flops 18873984 | bytes 12584448 | tf_op jit(solution)/shard_map/reduce_sum | solution.py:339
  13.1 2.1 %collective-permute-done.1 = bf16[384,512]{1,0:T(8,128)(2,1)S(1)} collective-permute-done((bf16[384,512]{1,0:T(8,128)(2,1)}, bf16[384,512]{1,0:T(8,128)(2,1)S(1)}, u32[]{:S(2)}, u32[]{:S(2)}) %collective-permute-start.1) | collective-permute-done | bytes 393248 | tf_op jit(solution)/shard_map/ppermute | solution.py:32
  15.4 3.1 %collective-permute-start.3 = (bf16[2,384,512]{2,1,0:T(8,128)(2,1)S(1)}, bf16[2,384,512]{2,1,0:T(8,128)(2,1)S(1)}, u32[]{:S(2)}, u32[]{:S(2)}) collective-permute-start(bf16[2,384,512]{2,1,0:T(8,128)(2,1)S(1)} %pad_maximum_fusion.refs_0_), channel_id=1, source_target_pairs={{0,96},{4,28},{8,104},{12,4},{16,112},{20,12},{24,120},{28,20},{32... | collective-permute-start | bytes 2359304 | tf_op jit(solution)/shard_map/ppermute | solution.py:32
  18.5 3.2 %collective-permute-start.8 = (bf16[2,384,512]{2,1,0:T(8,128)(2,1)S(1)}, bf16[2,384,512]{2,1,0:T(8,128)(2,1)}, u32[]{:S(2)}, u32[]{:S(2)}) collective-permute-start(bf16[2,384,512]{2,1,0:T(8,128)(2,1)S(1)} %pad_maximum_fusion.1.refs_1_), channel_id=1, source_target_pairs={{0,96},{4,28},{8,104},{12,4},{16,112},{20,12},{24,120},{28,20},{32... | collective-permute-start | bytes 2359304 | tf_op jit(solution)/shard_map/ppermute | solution.py:32
  21.8 6.2 %shard_map.28 = (bf16[768,8192]{1,0:T(8,128)(2,1)S(1)}, f32[8,128]{1,0:T(8,128)}) custom-call(s32[16]{0:T(128)S(1)} %stack.139.ids_ref, bf16[384,16384]{1,0:T(8,128)(2,1)} %refs_0_.3, bf16[384,16384]{1,0:T(8,128)(2,1)} %collective-permute-done.5.data_other_ref.refs_1_), custom_call_target="tpu_custom_call" | custom-call | bytes 25165824 | tf_op jit(solution)/shard_map/pallas_call | solution.py:68
  29.5 2.2 %collective-permute-done.4.refs_3_ = bf16[2,384,512]{2,1,0:T(8,128)(2,1)S(1)} collective-permute-done((bf16[2,384,512]{2,1,0:T(8,128)(2,1)S(1)}, bf16[2,384,512]{2,1,0:T(8,128)(2,1)S(1)}, u32[]{:S(2)}, u32[]{:S(2)}) %collective-permute-start.4) | collective-permute-done | bytes 786464 | tf_op jit(solution)/shard_map/ppermute | solution.py:32
  33.7 2.7 %collective-permute-done.8.refs_1_ = bf16[2,384,512]{2,1,0:T(8,128)(2,1)} collective-permute-done((bf16[2,384,512]{2,1,0:T(8,128)(2,1)S(1)}, bf16[2,384,512]{2,1,0:T(8,128)(2,1)}, u32[]{:S(2)}, u32[]{:S(2)}) %collective-permute-start.8) | collective-permute-done | bytes 786464 | tf_op jit(solution)/shard_map/ppermute | solution.py:32
  36.4 3.8 %collective-permute-done.9.refs_2_ = bf16[2,384,512]{2,1,0:T(8,128)(2,1)} collective-permute-done((bf16[2,384,512]{2,1,0:T(8,128)(2,1)S(1)}, bf16[2,384,512]{2,1,0:T(8,128)(2,1)}, u32[]{:S(2)}, u32[]{:S(2)}) %collective-permute-start.9) | collective-permute-done | bytes 786464 | tf_op jit(solution)/shard_map/ppermute | solution.py:32
  40.2 4.0 %shard_map.30.refs_3_ = f32[384,768]{1,0:T(8,128)S(1)} custom-call(bf16[2,384,512]{2,1,0:T(8,128)(2,1)S(1)} %collective-permute-done.3.refs_0_, bf16[2,384,512]{2,1,0:T(8,128)(2,1)} %collective-permute-done.8.refs_1_, bf16[2,384,512]{2,1,0:T(8,128)(2,1)} %collective-permute-done.9.refs_2_, bf16[2,384,512]{2,1,0:T(8,128)(2,1)S(1)} %collective-permute-done.4.refs_3_, ...), custom_call_target="tpu_custom_call" | custom-call | flops 2415919104 | bytes 9437184 | tf_op jit(solution)/shard_map/pallas_call | solution.py:68
  44.8 3.7 %collective-permute-done.7.refs_1_ = bf16[2,384,512]{2,1,0:T(8,128)(2,1)S(1)} collective-permute-done((bf16[2,384,512]{2,1,0:T(8,128)(2,1)S(1)}, bf16[2,384,512]{2,1,0:T(8,128)(2,1)S(1)}, u32[]{:S(2)}, u32[]{:S(2)}) %collective-permute-start.7) | collective-permute-done | bytes 786464 | tf_op jit(solution)/shard_map/ppermute | solution.py:32
  52.3 11.7 %all_to_all.23 = f32[32,2,384]{2,1,0:T(2,128)S(1)} all-to-all(f32[32,2,384]{2,1,0:T(2,128)S(1)} %broadcast_in_dim.9), channel_id=1, replica_groups=mesh['dp'=32,'noise'=4] {'dp'}, dimensions={0} | all-to-all | bytes 196608 | tf_op jit(solution)/shard_map/all_to_all | solution.py:52
  64.5 3.1 %collective-permute-start.11 = (f32[384]{0:T(512)S(1)}, f32[384]{0:T(512)S(1)}, u32[]{:S(2)}, u32[]{:S(2)}) collective-permute-start(f32[384]{0:T(512)S(1)} %log_add_fusion.4), channel_id=1, source_target_pairs={{0,2},{1,3},{2,0},{3,1},{4,6},{5,7},{6,4},{7,5},{8,10},{9,11},{10,... | collective-permute-start | bytes 4616 | tf_op jit(solution)/shard_map/ppermute | solution.py:62
  68.2 2.6 %collective-permute-start.13 = (f32[384]{0:T(512)S(1)}, f32[384]{0:T(512)S(1)}, u32[]{:S(2)}, u32[]{:S(2)}) collective-permute-start(f32[384]{0:T(512)S(1)} %log_add_fusion.4), channel_id=1, source_target_pairs={{0,3},{1,0},{2,1},{3,2},{4,7},{5,4},{6,5},{7,6},{8,11},{9,8},{10,9... | collective-permute-start | bytes 4616 | tf_op jit(solution)/shard_map/ppermute | solution.py:62
  70.8 1.5 collective-permute-done.12
  72.9 10.9 %all_to_all.24 = f32[32,1,384]{2,1,0:T(1,128)S(1)} all-to-all(f32[32,1,384]{2,1,0:T(1,128)S(1)} %broadcast_in_dim.10), channel_id=1, replica_groups=mesh['dp'=32,'noise'=4] {'dp'}, dimensions={0} | all-to-all | bytes 98304 | tf_op jit(solution)/shard_map/all_to_all | solution.py:52
  84.3 1.5 collective-permute-start.14
  85.8 2.6 %collective-permute-start.15 = (f32[384]{0:T(512)S(1)}, f32[384]{0:T(512)S(1)}, u32[]{:S(2)}, u32[]{:S(2)}) collective-permute-start(f32[384]{0:T(512)S(1)} %log_add_fusion.2), channel_id=1, source_target_pairs={{0,1},{1,2},{2,3},{3,0},{4,5},{5,6},{6,7},{7,4},{8,9},{9,10},{10,1... | collective-permute-start | bytes 4616 | tf_op jit(solution)/shard_map/ppermute | solution.py:62
  92.5 10.8 %all_to_all.25 = f32[32,1,384]{2,1,0:T(1,128)S(1)} all-to-all(f32[32,1,384]{2,1,0:T(1,128)S(1)} %broadcast_in_dim.11), channel_id=1, replica_groups=mesh['dp'=32,'noise'=4] {'dp'}, dimensions={0} | all-to-all | bytes 98304 | tf_op jit(solution)/shard_map/all_to_all | solution.py:52
  104.6 2.0 %collective-permute-start.18 = (f32[384]{0:T(512)S(1)}, f32[384]{0:T(512)S(1)}, u32[]{:S(2)}, u32[]{:S(2)}) collective-permute-start(f32[384]{0:T(512)S(1)} %log_add_fusion), channel_id=1, source_target_pairs={{0,1},{1,2},{2,3},{3,0},{4,5},{5,6},{6,7},{7,4},{8,9},{9,10},{10,1... | collective-permute-start | bytes 4616 | tf_op jit(solution)/shard_map/ppermute | solution.py:62
  107.8 2.5 %shard_map.33 = (bf16[768,2048]{1,0:T(8,128)(2,1)S(1)}, f32[8,128]{1,0:T(8,128)S(1)}) custom-call(s32[16]{0:T(128)S(1)} %stack.139.ids_ref, bf16[384,16384]{1,0:T(8,128)(2,1)} %refs_0_.3, bf16[384,16384]{1,0:T(8,128)(2,1)} %collective-permute-done.5.data_other_ref.refs_1_), custom_call_target="tpu_custom_call" | custom-call | bytes 6291456 | tf_op jit(solution)/shard_map/pallas_call | solution.py:68
  111.7 1.6 collective-permute-done.20.w_oth_ref
  113.2 2.3 %shard_map.34 = (bf16[4,208,512]{2,1,0:T(8,128)(2,1)S(1)}, bf16[4,192,512]{2,1,0:T(8,128)(2,1)S(1)}) custom-call(s32[16]{0:T(128)S(1)} %stack.139.ids_ref, bf16[384,384]{1,0:T(8,128)(2,1)S(1)} %exponential_convert_fusion.w_own_ref, bf16[384,384]{1,0:T(8,128)(2,1)S(1)} %collective-permute-done.20.w_oth_ref, bf16[768,2048]{1,0:T(8,128)(2,1)S(1)} %get-tuple-element.47.refs_0_, ...), custom_call_target="tpu_custom_call" | custom-call | flops 1207959552 | bytes 4718592 | tf_op jit(solution)/shard_map/pallas_call | solution.py:68
  117.6 7.1 %shard_map.35 = (bf16[3,208,512]{2,1,0:T(8,128)(2,1)S(1)}, bf16[3,192,512]{2,1,0:T(8,128)(2,1)S(1)}, bf16[1,208,512]{2,1,0:T(8,128)(2,1)S(1)}, bf16[1,192,512]{2...) custom-call(s32[16]{0:T(128)S(1)} %stack.139.ids_ref, ...), custom_call_target="tpu_custom_call" | custom-call | flops 2415919104 | bytes 9437184 | tf_op jit(solution)/shard_map/pallas_call | solution.py:68
  124.7 2.4 %collective-permute-start.25 = (bf16[3,208,512]{2,1,0:T(8,128)(2,1)S(1)}, bf16[3,208,512]{2,1,0:T(8,128)(2,1)S(1)}, u32[]{:S(2)}, u32[]{:S(2)}) collective-permute-start(bf16[3,208,512]{2,1,0:T(8,128)(2,1)S(1)} %get-tuple-element.63), channel_id=1, source_target_pairs={{0,96},{4,28},{8,104},{12,4},{16,112},{20,12},{24,120},{28,20},{32... | collective-permute-start | bytes 1916936 | tf_op jit(solution)/shard_map/ppermute | solution.py:32
  127.8 2.8 %collective-permute-done.21 = bf16[4,208,512]{2,1,0:T(8,128)(2,1)S(1)} collective-permute-done((bf16[4,208,512]{2,1,0:T(8,128)(2,1)S(1)}, bf16[4,208,512]{2,1,0:T(8,128)(2,1)S(1)}, u32[]{:S(2)}, u32[]{:S(2)}) %collective-permute-start.21) | collective-permute-done | bytes 852000 | tf_op jit(solution)/shard_map/ppermute | solution.py:32
  133.1 3.9 %shard_map.36 = (bf16[4,208,512]{2,1,0:T(8,128)(2,1)S(1)}, bf16[4,192,512]{2,1,0:T(8,128)(2,1)S(1)}) custom-call(s32[16]{0:T(128)S(1)} %stack.139.ids_ref, bf16[384,384]{1,0:T(8,128)(2,1)S(1)} %exponential_convert_fusion.w_own_ref, bf16[384,384]{1,0:T(8,128)(2,1)S(1)} %collective-permute-done.20.w_oth_ref, bf16[384,16384]{1,0:T(8,128)(2,1)} %refs_0_.3, ...), custom_call_target="tpu_custom_call" | custom-call | flops 1207959552 | bytes 4718592 | tf_op jit(solution)/shard_map/pallas_call | solution.py:68
  139.1 2.4 %collective-permute-done.28 = bf16[3,192,512]{2,1,0:T(8,128)(2,1)S(1)} collective-permute-done((bf16[3,192,512]{2,1,0:T(8,128)(2,1)S(1)}, bf16[3,192,512]{2,1,0:T(8,128)(2,1)S(1)}, u32[]{:S(2)}, u32[]{:S(2)}) %collective-permute-start.28) | collective-permute-done | bytes 589856 | tf_op jit(solution)/shard_map/ppermute | solution.py:32
  141.7 3.3 %collective-permute-done.26 = bf16[3,208,512]{2,1,0:T(8,128)(2,1)S(1)} collective-permute-done((bf16[3,208,512]{2,1,0:T(8,128)(2,1)S(1)}, bf16[3,208,512]{2,1,0:T(8,128)(2,1)S(1)}, u32[]{:S(2)}, u32[]{:S(2)}) %collective-permute-start.26) | collective-permute-done | bytes 639008 | tf_op jit(solution)/shard_map/ppermute | solution.py:32
  147.6 2.4 %collective-permute-start.31 = (bf16[400,512]{1,0:T(8,128)(2,1)S(1)}, bf16[400,512]{1,0:T(8,128)(2,1)S(1)}, u32[]{:S(2)}, u32[]{:S(2)}) collective-permute-start(bf16[400,512]{1,0:T(8,128)(2,1)S(1)} %pad_maximum_fusion.6), channel_id=1, source_target_pairs={{0,24},{4,100},{8,0},{12,108},{16,8},{20,116},{24,16},{28,124},{32... | collective-permute-start | bytes 1228808 | tf_op jit(solution)/shard_map/ppermute | solution.py:32
  150.0 5.1 %collective-permute-done.23 = bf16[400,512]{1,0:T(8,128)(2,1)S(1)} collective-permute-done((bf16[400,512]{1,0:T(8,128)(2,1)S(1)}, bf16[400,512]{1,0:T(8,128)(2,1)S(1)}, u32[]{:S(2)}, u32[]{:S(2)}) %collective-permute-start.23) | collective-permute-done | bytes 409632 | tf_op jit(solution)/shard_map/ppermute | solution.py:32
  155.1 4.2 %collective-permute-done.30 = bf16[400,512]{1,0:T(8,128)(2,1)S(1)} collective-permute-done((bf16[400,512]{1,0:T(8,128)(2,1)S(1)}, bf16[400,512]{1,0:T(8,128)(2,1)S(1)}, u32[]{:S(2)}, u32[]{:S(2)}) %collective-permute-start.30) | collective-permute-done | bytes 409632 | tf_op jit(solution)/shard_map/ppermute | solution.py:32
  (128 shorter events, 31.4 us)
Async XLA Ops:
  0.0 21.8 %collective-permute-start.5 = (bf16[384,16384]{1,0:T(8,128)(2,1)}, bf16[384,16384]{1,0:T(8,128)(2,1)}, u32[]{:S(2)}, u32[]{:S(2)}) collective-permute-start(bf16[384,16384]{1,0:T(8,128)(2,1)} %refs_0_.3), channel_id=1, source_target_pairs={{0,4},{4,0},{8,12},{12,8},{16,20},{20,16},{24,28},{28,24},{32,36},... | collective-permute-start | bytes 37748744 | tf_op jit(solution)/shard_map/ppermute | solution.py:21
  0.0 13.1 %collective-permute-start = (bf16[384,512]{1,0:T(8,128)(2,1)}, bf16[384,512]{1,0:T(8,128)(2,1)S(1)}, u32[]{:S(2)}, u32[]{:S(2)}) collective-permute-start(bf16[384,512]{1,0:T(8,128)(2,1)} %param.2), channel_id=1, source_target_pairs={{0,16},{4,68},{8,24},{12,76},{16,0},{20,84},{24,8},{28,92},{32,48}... | collective-permute-start | bytes 1179656 | tf_op jit(solution)/shard_map/ppermute | solution.py:32
  4.0 11.2 %collective-permute-start.1 = (bf16[384,512]{1,0:T(8,128)(2,1)}, bf16[384,512]{1,0:T(8,128)(2,1)S(1)}, u32[]{:S(2)}, u32[]{:S(2)}) collective-permute-start(bf16[384,512]{1,0:T(8,128)(2,1)} %param.2), channel_id=1, source_target_pairs={{0,24},{4,100},{8,0},{12,108},{16,8},{20,116},{24,16},{28,124},{32... | collective-permute-start | bytes 1179656 | tf_op jit(solution)/shard_map/ppermute | solution.py:32
  4.7 10.6 %collective-permute-start.2 = (bf16[384,512]{1,0:T(8,128)(2,1)}, bf16[384,512]{1,0:T(8,128)(2,1)S(1)}, u32[]{:S(2)}, u32[]{:S(2)}) collective-permute-start(bf16[384,512]{1,0:T(8,128)(2,1)} %param.2), channel_id=1, source_target_pairs={{0,8},{4,36},{8,16},{12,44},{16,24},{20,52},{24,0},{28,60},{32,40}... | collective-permute-start | bytes 1179656 | tf_op jit(solution)/shard_map/ppermute | solution.py:32
  15.4 14.1 %collective-permute-start.3 = (bf16[2,384,512]{2,1,0:T(8,128)(2,1)S(1)}, bf16[2,384,512]{2,1,0:T(8,128)(2,1)S(1)}, u32[]{:S(2)}, u32[]{:S(2)}) collective-permute-start(bf16[2,384,512]{2,1,0:T(8,128)(2,1)S(1)} %pad_maximum_fusion.refs_0_), channel_id=1, source_target_pairs={{0,96},{4,28},{8,104},{12,4},{16,112},{20,12},{24,120},{28,20},{32... | collective-permute-start | bytes 2359304 | tf_op jit(solution)/shard_map/ppermute | solution.py:32
  18.5 13.2 %collective-permute-start.4 = (bf16[2,384,512]{2,1,0:T(8,128)(2,1)S(1)}, bf16[2,384,512]{2,1,0:T(8,128)(2,1)S(1)}, u32[]{:S(2)}, u32[]{:S(2)}) collective-permute-start(bf16[2,384,512]{2,1,0:T(8,128)(2,1)S(1)} %pad_maximum_fusion.1.refs_1_), channel_id=1, source_target_pairs={{0,32},{4,12},{8,40},{12,20},{16,48},{20,28},{24,56},{28,4},{32,64... | collective-permute-start | bytes 2359304 | tf_op jit(solution)/shard_map/ppermute | solution.py:32
  18.5 17.9 %collective-permute-start.8 = (bf16[2,384,512]{2,1,0:T(8,128)(2,1)S(1)}, bf16[2,384,512]{2,1,0:T(8,128)(2,1)}, u32[]{:S(2)}, u32[]{:S(2)}) collective-permute-start(bf16[2,384,512]{2,1,0:T(8,128)(2,1)S(1)} %pad_maximum_fusion.1.refs_1_), channel_id=1, source_target_pairs={{0,96},{4,28},{8,104},{12,4},{16,112},{20,12},{24,120},{28,20},{32... | collective-permute-start | bytes 2359304 | tf_op jit(solution)/shard_map/ppermute | solution.py:32
  21.7 18.5 %collective-permute-start.9 = (bf16[2,384,512]{2,1,0:T(8,128)(2,1)S(1)}, bf16[2,384,512]{2,1,0:T(8,128)(2,1)}, u32[]{:S(2)}, u32[]{:S(2)}) collective-permute-start(bf16[2,384,512]{2,1,0:T(8,128)(2,1)S(1)} %pad_maximum_fusion.refs_0_), channel_id=1, source_target_pairs={{0,32},{4,12},{8,40},{12,20},{16,48},{20,28},{24,56},{28,4},{32,64... | collective-permute-start | bytes 2359304 | tf_op jit(solution)/shard_map/ppermute | solution.py:32
  31.7 13.2 %collective-permute-start.6 = (bf16[2,384,512]{2,1,0:T(8,128)(2,1)S(1)}, bf16[2,384,512]{2,1,0:T(8,128)(2,1)S(1)}, u32[]{:S(2)}, u32[]{:S(2)}) collective-permute-start(bf16[2,384,512]{2,1,0:T(8,128)(2,1)S(1)} %collective-permute-done.3.refs_0_), channel_id=1, source_target_pairs={{0,96},{4,28},{8,104},{12,4},{16,112},{20,12},{24,120},{28,20},{32... | collective-permute-start | bytes 2359304 | tf_op jit(solution)/shard_map/ppermute | solution.py:32
  32.8 15.7 %collective-permute-start.7 = (bf16[2,384,512]{2,1,0:T(8,128)(2,1)S(1)}, bf16[2,384,512]{2,1,0:T(8,128)(2,1)S(1)}, u32[]{:S(2)}, u32[]{:S(2)}) collective-permute-start(bf16[2,384,512]{2,1,0:T(8,128)(2,1)S(1)} %collective-permute-done.4.refs_3_), channel_id=1, source_target_pairs={{0,32},{4,12},{8,40},{12,20},{16,48},{20,28},{24,56},{28,4},{32,64... | collective-permute-start | bytes 2359304 | tf_op jit(solution)/shard_map/ppermute | solution.py:32
  49.5 2.3 %collective-permute-start.10 = (f32[384,384]{1,0:T(8,128)S(1)}, f32[384,384]{1,0:T(8,128)S(1)}, u32[]{:S(2)}, u32[]{:S(2)}) collective-permute-start(f32[384,384]{1,0:T(8,128)S(1)} %shard_map.32), channel_id=1, source_target_pairs={{0,4},{4,0},{8,12},{12,8},{16,20},{20,16},{24,28},{28,24},{32,36},... | collective-permute-start | bytes 1769480 | tf_op jit(solution)/shard_map/ppermute | solution.py:21
  64.5 6.3 %collective-permute-start.11 = (f32[384]{0:T(512)S(1)}, f32[384]{0:T(512)S(1)}, u32[]{:S(2)}, u32[]{:S(2)}) collective-permute-start(f32[384]{0:T(512)S(1)} %log_add_fusion.4), channel_id=1, source_target_pairs={{0,2},{1,3},{2,0},{3,1},{4,6},{5,7},{6,4},{7,5},{8,10},{9,11},{10,... | collective-permute-start | bytes 4616 | tf_op jit(solution)/shard_map/ppermute | solution.py:62
  67.6 4.8 %collective-permute-start.12 = (f32[384]{0:T(512)S(1)}, f32[384]{0:T(512)S(1)}, u32[]{:S(2)}, u32[]{:S(2)}) collective-permute-start(f32[384]{0:T(512)S(1)} %log_add_fusion.4), channel_id=1, source_target_pairs={{0,1},{1,2},{2,3},{3,0},{4,5},{5,6},{6,7},{7,4},{8,9},{9,10},{10,1... | collective-permute-start | bytes 4616 | tf_op jit(solution)/shard_map/ppermute | solution.py:62
  68.2 4.2 %collective-permute-start.13 = (f32[384]{0:T(512)S(1)}, f32[384]{0:T(512)S(1)}, u32[]{:S(2)}, u32[]{:S(2)}) collective-permute-start(f32[384]{0:T(512)S(1)} %log_add_fusion.4), channel_id=1, source_target_pairs={{0,3},{1,0},{2,1},{3,2},{4,7},{5,4},{6,5},{7,6},{8,11},{9,8},{10,9... | collective-permute-start | bytes 4616 | tf_op jit(solution)/shard_map/ppermute | solution.py:62
  84.3 5.2 %collective-permute-start.14 = (f32[384]{0:T(512)S(1)}, f32[384]{0:T(512)S(1)}, u32[]{:S(2)}, u32[]{:S(2)}) collective-permute-start(f32[384]{0:T(512)S(1)} %log_add_fusion.2), channel_id=1, source_target_pairs={{0,2},{1,3},{2,0},{3,1},{4,6},{5,7},{6,4},{7,5},{8,10},{9,11},{10,... | collective-permute-start | bytes 4616 | tf_op jit(solution)/shard_map/ppermute | solution.py:62
  85.8 4.8 %collective-permute-start.15 = (f32[384]{0:T(512)S(1)}, f32[384]{0:T(512)S(1)}, u32[]{:S(2)}, u32[]{:S(2)}) collective-permute-start(f32[384]{0:T(512)S(1)} %log_add_fusion.2), channel_id=1, source_target_pairs={{0,1},{1,2},{2,3},{3,0},{4,5},{5,6},{6,7},{7,4},{8,9},{9,10},{10,1... | collective-permute-start | bytes 4616 | tf_op jit(solution)/shard_map/ppermute | solution.py:62
  88.4 3.6 %collective-permute-start.16 = (f32[384]{0:T(512)S(1)}, f32[384]{0:T(512)S(1)}, u32[]{:S(2)}, u32[]{:S(2)}) collective-permute-start(f32[384]{0:T(512)S(1)} %log_add_fusion.2), channel_id=1, source_target_pairs={{0,3},{1,0},{2,1},{3,2},{4,7},{5,4},{6,5},{7,6},{8,11},{9,8},{10,9... | collective-permute-start | bytes 4616 | tf_op jit(solution)/shard_map/ppermute | solution.py:62
  103.8 6.5 %collective-permute-start.17 = (f32[384]{0:T(512)S(1)}, f32[384]{0:T(512)S(1)}, u32[]{:S(2)}, u32[]{:S(2)}) collective-permute-start(f32[384]{0:T(512)S(1)} %log_add_fusion), channel_id=1, source_target_pairs={{0,2},{1,3},{2,0},{3,1},{4,6},{5,7},{6,4},{7,5},{8,10},{9,11},{10,... | collective-permute-start | bytes 4616 | tf_op jit(solution)/shard_map/ppermute | solution.py:62
  104.6 5.7 %collective-permute-start.18 = (f32[384]{0:T(512)S(1)}, f32[384]{0:T(512)S(1)}, u32[]{:S(2)}, u32[]{:S(2)}) collective-permute-start(f32[384]{0:T(512)S(1)} %log_add_fusion), channel_id=1, source_target_pairs={{0,1},{1,2},{2,3},{3,0},{4,5},{5,6},{6,7},{7,4},{8,9},{9,10},{10,1... | collective-permute-start | bytes 4616 | tf_op jit(solution)/shard_map/ppermute | solution.py:62
  106.6 3.8 %collective-permute-start.19 = (f32[384]{0:T(512)S(1)}, f32[384]{0:T(512)S(1)}, u32[]{:S(2)}, u32[]{:S(2)}) collective-permute-start(f32[384]{0:T(512)S(1)} %log_add_fusion), channel_id=1, source_target_pairs={{0,3},{1,0},{2,1},{3,2},{4,7},{5,4},{6,5},{7,6},{8,11},{9,8},{10,9... | collective-permute-start | bytes 4616 | tf_op jit(solution)/shard_map/ppermute | solution.py:62
  111.6 1.7 %collective-permute-start.20 = (bf16[384,384]{1,0:T(8,128)(2,1)S(1)}, bf16[384,384]{1,0:T(8,128)(2,1)S(1)}, u32[]{:S(2)}, u32[]{:S(2)}) collective-permute-start(bf16[384,384]{1,0:T(8,128)(2,1)S(1)} %exponential_convert_fusion.w_own_ref), channel_id=1, source_target_pairs={{0,4},{4,0},{8,12},{12,8},{16,20},{20,16},{24,28},{28,24},{32,36},... | collective-permute-start | bytes 884744 | tf_op jit(solution)/shard_map/ppermute | solution.py:21
  115.5 12.1 %collective-permute-start.22 = (bf16[4,192,512]{2,1,0:T(8,128)(2,1)S(1)}, bf16[4,192,512]{2,1,0:T(8,128)(2,1)S(1)}, u32[]{:S(2)}, u32[]{:S(2)}) collective-permute-start(bf16[4,192,512]{2,1,0:T(8,128)(2,1)S(1)} %get-tuple-element.55), channel_id=1, source_target_pairs={{0,96},{4,28},{8,104},{12,4},{16,112},{20,12},{24,120},{28,20},{32... | collective-permute-start | bytes 2359304 | tf_op jit(solution)/shard_map/ppermute | solution.py:32
  116.7 13.9 %collective-permute-start.21 = (bf16[4,208,512]{2,1,0:T(8,128)(2,1)S(1)}, bf16[4,208,512]{2,1,0:T(8,128)(2,1)S(1)}, u32[]{:S(2)}, u32[]{:S(2)}) collective-permute-start(bf16[4,208,512]{2,1,0:T(8,128)(2,1)S(1)} %get-tuple-element.53), channel_id=1, source_target_pairs={{0,32},{4,12},{8,40},{12,20},{16,48},{20,28},{24,56},{28,4},{32,64... | collective-permute-start | bytes 2555912 | tf_op jit(solution)/shard_map/ppermute | solution.py:32
  124.7 17.0 %collective-permute-start.25 = (bf16[3,208,512]{2,1,0:T(8,128)(2,1)S(1)}, bf16[3,208,512]{2,1,0:T(8,128)(2,1)S(1)}, u32[]{:S(2)}, u32[]{:S(2)}) collective-permute-start(bf16[3,208,512]{2,1,0:T(8,128)(2,1)S(1)} %get-tuple-element.63), channel_id=1, source_target_pairs={{0,96},{4,28},{8,104},{12,4},{16,112},{20,12},{24,120},{28,20},{32... | collective-permute-start | bytes 1916936 | tf_op jit(solution)/shard_map/ppermute | solution.py:32
  127.1 11.1 %collective-permute-start.27 = (bf16[3,192,512]{2,1,0:T(8,128)(2,1)S(1)}, bf16[3,192,512]{2,1,0:T(8,128)(2,1)S(1)}, u32[]{:S(2)}, u32[]{:S(2)}) collective-permute-start(bf16[3,192,512]{2,1,0:T(8,128)(2,1)S(1)} %get-tuple-element.65), channel_id=1, source_target_pairs={{0,32},{4,12},{8,40},{12,20},{16,48},{20,28},{24,56},{28,4},{32,64... | collective-permute-start | bytes 1769480 | tf_op jit(solution)/shard_map/ppermute | solution.py:32
  130.8 10.7 %collective-permute-start.28 = (bf16[3,192,512]{2,1,0:T(8,128)(2,1)S(1)}, bf16[3,192,512]{2,1,0:T(8,128)(2,1)S(1)}, u32[]{:S(2)}, u32[]{:S(2)}) collective-permute-start(bf16[3,192,512]{2,1,0:T(8,128)(2,1)S(1)} %add_convert_fusion.1), channel_id=1, source_target_pairs={{0,96},{4,28},{8,104},{12,4},{16,112},{20,12},{24,120},{28,20},{32... | collective-permute-start | bytes 1769480 | tf_op jit(solution)/shard_map/ppermute | solution.py:32
  130.9 19.1 %collective-permute-start.24 = (bf16[400,512]{1,0:T(8,128)(2,1)S(1)}, bf16[400,512]{1,0:T(8,128)(2,1)S(1)}, u32[]{:S(2)}, u32[]{:S(2)}) collective-permute-start(bf16[400,512]{1,0:T(8,128)(2,1)S(1)} %pad_maximum_fusion.3), channel_id=1, source_target_pairs={{0,96},{4,28},{8,104},{12,4},{16,112},{20,12},{24,120},{28,20},{32... | collective-permute-start | bytes 1228808 | tf_op jit(solution)/shard_map/ppermute | solution.py:32
  131.9 13.2 %collective-permute-start.26 = (bf16[3,208,512]{2,1,0:T(8,128)(2,1)S(1)}, bf16[3,208,512]{2,1,0:T(8,128)(2,1)S(1)}, u32[]{:S(2)}, u32[]{:S(2)}) collective-permute-start(bf16[3,208,512]{2,1,0:T(8,128)(2,1)S(1)} %add_convert_fusion), channel_id=1, source_target_pairs={{0,32},{4,12},{8,40},{12,20},{16,48},{20,28},{24,56},{28,4},{32,64... | collective-permute-start | bytes 1916936 | tf_op jit(solution)/shard_map/ppermute | solution.py:32
  138.2 16.9 %collective-permute-start.23 = (bf16[400,512]{1,0:T(8,128)(2,1)S(1)}, bf16[400,512]{1,0:T(8,128)(2,1)S(1)}, u32[]{:S(2)}, u32[]{:S(2)}) collective-permute-start(bf16[400,512]{1,0:T(8,128)(2,1)S(1)} %pad_maximum_fusion.2), channel_id=1, source_target_pairs={{0,32},{4,12},{8,40},{12,20},{16,48},{20,28},{24,56},{28,4},{32,64... | collective-permute-start | bytes 1228808 | tf_op jit(solution)/shard_map/ppermute | solution.py:32
  145.4 9.8 %collective-permute-start.29 = (bf16[400,512]{1,0:T(8,128)(2,1)S(1)}, bf16[400,512]{1,0:T(8,128)(2,1)S(1)}, u32[]{:S(2)}, u32[]{:S(2)}) collective-permute-start(bf16[400,512]{1,0:T(8,128)(2,1)S(1)} %pad_maximum_fusion.4), channel_id=1, source_target_pairs={{0,16},{4,68},{8,24},{12,76},{16,0},{20,84},{24,8},{28,92},{32,48}... | collective-permute-start | bytes 1228808 | tf_op jit(solution)/shard_map/ppermute | solution.py:32
  146.6 12.7 %collective-permute-start.30 = (bf16[400,512]{1,0:T(8,128)(2,1)S(1)}, bf16[400,512]{1,0:T(8,128)(2,1)S(1)}, u32[]{:S(2)}, u32[]{:S(2)}) collective-permute-start(bf16[400,512]{1,0:T(8,128)(2,1)S(1)} %pad_maximum_fusion.5), channel_id=1, source_target_pairs={{0,8},{4,36},{8,16},{12,44},{16,24},{20,52},{24,0},{28,60},{32,40}... | collective-permute-start | bytes 1228808 | tf_op jit(solution)/shard_map/ppermute | solution.py:32
  147.6 11.7 %collective-permute-start.31 = (bf16[400,512]{1,0:T(8,128)(2,1)S(1)}, bf16[400,512]{1,0:T(8,128)(2,1)S(1)}, u32[]{:S(2)}, u32[]{:S(2)}) collective-permute-start(bf16[400,512]{1,0:T(8,128)(2,1)S(1)} %pad_maximum_fusion.6), channel_id=1, source_target_pairs={{0,24},{4,100},{8,0},{12,108},{16,8},{20,116},{24,16},{28,124},{32... | collective-permute-start | bytes 1228808 | tf_op jit(solution)/shard_map/ppermute | solution.py:32
  (2 other events, 6.4 us)
